TPU v7x, 512 devices: a whole 4x4x16 slice. The times are simulated.
512 devices in a mesh: dp: 16 (over z_lo, core), row: 4 (over y), col: 8 (over z_hi, x).
Axes of the slice: x: 4, y: 4, z: 16 (z_hi: 2, z_lo: 8; z = z_hi * 8 + z_lo), core: 2. Of those that a mesh axis runs over, the one named last changes fastest.
Arguments:
- tokens: bfloat16 [12288, 16384], P('dp', 'col'), may hold values from -6 to 6
- out_grad: bfloat16 [12288, 16384], P('dp', 'col'), may hold values from -6 to 6
- router_logits: float32 [98304], P('dp'), may hold values from -8 to 8
- routed_counts: int32 [16], P('dp'), may hold values from 192 to 768, as said below
- routed_positions: int32 [12288], P('dp'), may hold values from 0 to 6143, as said below
- gate_values: bfloat16 [16384, 512], P(('col', 'dp'), 'row'), may hold values from -4 to 4
- up_values: bfloat16 [16384, 512], P(('col', 'dp'), 'row'), may hold values from -4 to 4
- down_values: bfloat16 [512, 16384], P('row', ('col', 'dp')), may hold values from -4 to 4
- gate_scales: float32 [128, 4], P('col', 'row'), may hold values from 0.00390625 to 0.015625
- up_scales: float32 [128, 4], P('col', 'row'), may hold values from 0.00390625 to 0.015625
- down_scales: float32 [4, 128], P('row', 'col'), may hold values from 0.00390625 to 0.015625
Outputs:
- grad_tokens: bfloat16 [12288, 16384], P('dp', 'col')
- grad_gate: float32 [16384, 512], P(('col', 'dp'), 'row')
- grad_up: float32 [16384, 512], P(('col', 'dp'), 'row')
- grad_down: float32 [512, 16384], P('row', ('col', 'dp'))
- grad_logits: float32 [98304], P('dp')
Inputs may be any that keep to these rules, and one draw needn't show every extreme that they name: `routed_counts`: live routed rows of each data group; in every draw some group has all 768 rows live. `routed_positions`: within each data group, 768 distinct positions in increasing order, 0 and 6143 among them; slots at or past the group's count are padding.
All inputs are finite; a program needn't handle non-finite values.
Results may differ from a plain program's by a relative error of at most 0.0075.
Values may be sent and summed in bfloat16 or wider, within the bound.
No kernel may reach another device: no remote copies, remote signals or barrier semaphores. Data moves between devices by JAX's collectives and lax.ppermute only.
A program may use at most 128 MiB of HBM per device.

v0:
```python
import jax
import jax.numpy as jnp
from jax import lax
from jax.sharding import PartitionSpec as P

CONTRACT_ROWS = (((0,), (0,)), ((), ()))
CONTRACT_COLS = (((1,), (1,)), ((), ()))


def dequantize(values, scales):
    height, breadth = values.shape
    row_blocks, col_blocks = scales.shape
    quant_tiles = values.astype(jnp.float32).reshape(
        row_blocks, height // row_blocks, col_blocks, breadth // col_blocks
    )
    return (quant_tiles * scales[:, None, :, None]).reshape(height, breadth).astype(jnp.bfloat16)


def swiglu_backward(gate_sum, up_sum, back_sum, row_weight):
    gate_sigmoid = jax.nn.sigmoid(gate_sum)
    activated = gate_sum * gate_sigmoid
    hidden_full = activated * up_sum
    hidden_delta = back_sum * row_weight[:, None]
    up_delta = (hidden_delta * activated).astype(jnp.bfloat16)
    gate_delta = (
        hidden_delta * up_sum * gate_sigmoid * (1.0 + gate_sum * (1.0 - gate_sigmoid))
    ).astype(jnp.bfloat16)
    router_part = jnp.sum(back_sum * hidden_full, axis=1)
    return (hidden_full.astype(jnp.bfloat16), gate_delta, up_delta, router_part)


def rounded_term(term):
    return lax.optimization_barrier(term.astype(jnp.bfloat16)).astype(jnp.float32)


def local(
    tokens,
    out_grad,
    router_logits,
    routed_counts,
    routed_positions,
    gate_values,
    up_values,
    down_values,
    gate_scales,
    up_scales,
    down_scales,
):
    gate_whole, up_whole = (
        lax.all_gather(gate_values, "dp", axis=0, tiled=True),
        lax.all_gather(up_values, "dp", axis=0, tiled=True),
    )
    down_whole = lax.all_gather(down_values, "dp", axis=1, tiled=True)
    w_gate = dequantize(gate_whole, gate_scales)
    w_up = dequantize(up_whole, up_scales)
    w_down = dequantize(down_whole, down_scales)
    capacity = tokens.shape[0]
    row_count = routed_counts[0]
    live_rows = (jnp.arange(capacity) < row_count).astype(jnp.float32)
    router_rate = jax.nn.sigmoid(jnp.take(router_logits, routed_positions))
    row_weight = router_rate * live_rows
    scaled_grad = (out_grad.astype(jnp.float32) * row_weight[:, None]).astype(jnp.bfloat16)
    gate_part = jnp.dot(tokens, w_gate, preferred_element_type=jnp.float32)
    up_part = jnp.dot(tokens, w_up, preferred_element_type=jnp.float32)
    back_part = lax.dot_general(out_grad, w_down, CONTRACT_COLS, preferred_element_type=jnp.float32)
    gate_sum, up_sum, back_sum = lax.psum((gate_part, up_part, back_part), "col")
    hidden, gate_delta, up_delta, router_part = swiglu_backward(
        gate_sum, up_sum, back_sum, row_weight
    )
    input_part = lax.dot_general(
        gate_delta, w_gate, CONTRACT_COLS, preferred_element_type=jnp.float32
    ) + lax.dot_general(up_delta, w_up, CONTRACT_COLS, preferred_element_type=jnp.float32)
    input_sum, router_sum = lax.psum((input_part, router_part), "row")
    grad_tokens = input_sum.astype(jnp.bfloat16)
    logit_delta = router_sum * router_rate * (1.0 - router_rate) * live_rows
    grad_logits = jnp.zeros(router_logits.shape, jnp.float32).at[routed_positions].add(logit_delta)
    gate_term = rounded_term(
        lax.dot_general(tokens, gate_delta, CONTRACT_ROWS, preferred_element_type=jnp.float32)
    )
    up_term = rounded_term(
        lax.dot_general(tokens, up_delta, CONTRACT_ROWS, preferred_element_type=jnp.float32)
    )
    down_term = rounded_term(
        lax.dot_general(hidden, scaled_grad, CONTRACT_ROWS, preferred_element_type=jnp.float32)
    )
    grad_gate, grad_up = (
        lax.psum_scatter(gate_term, "dp", scatter_dimension=0, tiled=True),
        lax.psum_scatter(up_term, "dp", scatter_dimension=0, tiled=True),
    )
    grad_down = lax.psum_scatter(down_term, "dp", scatter_dimension=1, tiled=True)
    return (grad_tokens, grad_gate, grad_up, grad_down, grad_logits)


def solution(mesh):
    placed = (
        P("dp", "col"),
        P("dp", "col"),
        P("dp"),
        P("dp"),
        P("dp"),
        P(("col", "dp"), "row"),
        P(("col", "dp"), "row"),
        P("row", ("col", "dp")),
        P("col", "row"),
        P("col", "row"),
        P("row", "col"),
    )
    return jax.shard_map(
        local,
        mesh=mesh,
        in_specs=placed,
        out_specs=(
            P("dp", "col"),
            P(("col", "dp"), "row"),
            P(("col", "dp"), "row"),
            P("row", ("col", "dp")),
            P("dp"),
        ),
        check_vma=False,
    )
```

profile of v0, /device:TPU:1, one launch (start us, length us, event | category | flops | bytes accessed | tf_op | source)
XLA Modules:
  0.0 604.6 jit_solution(6190719977642325860)
XLA Ops:
  7.2 0.0 copy-start
  7.2 0.0 all-reduce.5.cloned.1.call-start
  7.2 0.9 broadcast_bitcast_fusion
  8.1 0.8 broadcast_bitcast_fusion.1
  8.9 0.7 broadcast_bitcast_fusion.2
  9.6 40.3 %all_gather.11 = bf16[2048,128]{1,0:T(8,128)(2,1)S(1)} all-gather(bf16[128,128]{1,0:T(8,128)(2,1)} %param.16), channel_id=1, replica_groups=mesh['dp'=16,'row'=4,'col'=8] {'dp'}, dimensions={0}, use_global_device_ids=true | all-gather | bytes 557056 | tf_op jit(solution)/shard_map/all_gather | solution.py:50
  49.8 28.0 %all_gather.10 = bf16[2048,128]{1,0:T(8,128)(2,1)S(1)} all-gather(bf16[128,128]{1,0:T(8,128)(2,1)} %param.17), channel_id=1, replica_groups=mesh['dp'=16,'row'=4,'col'=8] {'dp'}, dimensions={0}, use_global_device_ids=true | all-gather | bytes 557056 | tf_op jit(solution)/shard_map/all_gather | solution.py:51
  77.8 29.1 %all_gather.9 = bf16[128,2048]{1,0:T(8,128)(2,1)S(1)} all-gather(bf16[128,128]{1,0:T(8,128)(2,1)} %param.18), channel_id=1, replica_groups=mesh['dp'=16,'row'=4,'col'=8] {'dp'}, dimensions={1}, use_global_device_ids=true | all-gather | bytes 557056 | tf_op jit(solution)/shard_map/all_gather | solution.py:53
  106.9 0.0 copy-done
  106.9 2.4 convolution_bitcast_fusion
  109.3 2.4 convolution_bitcast_fusion.1
  111.7 0.0 copy-done.4
  111.7 0.0 copy-done.2
  111.7 0.0 copy-done.5
  111.7 0.0 copy-start.1
  111.7 1.9 convolution_bitcast_fusion.2
  113.6 0.0 all-reduce.5.cloned.1.call-update
  113.7 0.0 reduce-scatter.4.cloned.1.call-start
  114.4 0.0 copy-start.10
  114.4 0.6 copy-done.10
  115.0 4.5 gather_fusion
  119.5 0.6 fusion.12
  120.1 166.0 %all-reduce.5.cloned.1.call-done = (f32[768,128]{0,1:T(8,128)}, f32[768,128]{0,1:T(8,128)}, f32[768,128]{0,1:T(8,128)}) async-done(((f32[768,128]{0,1:T(8,128)}, f32[768,128]{0,1:T(8,128)}, f32[768,128]{0,1:T(8,128)}), (f32[768,128]{0,1:T(8,128)}, f32[768,128]{0,1:T(8,128)}, f32[768,128]{0,1:T(8,128)})) %all-reduce.5.cloned.1.call-update) | async-done | bytes 1179664 | tf_op jit(solution)/shard_map/psum | solution.py:66
  286.1 0.0 copy-done.8
  286.1 2.1 multiply_reduce_fusion
  288.2 0.6 fusion.3
  288.8 1.1 convert_element_type.72
  289.9 0.0 reduce-scatter.4.cloned.1.call-update
  289.9 0.0 reduce-scatter.6.cloned.1.call-start
  290.0 0.6 fusion.4
  290.6 1.1 convert_element_type.75
  291.7 0.0 reduce-scatter.6.cloned.1.call-update
  291.7 0.0 reduce-scatter.8.cloned.1.call-start
  291.7 3.0 fusion.2
  294.8 1.1 convert_element_type.80
  295.9 2.2 fusion.7
  298.1 0.0 copy-start.11
  298.2 3.8 convolution_add_fusion
  301.9 0.0 reduce-scatter.8.cloned.1.call-update
  302.0 0.0 copy-start.7
  302.0 0.0 copy-start.9
  302.0 112.3 %all-reduce.6 = (bf16[768,2048]{1,0:T(8,128)(2,1)}, f32[768]{0:T(1024)S(1)}) all-reduce(f32[768,2048]{1,0:T(8,128)} %convolution_add_fusion, f32[768]{0:T(1024)S(1)} %copy-done.11), channel_id=1, replica_groups=mesh['dp'=16,'row'=4,'col'=8] {'row'}, use_global_device_ids=true, to_apply=%region_3.4 | all-reduce | flops 1573632 | bytes 9443328 | tf_op jit(solution)/shard_map/psum | solution.py:73
  414.3 0.0 copy-done.9
  414.3 6.6 %scatter_custom_fusion = f32[6144]{0:T(1024)} fusion(s32[768]{0:T(1024)} %copy-done.10, f32[768]{0:T(1024)S(1)} %multiply_select_fusion, f32[]{:T(128)} %constant.25.clone.1), kind=kCustom, calls=%fused_computation.26 | custom fusion | flops 768 | bytes 25088 | tf_op jit(solution)/shard_map/scatter-add | solution.py:76
  420.9 1.6 copy.18
  422.5 72.3 %reduce-scatter.6.cloned.1.call-done = f32[128,128]{0,1:T(8,128)} async-done(((f32[2048,128]{0,1:T(8,128)}), f32[128,128]{0,1:T(8,128)}) %reduce-scatter.6.cloned.1.call-update) | async-done | bytes 65552 | tf_op jit(solution)/shard_map/reduce_scatter | solution.py:88
  494.8 1.6 copy.19
  496.4 101.7 %reduce-scatter.8.cloned.1.call-done = f32[128,128]{1,0:T(8,128)} async-done(((f32[128,2048]{1,0:T(8,128)}), f32[128,128]{1,0:T(8,128)}) %reduce-scatter.8.cloned.1.call-update) | async-done | bytes 65552 | tf_op jit(solution)/shard_map/reduce_scatter | solution.py:90
  (15 shorter events, 0.0 us)
Async XLA Ops:
  7.2 99.7 %copy-start = (bf16[768,2048]{1,0:T(8,128)(2,1)S(1)}, bf16[768,2048]{1,0:T(8,128)(2,1)}, u32[]{:S(2)}) copy-start(bf16[768,2048]{1,0:T(8,128)(2,1)} %param.11) | copy-start | bytes 9437188
  7.2 278.9 %all-reduce.5.cloned.1.call-start = ((), (), s32[]{:S(2)}) async-start(), calls=%async_computation.6 | async-start | bytes 2359296 | tf_op jit(solution)/shard_map/psum | solution.py:66
  49.8 61.8 %copy-start.4 = (bf16[2048,128]{1,0:T(8,128)(2,1)}, bf16[2048,128]{1,0:T(8,128)(2,1)S(1)}, u32[]{:S(2)}) copy-start(bf16[2048,128]{1,0:T(8,128)(2,1)S(1)} %all_gather.11) | copy-start | bytes 1572868
  77.8 33.9 %copy-start.2 = (bf16[2048,128]{1,0:T(8,128)(2,1)}, bf16[2048,128]{1,0:T(8,128)(2,1)S(1)}, u32[]{:S(2)}) copy-start(bf16[2048,128]{1,0:T(8,128)(2,1)S(1)} %all_gather.10) | copy-start | bytes 1572868
  106.9 4.8 copy-start.5
  111.7 2.7 copy-start.6
  111.7 3.3 copy-start.1
  113.7 307.3 %reduce-scatter.4.cloned.1.call-start = ((), (), s32[]{:S(2)}) async-start(), calls=%async_computation.3 | async-start | bytes 1114112 | tf_op jit(solution)/shard_map/reduce_scatter | solution.py:87
  114.4 0.6 copy-start.10
  119.5 166.7 %copy-start.8 = (f32[768]{0:T(1024)}, f32[768]{0:T(1024)S(1)}, u32[]{:S(2)}) copy-start(f32[768]{0:T(1024)S(1)} %gather_fusion) | copy-start | bytes 9220
  289.9 204.9 %reduce-scatter.6.cloned.1.call-start = ((), (), s32[]{:S(2)}) async-start(), calls=%async_computation.4 | async-start | bytes 1114112 | tf_op jit(solution)/shard_map/reduce_scatter | solution.py:88
  291.7 306.4 %reduce-scatter.8.cloned.1.call-start = ((), (), s32[]{:S(2)}) async-start(), calls=%async_computation.5 | async-start | bytes 1114112 | tf_op jit(solution)/shard_map/reduce_scatter | solution.py:90
  295.9 2.2 copy-start.3
  298.1 3.8 copy-start.11
  302.0 112.4 %copy-start.7 = (s32[768]{0:T(1024)S(1)}, s32[768]{0:T(1024)}, u32[]{:S(2)}) copy-start(s32[768]{0:T(1024)} %param.15) | copy-start | bytes 9220
  302.0 112.4 %copy-start.9 = (f32[768]{0:T(1024)S(1)}, f32[768]{0:T(1024)}, u32[]{:S(2)}) copy-start(f32[768]{0:T(1024)} %copy-done.8) | copy-start | bytes 9220
Sparse Core Ops, SparseCore 0:
  113.8 172.2 all-reduce.4
  290.0 101.8 reduce-scatter.3
  395.0 99.7 reduce-scatter.5
  498.1 100.0 reduce-scatter.7
where the time goes:
time: 612 us; the launch traced here: 605 us
  waiting for transfers between devices  340 us (56%)
  blocking collectives  210 us (34%)
  matrix products  16.9 us (3%)
  between operations  14.6 us (2%)
  other arithmetic  12.6 us (2%)
  local copies, waits for them, and re-layouts  10.6 us (2%)
    psum x1, waiting for transfers between devices, local(): lax.psum((gate_part, up_part, back_part), 'col')  166 us
    psum x1, blocking collectives, local(): input_sum, router_sum = lax.psum((input_part, router_part), 'row')  112 us
    reduce_scatter x1, waiting for transfers between devices, local(): lax.psum_scatter(down_term, 'dp', scatter_dimension=1, tiled=True)  102 us
    reduce_scatter x1, waiting for transfers between devices, local(): lax.psum_scatter(up_term, 'dp', scatter_dimension=0, tiled=True)  72.3 us
    all_gather x1, blocking collectives, local(): lax.all_gather(gate_values, 'dp', axis=0, tiled=True)  40.3 us
    all_gather x1, blocking collectives, local(): down_whole = lax.all_gather(down_values, 'dp', axis=1, tiled=True)  29.1 us
    all_gather x1, blocking collectives, local(): lax.all_gather(up_values, 'dp', axis=0, tiled=True)  28 us
  transfers between devices with their start and end apart: 4, of which 3 were waited for; matrix products, arithmetic and copies ran while one was open for 4% of the time, Pallas kernels for 0%

commit v1 on v0

v1 whole, which is shorter than its diff:
```python
import jax
import jax.numpy as jnp
from jax import lax
from jax.experimental import pallas as pl
from jax.experimental.pallas import tpu as pltpu
from jax.sharding import Mesh, PartitionSpec as P

BF = jnp.bfloat16
F32 = jnp.float32
Z, CORES, ROWS, Z_HI, XS = 8, 2, 4, 2, 4
T = 128
CAP = 768
D = 2048
RB = CAP // XS
MSG = RB + 16
AXES = ("z", "core", "row", "zhi", "x")
NT = (((1,), (1,)), ((), ()))
VMEM_LIMIT = 44 * 1024 * 1024


def swap(value, axis, size, mask):
    return lax.ppermute(value, axis, [(i, i ^ mask) for i in range(size)])


def far_first(i):
    return ((i & 1) << 2) | (i & 2) | ((i >> 2) & 1)


def tile_kernel(ids, gs, us, ds, gate, up, down, out):
    dp = ids[0] * CORES + ids[1]
    out[:, 0:T] = (gate[...].astype(F32) * gs[dp, 0]).astype(BF)
    out[:, T : 2 * T] = (up[...].astype(F32) * us[dp, 0]).astype(BF)
    out[:, 2 * T : 3 * T] = (down[...].astype(F32) * ds[0, dp]).T.astype(BF)


def own_tiles(ids, gate_scales, up_scales, down_scales, gate, up, down):
    smem = pl.BlockSpec(memory_space=pltpu.SMEM)
    vmem = pl.BlockSpec(memory_space=pltpu.VMEM)
    return pl.pallas_call(
        tile_kernel,
        out_shape=jax.ShapeDtypeStruct((T, 3 * T), BF),
        in_specs=[smem] * 4 + [vmem] * 3,
        out_specs=vmem,
        name="own_tiles",
    )(ids, gate_scales, up_scales, down_scales, gate, up, down)


def forward_kernel(ids, tokens, out_grad, mine, theirs, own, p1, p2, p3, w_out, w_down):
    step = pl.program_id(0)
    z, core = ids[0], ids[1]

    @pl.when(step == 0)
    def _():
        for i in range(Z):
            base = (z ^ far_first(i)) * (2 * T)
            for ref, side in ((mine, core), (theirs, 1 - core)):
                rows = pl.ds(pl.multiple_of(base + side * T, T), T)
                w_out[rows, :] = ref[i * T : (i + 1) * T, 0 : 2 * T]
                w_down[rows, :] = ref[i * T : (i + 1) * T, 2 * T : 3 * T]

    gate_up = jnp.dot(tokens[...], w_out[...], preferred_element_type=F32)
    back = jnp.dot(out_grad[...], w_down[...], preferred_element_type=F32)

    @pl.when(step == 0)
    def _():
        own[:, 0 : 2 * T] = gate_up
        own[:, 2 * T : 3 * T] = back

    for k, ref in ((1, p1), (2, p2), (3, p3)):

        @pl.when(step == k)
        def _():
            ref[:, 0 : 2 * T] = gate_up.astype(BF)
            ref[:, 2 * T : 3 * T] = back.astype(BF)


def forward(ids, tokens, out_grad, mine, theirs):
    whole = lambda *shape: pl.BlockSpec(shape, lambda r, ids: (0,) * len(shape))
    rows = pl.BlockSpec((RB, D), lambda r, ids: (ids[2] ^ r, 0))
    part = jax.ShapeDtypeStruct((RB, 3 * T), BF)
    return pl.pallas_call(
        forward_kernel,
        grid_spec=pltpu.PrefetchScalarGridSpec(
            num_scalar_prefetch=1,
            grid=(XS,),
            in_specs=[rows, rows, whole(Z * T, 3 * T), whole(Z * T, 3 * T)],
            out_specs=[whole(RB, 3 * T)] * 4 + [whole(D, 2 * T)],
            scratch_shapes=[pltpu.VMEM((D, T), BF)],
        ),
        out_shape=[
            jax.ShapeDtypeStruct((RB, 3 * T), F32),
            part,
            part,
            part,
            jax.ShapeDtypeStruct((D, 2 * T), BF),
        ],
        compiler_params=pltpu.CompilerParams(
            dimension_semantics=("arbitrary",), vmem_limit_bytes=VMEM_LIMIT
        ),
        cost_estimate=pl.CostEstimate(
            flops=2 * CAP * D * 3 * T, bytes_accessed=12 * 1024 * 1024, transcendentals=0
        ),
        name="forward",
    )(ids, tokens, out_grad, mine, theirs)


def delta_kernel(s_mine, s_theirs, weight, out):
    total = s_mine[...].astype(F32) + s_theirs[...].astype(F32)
    gate, up, back = total[:, 0:T], total[:, T : 2 * T], total[:, 2 * T : 3 * T]
    s = jax.nn.sigmoid(gate)
    act = gate * s
    hidden_full = act * up
    delta = back * weight[...]
    out[0:RB, 0:T] = (delta * up * s * (1.0 + gate * (1.0 - s))).astype(BF)
    out[0:RB, T : 2 * T] = (delta * act).astype(BF)
    out[0:RB, 2 * T : 3 * T] = hidden_full.astype(BF)
    router = lax.dot_general(
        jnp.ones((8, T), F32),
        back * hidden_full,
        NT,
        precision=lax.Precision.HIGHEST,
        preferred_element_type=F32,
    )
    router = jnp.concatenate([router, jnp.zeros((8, 2 * T - RB), F32)], axis=1)
    hi = router.astype(BF).astype(F32)
    mid = (router - hi).astype(BF).astype(F32)
    low = router - hi - mid
    row = lax.broadcasted_iota(jnp.int32, (8, 2 * T), 0)
    pieces = jnp.where(row == 0, hi, jnp.where(row == 1, mid, jnp.where(row == 2, low, 0.0)))
    out[RB:MSG, 0 : 2 * T] = jnp.concatenate([pieces, jnp.zeros_like(pieces)], axis=0).astype(BF)
    out[RB:MSG, 2 * T : 3 * T] = jnp.zeros((16, T), BF)


def deltas(s_mine, s_theirs, weight):
    vmem = pl.BlockSpec(memory_space=pltpu.VMEM)
    return pl.pallas_call(
        delta_kernel,
        out_shape=jax.ShapeDtypeStruct((MSG, 3 * T), BF),
        in_specs=[vmem] * 3,
        out_specs=vmem,
        name="deltas",
    )(s_mine, s_theirs, weight)


def weight_grad_kernel(ids, tokens, out_grad, weight, d0, d1, d2, d3, keep, send, flat, turned):
    step = pl.program_id(0)
    core, x = ids[1], ids[2]

    @pl.when(step == 0)
    def _():
        for r, ref in enumerate((d0, d1, d2, d3)):
            rows = pl.ds(pl.multiple_of((x ^ r) * RB, RB), RB)
            flat[rows, :] = ref[0:RB, :]
        turned[...] = flat[...].astype(F32).T.astype(BF)

    scaled = (out_grad[...].astype(F32) * weight[...]).astype(BF)
    gate_up = jnp.dot(turned[0 : 2 * T, :], tokens[...], preferred_element_type=F32)
    down = jnp.dot(turned[2 * T : 3 * T, :], scaled, preferred_element_type=F32)
    for rows, value in ((slice(0, 2 * T), gate_up), (slice(2 * T, 3 * T), down)):
        low, high = value[:, 0:T].astype(BF), value[:, T : 2 * T].astype(BF)
        keep[rows, :] = jnp.where(core == 0, low, high)
        send[rows, :] = jnp.where(core == 0, high, low)


def weight_grads(ids, tokens, out_grad, weight, parts):
    whole = lambda *shape: pl.BlockSpec(shape, lambda i, ids: (0,) * len(shape))
    columns = pl.BlockSpec((CAP, 2 * T), lambda i, ids: (0, ids[0] ^ far_first(i)))
    block = pl.BlockSpec((3 * T, T), lambda i, ids: (i, 0))
    return pl.pallas_call(
        weight_grad_kernel,
        grid_spec=pltpu.PrefetchScalarGridSpec(
            num_scalar_prefetch=1,
            grid=(Z,),
            in_specs=[columns, columns, whole(CAP, 1)] + [whole(MSG, 3 * T)] * 4,
            out_specs=[block, block],
            scratch_shapes=[pltpu.VMEM((CAP, 3 * T), BF), pltpu.VMEM((3 * T, CAP), BF)],
        ),
        out_shape=[jax.ShapeDtypeStruct((Z * 3 * T, T), BF)] * 2,
        compiler_params=pltpu.CompilerParams(
            dimension_semantics=("arbitrary",), vmem_limit_bytes=VMEM_LIMIT
        ),
        cost_estimate=pl.CostEstimate(
            flops=2 * CAP * D * 3 * T, bytes_accessed=12 * 1024 * 1024, transcendentals=0
        ),
        name="weight_grads",
    )(ids, tokens, out_grad, weight, *parts)


def token_grad_kernel(ids, w0, near, far, y0, y1, y2, y3, out, flat):
    step = pl.program_id(0)
    x = ids[2]

    @pl.when(step == 0)
    def _():
        for j, ref in enumerate((y0, y1, y2, y3)):
            for r in range(XS):
                rows = pl.ds(pl.multiple_of((x ^ r) * RB, RB), RB)
                flat[rows, j * 2 * T : (j + 1) * 2 * T] = ref[r * MSG : r * MSG + RB, :]

    def total(ref):
        value = lax.dot_general(flat[:, 0 : 2 * T], w0[...], NT, preferred_element_type=F32)
        for j in range(3):
            value += lax.dot_general(
                flat[:, (j + 1) * 2 * T : (j + 2) * 2 * T],
                ref[j],
                NT,
                preferred_element_type=F32,
            )
        return value.astype(BF)

    @pl.when(step < Z // 2)
    def _():
        out[...] = total(near)

    @pl.when(step >= Z // 2)
    def _():
        out[...] = total(far)


def token_grads(ids, w_own, near, far, rows_by_y):
    whole = lambda *shape: pl.BlockSpec(shape, lambda i, ids: (0,) * len(shape))
    half = Z // 2
    at = lambda i, ids: lax.rem(ids[1] * half + i, Z)
    block = lambda index: pl.BlockSpec((3, 2 * T, 2 * T), lambda i, ids: (0, index(i), 0))
    return pl.pallas_call(
        token_grad_kernel,
        grid_spec=pltpu.PrefetchScalarGridSpec(
            num_scalar_prefetch=1,
            grid=(Z,),
            in_specs=[
                pl.BlockSpec((2 * T, 2 * T), lambda i, ids: (at(i, ids), 0)),
                block(lambda i: jnp.minimum(i, half - 1)),
                block(lambda i: jnp.maximum(i - half, 0)),
            ]
            + [whole(XS * MSG, 2 * T)] * 4,
            out_specs=pl.BlockSpec((CAP, 2 * T), lambda i, ids: (0, at(i, ids))),
            scratch_shapes=[pltpu.VMEM((CAP, 8 * T), BF)],
        ),
        out_shape=jax.ShapeDtypeStruct((CAP, D), BF),
        compiler_params=pltpu.CompilerParams(
            dimension_semantics=("arbitrary",), vmem_limit_bytes=VMEM_LIMIT
        ),
        cost_estimate=pl.CostEstimate(
            flops=2 * CAP * D * 8 * T, bytes_accessed=12 * 1024 * 1024, transcendentals=0
        ),
        name="token_grads",
    )(ids, w_own, near, far, *rows_by_y)


def local(
    tokens,
    out_grad,
    router_logits,
    routed_counts,
    routed_positions,
    gate_values,
    up_values,
    down_values,
    gate_scales,
    up_scales,
    down_scales,
):
    z, core, x = lax.axis_index("z"), lax.axis_index("core"), lax.axis_index("x")
    ids = jnp.stack([z, core, x]).astype(jnp.int32)

    held = own_tiles(ids, gate_scales, up_scales, down_scales, gate_values, up_values, down_values)
    for mask in (4, 2, 1):
        held = jnp.concatenate([held, swap(held, "z", Z, mask)], axis=0)
    held_other = swap(held, "core", CORES, 1)

    live = (jnp.arange(CAP) < routed_counts[0]).astype(F32)
    rate = jax.nn.sigmoid(jnp.take(router_logits, routed_positions))
    weight = rate * live
    weight_column = weight[:, None]
    weight_block = lax.dynamic_slice_in_dim(weight, x * RB, RB)[:, None]

    own, p1, p2, p3, w_own = forward(ids, tokens, out_grad, held, held_other)
    got = [swap(p, "x", XS, r) for r, p in ((1, p1), (2, p2), (3, p3))]
    total = own
    for g in got:
        total = total + g.astype(F32)
    total = total.astype(BF)
    total_other = swap(total, "zhi", Z_HI, 1)

    half = lax.dynamic_slice_in_dim(w_own, core * (D // 2), D // 2, axis=0)
    near = jnp.stack([swap(half, "row", ROWS, r) for r in (1, 2, 3)])
    far = swap(near, "core", CORES, 1)

    message = deltas(total, total_other, weight_block)
    parts = [message] + [swap(message, "x", XS, r) for r in (1, 2, 3)]

    keep, send = weight_grads(ids, tokens, out_grad, weight_column, parts)
    received = swap(send, "core", CORES, 1)
    sums = keep.astype(F32) + received.astype(F32)
    for mask, count in ((1, 4), (2, 2), (4, 1)):
        cut = count * 3 * T
        received = swap(sums[cut:].astype(BF), "z", Z, mask)
        sums = sums[:cut] + received.astype(F32)
    grad_gate = sums[0:T].T
    grad_up = sums[T : 2 * T].T
    grad_down = sums[2 * T : 3 * T]

    rows = jnp.concatenate([p[:, 0 : 2 * T] for p in parts], axis=0)
    rows_by_y = [rows] + [swap(rows, "row", ROWS, r) for r in (1, 2, 3)]
    grad_tokens = token_grads(ids, w_own, near, far, rows_by_y)

    def router_terms(block):
        pieces = block.reshape(XS, MSG, 2 * T)[:, RB : RB + 3, 0:RB].astype(F32)
        return pieces[:, 0] + pieces[:, 1] + pieces[:, 2]

    r0, r1, r2, r3 = (router_terms(block) for block in rows_by_y)
    router = (r0 + r1) + (r2 + r3)
    router = jnp.take(router, x ^ jnp.arange(XS), axis=0).reshape(CAP)
    logit_delta = router * rate * (1.0 - rate) * live
    grad_logits = jnp.zeros(router_logits.shape, F32).at[routed_positions].add(logit_delta)
    return (grad_tokens, grad_gate, grad_up, grad_down, grad_logits)


def solution(mesh):
    fine = Mesh(mesh.devices.reshape(Z, CORES, ROWS, Z_HI, XS), AXES)
    dp, col = ("z", "core"), ("zhi", "x")
    placed = (
        P(dp, col),
        P(dp, col),
        P(dp),
        P(dp),
        P(dp),
        P(col + dp, "row"),
        P(col + dp, "row"),
        P("row", col + dp),
        P(col, "row"),
        P(col, "row"),
        P("row", col),
    )
    return jax.shard_map(
        local,
        mesh=fine,
        in_specs=placed,
        out_specs=(P(dp, col), P(col + dp, "row"), P(col + dp, "row"), P("row", col + dp), P(dp)),
        check_vma=False,
    )
```

time: 612 us -> 233 us (0.38)
  waiting for transfers between devices: 340 us -> 50.5 us
  blocking collectives: 210 us -> 0 us
  starting transfers between devices: 0.16 us -> 113 us
  Pallas kernels: 0 us -> 21.3 us
  local copies, waits for them, and re-layouts: 10.6 us -> 28.4 us
  matrix products: 16.9 us -> 0 us
  between operations: 14.6 us -> 1.82 us
    reduce_scatter x3 -> x0, waiting for transfers between devices: 174 us -> none  [the longest x1 102 us: local(): lax.psum_scatter(down_term, 'dp', scatter_dimension=1, tiled=True)]
    psum x1 -> x0, waiting for transfers between devices: 166 us -> none  [local(): lax.psum((gate_part, up_part, back_part), 'col')]
    ppermute x0 -> x22, starting transfers between devices: none -> 113 us  [swap(): return lax.ppermute(value, axis, [(i, i ^ mask) for i in range(size)])]
    psum x1 -> x0, blocking collectives: 112 us -> none  [local(): input_sum, router_sum = lax.psum((input_part, router_part), 'row')]
    all_gather x3 -> x0, blocking collectives: 97.3 us -> none  [the longest x1 40.3 us: local(): lax.all_gather(gate_values, 'dp', axis=0, tiled=True)]
    ppermute x0 -> x22, waiting for transfers between devices: none -> 50.5 us  [swap(): return lax.ppermute(value, axis, [(i, i ^ mask) for i in range(size)])]
    pallas_call x0 -> x5, Pallas kernels: none -> 21.3 us  [the longest x1 8.79 us: token_grads(): pl.pallas_call(token_grad_kernel, grid_spec=pltpu.PrefetchScalarGridSpec(...]
    dot_general x8 -> x0, matrix products: 16.9 us -> none  [the longest x1 3.78 us: local(): lax.dot_general(up_delta, w_up, CONTRACT_COLS, preferred_element_type=jnp...]
  transfers between devices with their start and end apart: 4 -> 22, of which waited for: 3 -> 11; matrix products, arithmetic and copies ran while one was open for 4% -> 11% of each run, Pallas kernels for 0% -> 3%
where the time goes in v1:
time: 233 us; the launch traced here: 232 us
  starting transfers between devices  113 us (48%)
  waiting for transfers between devices  50.5 us (22%)
  local copies, waits for them, and re-layouts  28.4 us (12%)
  Pallas kernels  21.3 us (9%)
  other arithmetic  16.6 us (7%)
    ppermute x22, starting transfers between devices, swap(): return lax.ppermute(value, axis, [(i, i ^ mask) for i in range(size)])  113 us
    ppermute x22, waiting for transfers between devices, swap(): return lax.ppermute(value, axis, [(i, i ^ mask) for i in range(size)])  50.5 us
    unnamed x42, local copies, waits for them, and re-layouts  17.9 us
    pallas_call x1, Pallas kernels, token_grads(): pl.pallas_call(token_grad_kernel, grid_spec=pltpu.PrefetchScalarGridSpec(...  8.79 us
    scatter-add x1, other arithmetic, local(): jnp.zeros(router_logits.shape, F32).at[routed_positions].add(logit_delta)  6.44 us
    pallas_call x1, Pallas kernels, weight_grads(): pl.pallas_call(weight_grad_kernel, grid_spec=pltpu.PrefetchScalarGridSpec...  4.77 us
  transfers between devices with their start and end apart: 22, of which 11 were waited for; matrix products, arithmetic and copies ran while one was open for 11% of the time, Pallas kernels for 3%

profile of v1, /device:TPU:1, one launch (start us, length us, event | category | flops | bytes accessed | tf_op | source)
XLA Modules:
  0.0 231.5 jit_solution(11450314962286984429)
XLA Ops:
  0.7 1.3 copy.24.gs
  2.0 1.3 copy.25.us
  3.9 1.8 own_tiles.1
  5.8 9.6 %collective-permute-start = (bf16[128,384]{1,0:T(8,128)(2,1)}, bf16[128,384]{1,0:T(8,128)(2,1)S(1)}, u32[]{:S(2)}, u32[]{:S(2)}) collective-permute-start(bf16[128,384]{1,0:T(8,128)(2,1)} %own_tiles.1), channel_id=1, source_target_pairs={{0,256},{64,320},{128,384},{192,448},{256,0},{320,64},{384,128},{4... | collective-permute-start | bytes 294920 | tf_op jit(solution)/shard_map/ppermute | solution.py:22
  15.4 2.2 collective-permute-done
  18.5 8.9 %collective-permute-start.1 = (bf16[256,384]{1,0:T(8,128)(2,1)S(1)}, bf16[256,384]{1,0:T(8,128)(2,1)S(1)}, u32[]{:S(2)}, u32[]{:S(2)}) collective-permute-start(bf16[256,384]{1,0:T(8,128)(2,1)S(1)} %pad_maximum_fusion.4), channel_id=1, source_target_pairs={{0,128},{64,192},{128,0},{192,64},{256,384},{320,448},{384,256},{4... | collective-permute-start | bytes 589832 | tf_op jit(solution)/shard_map/ppermute | solution.py:22
  27.4 3.0 %collective-permute-done.1 = bf16[256,384]{1,0:T(8,128)(2,1)S(1)} collective-permute-done((bf16[256,384]{1,0:T(8,128)(2,1)S(1)}, bf16[256,384]{1,0:T(8,128)(2,1)S(1)}, u32[]{:S(2)}, u32[]{:S(2)}) %collective-permute-start.1) | collective-permute-done | bytes 196640 | tf_op jit(solution)/shard_map/ppermute | solution.py:22
  31.4 8.9 %collective-permute-start.2 = (bf16[512,384]{1,0:T(8,128)(2,1)S(1)}, bf16[512,384]{1,0:T(8,128)(2,1)S(1)}, u32[]{:S(2)}, u32[]{:S(2)}) collective-permute-start(bf16[512,384]{1,0:T(8,128)(2,1)S(1)} %pad_maximum_fusion.3), channel_id=1, source_target_pairs={{0,64},{64,0},{128,192},{192,128},{256,320},{320,256},{384,448},{4... | collective-permute-start | bytes 1179656 | tf_op jit(solution)/shard_map/ppermute | solution.py:22
  40.3 7.8 %collective-permute-done.2 = bf16[512,384]{1,0:T(8,128)(2,1)S(1)} collective-permute-done((bf16[512,384]{1,0:T(8,128)(2,1)S(1)}, bf16[512,384]{1,0:T(8,128)(2,1)S(1)}, u32[]{:S(2)}, u32[]{:S(2)}) %collective-permute-start.2) | collective-permute-done | bytes 393248 | tf_op jit(solution)/shard_map/ppermute | solution.py:22
  49.0 4.2 %collective-permute-start.3 = (bf16[1024,384]{1,0:T(8,128)(2,1)S(1)}, bf16[1024,384]{1,0:T(8,128)(2,1)S(1)}, u32[]{:S(2)}, u32[]{:S(2)}) collective-permute-start(bf16[1024,384]{1,0:T(8,128)(2,1)S(1)} %pad_maximum_fusion.1.mine), channel_id=1, source_target_pairs={{0,32},{32,0},{1,33},{33,1},{2,34},{34,2},{3,35},{35,3},{4,36},{36... | collective-permute-start | bytes 2359304 | tf_op jit(solution)/shard_map/ppermute | solution.py:22
  53.2 1.9 collective-permute-done.3.theirs
  55.1 1.9 copy-done.1
  57.0 1.9 copy-done.3
  58.9 3.9 %forward.1 = (f32[192,384]{1,0:T(8,128)S(1)}, bf16[192,384]{1,0:T(8,128)(2,1)}, bf16[192,384]{1,0:T(8,128)(2,1)}, bf16[192,384]{1,0:T(8,128)(2,1)}, bf16[2048,256]{1,0:T(8,128)(2,1)S(1)}) custom-call(s32[3]{0:T(128)S(1)} %copy-done.8, bf16[768,2048]{1,0:T(8,128)(2,1)S(1)} %copy-done.1, bf16[768,2048]{1,0:T(8,128)(2,1)S(1)} %copy-done.3, ...), custom_call_target="tpu_custom_call" | custom-call | flops 1207959552 | bytes 12582912 | tf_op jit(solution)/shard_map/forward/pallas_call | solution.py:81
  63.8 3.1 %collective-permute-start.8 = (bf16[192,384]{1,0:T(8,128)(2,1)}, bf16[192,384]{1,0:T(8,128)(2,1)}, u32[]{:S(2)}, u32[]{:S(2)}) collective-permute-start(bf16[192,384]{1,0:T(8,128)(2,1)} %get-tuple-element.14), channel_id=1, source_target_pairs={{0,1},{1,0},{2,3},{3,2},{4,5},{5,4},{6,7},{7,6},{8,9},{9,8},{10,11... | collective-permute-start | bytes 442376 | tf_op jit(solution)/shard_map/ppermute | solution.py:22
  66.9 4.4 %collective-permute-start.9 = (bf16[192,384]{1,0:T(8,128)(2,1)}, bf16[192,384]{1,0:T(8,128)(2,1)}, u32[]{:S(2)}, u32[]{:S(2)}) collective-permute-start(bf16[192,384]{1,0:T(8,128)(2,1)} %get-tuple-element.15), channel_id=1, source_target_pairs={{0,2},{1,3},{2,0},{3,1},{4,6},{5,7},{6,4},{7,5},{8,10},{9,11},{10,... | collective-permute-start | bytes 442376 | tf_op jit(solution)/shard_map/ppermute | solution.py:22
  71.3 2.1 collective-permute-start.10
  74.1 4.5 %gather_fusion = f32[768]{0:T(1024)S(1)} fusion(f32[6144]{0:T(1024)S(1)} %copy-done, s32[1024]{0:T(1024)S(1)} %pad_clamp_fusion.1), kind=kCustom, calls=%fused_computation | custom fusion | bytes 9216 | tf_op jit(solution)/shard_map/jit(_take)/gather | solution.py:272
  78.5 2.0 constant_dynamic-slice_fusion
  80.6 4.6 %collective-permute-start.6 = (bf16[1024,256]{1,0:T(8,128)(2,1)}, bf16[1024,256]{1,0:T(8,128)(2,1)}, u32[]{:S(2)}, u32[]{:S(2)}) collective-permute-start(bf16[1024,256]{1,0:T(8,128)(2,1)} %constant_dynamic-slice_fusion), channel_id=1, source_target_pairs={{0,24},{8,16},{16,8},{24,0},{1,25},{9,17},{17,9},{25,1},{2,26},{10... | collective-permute-start | bytes 1572872 | tf_op jit(solution)/shard_map/ppermute | solution.py:22
  85.2 2.3 collective-permute-start.5
  87.5 1.8 add_convert_fusion.s_mine
  89.3 15.8 %collective-permute-start.11 = (bf16[192,384]{1,0:T(8,128)(2,1)}, bf16[192,384]{1,0:T(8,128)(2,1)S(1)}, u32[]{:S(2)}, u32[]{:S(2)}) collective-permute-start(bf16[192,384]{1,0:T(8,128)(2,1)} %add_convert_fusion.s_mine), channel_id=1, source_target_pairs={{0,4},{4,0},{1,5},{5,1},{2,6},{6,2},{3,7},{7,3},{8,12},{12,8},{9,1... | collective-permute-start | bytes 442376 | tf_op jit(solution)/shard_map/ppermute | solution.py:22
  106.0 2.2 collective-permute-done.11.s_theirs
  108.8 2.0 deltas.1.d0
  110.8 4.4 %collective-permute-start.14 = (bf16[208,384]{1,0:T(8,128)(2,1)}, bf16[208,384]{1,0:T(8,128)(2,1)S(1)}, u32[]{:S(2)}, u32[]{:S(2)}) collective-permute-start(bf16[208,384]{1,0:T(8,128)(2,1)} %deltas.1.d0), channel_id=1, source_target_pairs={{0,3},{1,2},{2,1},{3,0},{4,7},{5,6},{6,5},{7,4},{8,11},{9,10},{10,... | collective-permute-start | bytes 479240 | tf_op jit(solution)/shard_map/ppermute | solution.py:22
  115.2 1.9 collective-permute-start.13
  117.1 2.7 %collective-permute-start.12 = (bf16[208,384]{1,0:T(8,128)(2,1)}, bf16[208,384]{1,0:T(8,128)(2,1)S(1)}, u32[]{:S(2)}, u32[]{:S(2)}) collective-permute-start(bf16[208,384]{1,0:T(8,128)(2,1)} %deltas.1.d0), channel_id=1, source_target_pairs={{0,1},{1,0},{2,3},{3,2},{4,5},{5,4},{6,7},{7,6},{8,9},{9,8},{10,11... | collective-permute-start | bytes 479240 | tf_op jit(solution)/shard_map/ppermute | solution.py:22
  120.9 2.1 collective-permute-start.4
  123.3 1.9 copy-done.4
  126.1 4.8 %weight_grads.1 = (bf16[3072,128]{1,0:T(8,128)(2,1)S(1)}, bf16[3072,128]{1,0:T(8,128)(2,1)S(1)}) custom-call(s32[3]{0:T(128)S(1)} %copy-done.8, bf16[768,2048]{1,0:T(8,128)(2,1)S(1)} %copy-done.2, bf16[768,2048]{1,0:T(8,128)(2,1)S(1)} %copy-done.4, f32[768,1]{1,0:T(8,128)S(1)} %mul.27.weight, bf16[208,384]{1,0:T(8,128)(2,1)S(1)} %copy-done.5, ...), custom_call_target="tpu_custom_call" | custom-call | flops 1207959552 | bytes 12582912 | tf_op jit(solution)/shard_map/weight_grads/pallas_call | solution.py:169
  130.9 11.5 %collective-permute-start.18 = (bf16[3072,128]{1,0:T(8,128)(2,1)S(1)}, bf16[3072,128]{1,0:T(8,128)(2,1)S(1)}, u32[]{:S(2)}, u32[]{:S(2)}) collective-permute-start(bf16[3072,128]{1,0:T(8,128)(2,1)S(1)} %get-tuple-element.18), channel_id=1, source_target_pairs={{0,32},{32,0},{1,33},{33,1},{2,34},{34,2},{3,35},{35,3},{4,36},{36... | collective-permute-start | bytes 2359304 | tf_op jit(solution)/shard_map/ppermute | solution.py:22
  142.6 4.0 %collective-permute-start.17 = (bf16[832,256]{1,0:T(8,128)(2,1)S(1)}, bf16[832,256]{1,0:T(8,128)(2,1)S(1)}, u32[]{:S(2)}, u32[]{:S(2)}) collective-permute-start(bf16[832,256]{1,0:T(8,128)(2,1)S(1)} %pad_maximum_fusion.2.y0), channel_id=1, source_target_pairs={{0,24},{8,16},{16,8},{24,0},{1,25},{9,17},{17,9},{25,1},{2,26},{10... | collective-permute-start | bytes 1277960 | tf_op jit(solution)/shard_map/ppermute | solution.py:22
  146.5 2.5 %collective-permute-start.16 = (bf16[832,256]{1,0:T(8,128)(2,1)S(1)}, bf16[832,256]{1,0:T(8,128)(2,1)S(1)}, u32[]{:S(2)}, u32[]{:S(2)}) collective-permute-start(bf16[832,256]{1,0:T(8,128)(2,1)S(1)} %pad_maximum_fusion.2.y0), channel_id=1, source_target_pairs={{0,16},{8,24},{16,0},{24,8},{1,17},{9,25},{17,1},{25,9},{2,18},{10... | collective-permute-start | bytes 1277960 | tf_op jit(solution)/shard_map/ppermute | solution.py:22
  149.1 2.5 %collective-permute-start.15 = (bf16[832,256]{1,0:T(8,128)(2,1)S(1)}, bf16[832,256]{1,0:T(8,128)(2,1)S(1)}, u32[]{:S(2)}, u32[]{:S(2)}) collective-permute-start(bf16[832,256]{1,0:T(8,128)(2,1)S(1)} %pad_maximum_fusion.2.y0), channel_id=1, source_target_pairs={{0,8},{8,0},{16,24},{24,16},{1,9},{9,1},{17,25},{25,17},{2,10},{10... | collective-permute-start | bytes 1277960 | tf_op jit(solution)/shard_map/ppermute | solution.py:22
  151.7 1.4 pad_maximum_fusion.near
  153.0 2.8 %collective-permute-start.7 = (bf16[3,1024,256]{2,1,0:T(8,128)(2,1)S(1)}, bf16[3,1024,256]{2,1,0:T(8,128)(2,1)}, u32[]{:S(2)}, u32[]{:S(2)}) collective-permute-start(bf16[3,1024,256]{2,1,0:T(8,128)(2,1)S(1)} %pad_maximum_fusion.near), channel_id=1, source_target_pairs={{0,32},{32,0},{1,33},{33,1},{2,34},{34,2},{3,35},{35,3},{4,36},{36... | collective-permute-start | bytes 4718600 | tf_op jit(solution)/shard_map/ppermute | solution.py:22
  155.8 10.4 %collective-permute-done.17.y3 = bf16[832,256]{1,0:T(8,128)(2,1)S(1)} collective-permute-done((bf16[832,256]{1,0:T(8,128)(2,1)S(1)}, bf16[832,256]{1,0:T(8,128)(2,1)S(1)}, u32[]{:S(2)}, u32[]{:S(2)}) %collective-permute-start.17) | collective-permute-done | bytes 426016 | tf_op jit(solution)/shard_map/ppermute | solution.py:22
  166.3 2.2 collective-permute-done.15.y1
  170.4 5.3 %collective-permute-start.19 = (bf16[1536,128]{1,0:T(8,128)(2,1)S(1)}, bf16[1536,128]{1,0:T(8,128)(2,1)S(1)}, u32[]{:S(2)}, u32[]{:S(2)}) collective-permute-start(bf16[1536,128]{1,0:T(8,128)(2,1)S(1)} %slice.194), channel_id=1, source_target_pairs={{0,64},{64,0},{128,192},{192,128},{256,320},{320,256},{384,448},{4... | collective-permute-start | bytes 1179656 | tf_op jit(solution)/shard_map/ppermute | solution.py:22
  176.2 7.7 %collective-permute-done.19 = bf16[1536,128]{1,0:T(8,128)(2,1)S(1)} collective-permute-done((bf16[1536,128]{1,0:T(8,128)(2,1)S(1)}, bf16[1536,128]{1,0:T(8,128)(2,1)S(1)}, u32[]{:S(2)}, u32[]{:S(2)}) %collective-permute-start.19) | collective-permute-done | bytes 393248 | tf_op jit(solution)/shard_map/ppermute | solution.py:22
  184.0 1.2 slice_add_fusion
  186.1 2.1 collective-permute-start.20
  188.3 10.9 %collective-permute-done.20 = bf16[768,128]{1,0:T(8,128)(2,1)} collective-permute-done((bf16[768,128]{1,0:T(8,128)(2,1)S(1)}, bf16[768,128]{1,0:T(8,128)(2,1)}, u32[]{:S(2)}, u32[]{:S(2)}) %collective-permute-start.20) | collective-permute-done | bytes 196640 | tf_op jit(solution)/shard_map/ppermute | solution.py:22
  201.0 7.4 %collective-permute-start.21 = (bf16[384,128]{1,0:T(8,128)(2,1)}, bf16[384,128]{1,0:T(8,128)(2,1)}, u32[]{:S(2)}, u32[]{:S(2)}) collective-permute-start(bf16[384,128]{1,0:T(8,128)(2,1)} %slice.196), channel_id=1, source_target_pairs={{0,256},{64,320},{128,384},{192,448},{256,0},{320,64},{384,128},{4... | collective-permute-start | bytes 294920 | tf_op jit(solution)/shard_map/ppermute | solution.py:22
  208.4 6.4 %scatter_custom_fusion = f32[6144]{0:T(1024)} fusion(s32[768]{0:T(1024)S(1)} %compare_select_fusion, f32[768]{0:T(1024)S(1)} %multiply_select_fusion, f32[]{:T(128)} %constant.58.clone.1), kind=kCustom, calls=%fused_computation.18 | custom fusion | flops 768 | bytes 24580 | tf_op jit(solution)/shard_map/scatter-add | solution.py:315
  214.8 1.8 collective-permute-done.21
  222.7 8.8 %token_grads.1 = bf16[768,2048]{1,0:T(8,128)(2,1)} custom-call(s32[3]{0:T(128)S(1)} %copy-done.8, bf16[2048,256]{1,0:T(8,128)(2,1)S(1)} %copy-done.7, bf16[3,1024,256]{2,1,0:T(8,128)(2,1)S(1)} %pad_maximum_fusion.near, bf16[3,1024,256]{2,1,0:T(8,128)(2,1)} %collective-permute-done.7.far, bf16[832,256]{1,0:T(8,128)(2,1)S(1)} %pad_maximum_fusion.2.y0, ...), custom_call_target="tpu_custom_call" | custom-call | flops 3221225472 | bytes 12582912 | tf_op jit(solution)/shard_map/token_grads/pallas_call | solution.py:225
  (85 shorter events, 19.7 us)
Async XLA Ops:
  0.6 73.4 %copy-start = (f32[6144]{0:T(1024)S(1)}, f32[6144]{0:T(1024)}, u32[]{:S(2)}) copy-start(f32[6144]{0:T(1024)} %param.13) | copy-start | bytes 73732
  0.6 52.6 %copy-start.18 = (s32[768]{0:T(1024)S(1)}, s32[768]{0:T(1024)}, u32[]{:S(2)}) copy-start(s32[768]{0:T(1024)} %param.15) | copy-start | bytes 9220
  3.9 51.1 %copy-start.8 = (s32[3]{0:T(128)S(1)}, s32[3]{0:T(128)}, u32[]{:S(2)}) copy-start(s32[3]{0:T(128)} %pad_add_fusion.ids) | copy-start | bytes 40
  5.8 11.8 %collective-permute-start = (bf16[128,384]{1,0:T(8,128)(2,1)}, bf16[128,384]{1,0:T(8,128)(2,1)S(1)}, u32[]{:S(2)}, u32[]{:S(2)}) collective-permute-start(bf16[128,384]{1,0:T(8,128)(2,1)} %own_tiles.1), channel_id=1, source_target_pairs={{0,256},{64,320},{128,384},{192,448},{256,0},{320,64},{384,128},{4... | collective-permute-start | bytes 294920 | tf_op jit(solution)/shard_map/ppermute | solution.py:22
  18.5 11.9 %collective-permute-start.1 = (bf16[256,384]{1,0:T(8,128)(2,1)S(1)}, bf16[256,384]{1,0:T(8,128)(2,1)S(1)}, u32[]{:S(2)}, u32[]{:S(2)}) collective-permute-start(bf16[256,384]{1,0:T(8,128)(2,1)S(1)} %pad_maximum_fusion.4), channel_id=1, source_target_pairs={{0,128},{64,192},{128,0},{192,64},{256,384},{320,448},{384,256},{4... | collective-permute-start | bytes 589832 | tf_op jit(solution)/shard_map/ppermute | solution.py:22
  31.4 16.7 %collective-permute-start.2 = (bf16[512,384]{1,0:T(8,128)(2,1)S(1)}, bf16[512,384]{1,0:T(8,128)(2,1)S(1)}, u32[]{:S(2)}, u32[]{:S(2)}) collective-permute-start(bf16[512,384]{1,0:T(8,128)(2,1)S(1)} %pad_maximum_fusion.3), channel_id=1, source_target_pairs={{0,64},{64,0},{128,192},{192,128},{256,320},{320,256},{384,448},{4... | collective-permute-start | bytes 1179656 | tf_op jit(solution)/shard_map/ppermute | solution.py:22
  49.0 6.1 %collective-permute-start.3 = (bf16[1024,384]{1,0:T(8,128)(2,1)S(1)}, bf16[1024,384]{1,0:T(8,128)(2,1)S(1)}, u32[]{:S(2)}, u32[]{:S(2)}) collective-permute-start(bf16[1024,384]{1,0:T(8,128)(2,1)S(1)} %pad_maximum_fusion.1.mine), channel_id=1, source_target_pairs={{0,32},{32,0},{1,33},{33,1},{2,34},{34,2},{3,35},{35,3},{4,36},{36... | collective-permute-start | bytes 2359304 | tf_op jit(solution)/shard_map/ppermute | solution.py:22
  55.1 1.9 copy-start.1
  57.0 1.9 copy-start.3
  62.8 1.0 copy-start.6
  63.8 23.7 %collective-permute-start.8 = (bf16[192,384]{1,0:T(8,128)(2,1)}, bf16[192,384]{1,0:T(8,128)(2,1)}, u32[]{:S(2)}, u32[]{:S(2)}) collective-permute-start(bf16[192,384]{1,0:T(8,128)(2,1)} %get-tuple-element.14), channel_id=1, source_target_pairs={{0,1},{1,0},{2,3},{3,2},{4,5},{5,4},{6,7},{7,6},{8,9},{9,8},{10,11... | collective-permute-start | bytes 442376 | tf_op jit(solution)/shard_map/ppermute | solution.py:22
  66.9 20.6 %collective-permute-start.9 = (bf16[192,384]{1,0:T(8,128)(2,1)}, bf16[192,384]{1,0:T(8,128)(2,1)}, u32[]{:S(2)}, u32[]{:S(2)}) collective-permute-start(bf16[192,384]{1,0:T(8,128)(2,1)} %get-tuple-element.15), channel_id=1, source_target_pairs={{0,2},{1,3},{2,0},{3,1},{4,6},{5,7},{6,4},{7,5},{8,10},{9,11},{10,... | collective-permute-start | bytes 442376 | tf_op jit(solution)/shard_map/ppermute | solution.py:22
  71.3 16.2 %collective-permute-start.10 = (bf16[192,384]{1,0:T(8,128)(2,1)}, bf16[192,384]{1,0:T(8,128)(2,1)}, u32[]{:S(2)}, u32[]{:S(2)}) collective-permute-start(bf16[192,384]{1,0:T(8,128)(2,1)} %get-tuple-element.16), channel_id=1, source_target_pairs={{0,3},{1,2},{2,1},{3,0},{4,7},{5,6},{6,5},{7,4},{8,11},{9,10},{10,... | collective-permute-start | bytes 442376 | tf_op jit(solution)/shard_map/ppermute | solution.py:22
  78.5 44.8 %copy-start.2 = (bf16[768,2048]{1,0:T(8,128)(2,1)S(1)}, bf16[768,2048]{1,0:T(8,128)(2,1)}, u32[]{:S(2)}) copy-start(bf16[768,2048]{1,0:T(8,128)(2,1)} %tokens.3) | copy-start | bytes 9437188
  80.6 66.0 %collective-permute-start.6 = (bf16[1024,256]{1,0:T(8,128)(2,1)}, bf16[1024,256]{1,0:T(8,128)(2,1)}, u32[]{:S(2)}, u32[]{:S(2)}) collective-permute-start(bf16[1024,256]{1,0:T(8,128)(2,1)} %constant_dynamic-slice_fusion), channel_id=1, source_target_pairs={{0,24},{8,16},{16,8},{24,0},{1,25},{9,17},{17,9},{25,1},{2,26},{10... | collective-permute-start | bytes 1572872 | tf_op jit(solution)/shard_map/ppermute | solution.py:22
  85.2 63.9 %collective-permute-start.5 = (bf16[1024,256]{1,0:T(8,128)(2,1)}, bf16[1024,256]{1,0:T(8,128)(2,1)}, u32[]{:S(2)}, u32[]{:S(2)}) collective-permute-start(bf16[1024,256]{1,0:T(8,128)(2,1)} %constant_dynamic-slice_fusion), channel_id=1, source_target_pairs={{0,16},{8,24},{16,0},{24,8},{1,17},{9,25},{17,1},{25,9},{2,18},{10... | collective-permute-start | bytes 1572872 | tf_op jit(solution)/shard_map/ppermute | solution.py:22
  89.3 18.8 %collective-permute-start.11 = (bf16[192,384]{1,0:T(8,128)(2,1)}, bf16[192,384]{1,0:T(8,128)(2,1)S(1)}, u32[]{:S(2)}, u32[]{:S(2)}) collective-permute-start(bf16[192,384]{1,0:T(8,128)(2,1)} %add_convert_fusion.s_mine), channel_id=1, source_target_pairs={{0,4},{4,0},{1,5},{5,1},{2,6},{6,2},{3,7},{7,3},{8,12},{12,8},{9,1... | collective-permute-start | bytes 442376 | tf_op jit(solution)/shard_map/ppermute | solution.py:22
  108.1 0.7 copy-start.17
  110.8 10.1 %collective-permute-start.14 = (bf16[208,384]{1,0:T(8,128)(2,1)}, bf16[208,384]{1,0:T(8,128)(2,1)S(1)}, u32[]{:S(2)}, u32[]{:S(2)}) collective-permute-start(bf16[208,384]{1,0:T(8,128)(2,1)} %deltas.1.d0), channel_id=1, source_target_pairs={{0,3},{1,2},{2,1},{3,0},{4,7},{5,6},{6,5},{7,4},{8,11},{9,10},{10,... | collective-permute-start | bytes 479240 | tf_op jit(solution)/shard_map/ppermute | solution.py:22
  115.2 7.8 %collective-permute-start.13 = (bf16[208,384]{1,0:T(8,128)(2,1)}, bf16[208,384]{1,0:T(8,128)(2,1)S(1)}, u32[]{:S(2)}, u32[]{:S(2)}) collective-permute-start(bf16[208,384]{1,0:T(8,128)(2,1)} %deltas.1.d0), channel_id=1, source_target_pairs={{0,2},{1,3},{2,0},{3,1},{4,6},{5,7},{6,4},{7,5},{8,10},{9,11},{10,... | collective-permute-start | bytes 479240 | tf_op jit(solution)/shard_map/ppermute | solution.py:22
  117.1 6.2 %collective-permute-start.12 = (bf16[208,384]{1,0:T(8,128)(2,1)}, bf16[208,384]{1,0:T(8,128)(2,1)S(1)}, u32[]{:S(2)}, u32[]{:S(2)}) collective-permute-start(bf16[208,384]{1,0:T(8,128)(2,1)} %deltas.1.d0), channel_id=1, source_target_pairs={{0,1},{1,0},{2,3},{3,2},{4,5},{5,4},{6,7},{7,6},{8,9},{9,8},{10,11... | collective-permute-start | bytes 479240 | tf_op jit(solution)/shard_map/ppermute | solution.py:22
  120.9 30.8 %collective-permute-start.4 = (bf16[1024,256]{1,0:T(8,128)(2,1)}, bf16[1024,256]{1,0:T(8,128)(2,1)S(1)}, u32[]{:S(2)}, u32[]{:S(2)}) collective-permute-start(bf16[1024,256]{1,0:T(8,128)(2,1)} %constant_dynamic-slice_fusion), channel_id=1, source_target_pairs={{0,8},{8,0},{16,24},{24,16},{1,9},{9,1},{17,25},{25,17},{2,10},{10... | collective-permute-start | bytes 1572872 | tf_op jit(solution)/shard_map/ppermute | solution.py:22
  123.3 1.9 copy-start.4
  125.2 0.9 copy-start.5
  130.9 37.6 %collective-permute-start.18 = (bf16[3072,128]{1,0:T(8,128)(2,1)S(1)}, bf16[3072,128]{1,0:T(8,128)(2,1)S(1)}, u32[]{:S(2)}, u32[]{:S(2)}) collective-permute-start(bf16[3072,128]{1,0:T(8,128)(2,1)S(1)} %get-tuple-element.18), channel_id=1, source_target_pairs={{0,32},{32,0},{1,33},{33,1},{2,34},{34,2},{3,35},{35,3},{4,36},{36... | collective-permute-start | bytes 2359304 | tf_op jit(solution)/shard_map/ppermute | solution.py:22
  142.6 23.7 %collective-permute-start.17 = (bf16[832,256]{1,0:T(8,128)(2,1)S(1)}, bf16[832,256]{1,0:T(8,128)(2,1)S(1)}, u32[]{:S(2)}, u32[]{:S(2)}) collective-permute-start(bf16[832,256]{1,0:T(8,128)(2,1)S(1)} %pad_maximum_fusion.2.y0), channel_id=1, source_target_pairs={{0,24},{8,16},{16,8},{24,0},{1,25},{9,17},{17,9},{25,1},{2,26},{10... | collective-permute-start | bytes 1277960 | tf_op jit(solution)/shard_map/ppermute | solution.py:22
  146.5 19.7 %collective-permute-start.16 = (bf16[832,256]{1,0:T(8,128)(2,1)S(1)}, bf16[832,256]{1,0:T(8,128)(2,1)S(1)}, u32[]{:S(2)}, u32[]{:S(2)}) collective-permute-start(bf16[832,256]{1,0:T(8,128)(2,1)S(1)} %pad_maximum_fusion.2.y0), channel_id=1, source_target_pairs={{0,16},{8,24},{16,0},{24,8},{1,17},{9,25},{17,1},{25,9},{2,18},{10... | collective-permute-start | bytes 1277960 | tf_op jit(solution)/shard_map/ppermute | solution.py:22
  149.1 19.4 %collective-permute-start.15 = (bf16[832,256]{1,0:T(8,128)(2,1)S(1)}, bf16[832,256]{1,0:T(8,128)(2,1)S(1)}, u32[]{:S(2)}, u32[]{:S(2)}) collective-permute-start(bf16[832,256]{1,0:T(8,128)(2,1)S(1)} %pad_maximum_fusion.2.y0), channel_id=1, source_target_pairs={{0,8},{8,0},{16,24},{24,16},{1,9},{9,1},{17,25},{25,17},{2,10},{10... | collective-permute-start | bytes 1277960 | tf_op jit(solution)/shard_map/ppermute | solution.py:22
  153.0 66.7 %collective-permute-start.7 = (bf16[3,1024,256]{2,1,0:T(8,128)(2,1)S(1)}, bf16[3,1024,256]{2,1,0:T(8,128)(2,1)}, u32[]{:S(2)}, u32[]{:S(2)}) collective-permute-start(bf16[3,1024,256]{2,1,0:T(8,128)(2,1)S(1)} %pad_maximum_fusion.near), channel_id=1, source_target_pairs={{0,32},{32,0},{1,33},{33,1},{2,34},{34,2},{3,35},{35,3},{4,36},{36... | collective-permute-start | bytes 4718600 | tf_op jit(solution)/shard_map/ppermute | solution.py:22
  166.2 2.4 %copy-start.9 = (bf16[832,256]{1,0:T(8,128)(2,1)}, bf16[832,256]{1,0:T(8,128)(2,1)S(1)}, u32[]{:S(2)}) copy-start(bf16[832,256]{1,0:T(8,128)(2,1)S(1)} %collective-permute-done.17.y3) | copy-start | bytes 1277956
  166.3 2.4 %copy-start.11 = (bf16[832,256]{1,0:T(8,128)(2,1)}, bf16[832,256]{1,0:T(8,128)(2,1)S(1)}, u32[]{:S(2)}) copy-start(bf16[832,256]{1,0:T(8,128)(2,1)S(1)} %collective-permute-done.16.y2) | copy-start | bytes 1277956
  168.5 0.8 copy-start.13
  169.2 1.1 copy-start.15
  170.4 13.6 %collective-permute-start.19 = (bf16[1536,128]{1,0:T(8,128)(2,1)S(1)}, bf16[1536,128]{1,0:T(8,128)(2,1)S(1)}, u32[]{:S(2)}, u32[]{:S(2)}) collective-permute-start(bf16[1536,128]{1,0:T(8,128)(2,1)S(1)} %slice.194), channel_id=1, source_target_pairs={{0,64},{64,0},{128,192},{192,128},{256,320},{320,256},{384,448},{4... | collective-permute-start | bytes 1179656 | tf_op jit(solution)/shard_map/ppermute | solution.py:22
  185.2 0.9 copy-start.16
  186.1 33.6 %copy-start.7 = (bf16[2048,256]{1,0:T(8,128)(2,1)S(1)}, bf16[2048,256]{1,0:T(8,128)(2,1)}, u32[]{:S(2)}) copy-start(bf16[2048,256]{1,0:T(8,128)(2,1)} %copy-done.6) | copy-start | bytes 3145732
  186.1 13.1 %collective-permute-start.20 = (bf16[768,128]{1,0:T(8,128)(2,1)S(1)}, bf16[768,128]{1,0:T(8,128)(2,1)}, u32[]{:S(2)}, u32[]{:S(2)}) collective-permute-start(bf16[768,128]{1,0:T(8,128)(2,1)S(1)} %slice.195), channel_id=1, source_target_pairs={{0,128},{64,192},{128,0},{192,64},{256,384},{320,448},{384,256},{4... | collective-permute-start | bytes 589832 | tf_op jit(solution)/shard_map/ppermute | solution.py:22
  201.0 15.7 %collective-permute-start.21 = (bf16[384,128]{1,0:T(8,128)(2,1)}, bf16[384,128]{1,0:T(8,128)(2,1)}, u32[]{:S(2)}, u32[]{:S(2)}) collective-permute-start(bf16[384,128]{1,0:T(8,128)(2,1)} %slice.196), channel_id=1, source_target_pairs={{0,256},{64,320},{128,384},{192,448},{256,0},{320,64},{384,128},{4... | collective-permute-start | bytes 294920 | tf_op jit(solution)/shard_map/ppermute | solution.py:22
  219.7 1.0 copy-start.10
  220.7 1.0 copy-start.12
  221.7 1.0 copy-start.14

commit v2 on v1

v2 whole, which is shorter than its diff:
```python
import jax
import jax.numpy as jnp
from jax import lax
from jax.experimental import pallas as pl
from jax.experimental.pallas import tpu as pltpu
from jax.sharding import Mesh, PartitionSpec as P

BF = jnp.bfloat16
F32 = jnp.float32
Z, CORES, ROWS, Z_HI, XS = 8, 2, 4, 2, 4
T = 128
CAP = 768
SEQ = 6144
D = 2048
RB = CAP // XS
MSG = RB + 16
AXES = ("z", "core", "row", "zhi", "x")
NT = (((1,), (1,)), ((), ()))


def swap(value, axis, size, mask):
    return lax.ppermute(value, axis, [(i, i ^ mask) for i in range(size)])


def far_first(i):
    return ((i & 1) << 2) | (i & 2) | ((i >> 2) & 1)


def split3(value):
    hi = value.astype(BF)
    rest = value - hi.astype(F32)
    mid = rest.astype(BF)
    return hi, mid, (rest - mid.astype(F32)).astype(BF)


def params(mib=24):
    return pltpu.CompilerParams(
        dimension_semantics=("arbitrary",), vmem_limit_bytes=mib * 1024 * 1024
    )


def work(flops, mib):
    return pl.CostEstimate(flops=flops, bytes_accessed=mib * 1024 * 1024, transcendentals=0)


VMEM = pl.BlockSpec(memory_space=pltpu.VMEM)
SMEM = pl.BlockSpec(memory_space=pltpu.SMEM)
ANY = pl.BlockSpec(memory_space=pl.ANY)
HBM = pl.BlockSpec(memory_space=pltpu.HBM)


def turn(row):
    return jnp.broadcast_to(row, (8, row.shape[1])).T[:, 0:1]


def rates_kernel(logits, positions, counts, out):
    place = turn(positions[...].astype(F32))
    at = place.astype(jnp.int32)
    lanes = lax.broadcasted_iota(jnp.int32, (CAP, T), 1)
    upper = jnp.where(lanes[:, 0 : SEQ // T] == (at >> 7), 1.0, 0.0).astype(BF)
    picked = jnp.zeros((CAP, T), F32)
    for piece in split3(logits[...]):
        picked = picked + jnp.dot(upper, piece, preferred_element_type=F32)
    logit = jnp.sum(jnp.where(lanes == (at & (T - 1)), picked, 0.0), axis=1, keepdims=True)
    rate = jax.nn.sigmoid(logit)
    row = lax.broadcasted_iota(jnp.int32, (CAP, 1), 0)
    live = jnp.where(row < counts[0], 1.0, 0.0)
    weight = rate * live
    slope = rate * (1.0 - rate) * live
    out[...] = jnp.where(lanes == 0, weight, jnp.where(lanes == 1, slope, place))


def rates(logits, positions, counts):
    return pl.pallas_call(
        rates_kernel,
        out_shape=jax.ShapeDtypeStruct((CAP, T), F32),
        in_specs=[VMEM, VMEM, SMEM],
        out_specs=VMEM,
        name="rates",
    )(logits, positions, counts)


def tile_kernel(ids, gs, us, ds, gate, up, down, out):
    dp = ids[0] * CORES + ids[1]
    lane = lax.broadcasted_iota(jnp.int32, (1, Z * CORES), 1)
    g, u, d = (
        jnp.sum(jnp.where(lane == dp, ref[...], 0.0), axis=1, keepdims=True) for ref in (gs, us, ds)
    )
    out[:, 0:T] = (gate[...].astype(F32) * g).astype(BF)
    out[:, T : 2 * T] = (up[...].astype(F32) * u).astype(BF)
    out[:, 2 * T : 3 * T] = (down[...].astype(F32) * d).T.astype(BF)


def own_tiles(ids, gate_scales, up_scales, down_scales, gate, up, down):
    return pl.pallas_call(
        tile_kernel,
        out_shape=jax.ShapeDtypeStruct((T, 3 * T), BF),
        in_specs=[SMEM] + [VMEM] * 6,
        out_specs=VMEM,
        name="own_tiles",
    )(ids, gate_scales, up_scales, down_scales, gate, up, down)


def forward_kernel(
    ids, tokens, out_grad, m0, m1, t0, t1, after, own, p1, p2, p3, w_out, half, w_down, rows_in, sems
):
    step = pl.program_id(0)
    z, core, x = ids[0], ids[1], ids[2]

    def fetch(k, r):
        source = (tokens, out_grad)[k].at[pl.ds(pl.multiple_of((x ^ r) * RB, RB), RB), :]
        return pltpu.make_async_copy(source, rows_in.at[k, r], sems.at[k, r])

    @pl.when(step == 0)
    def _():
        for r in range(XS):
            for k in range(2):
                fetch(k, r).start()
        for i in range(Z):
            base = (z ^ far_first(i)) * (2 * T)
            for pair, side in (((m0, m1), core), ((t0, t1), 1 - core)):
                ref, j = pair[i // 4], i % 4
                rows = pl.ds(pl.multiple_of(base + side * T, T), T)
                w_out[rows, :] = ref[j * T : (j + 1) * T, 0 : 2 * T]
                w_down[rows, :] = ref[j * T : (j + 1) * T, 2 * T : 3 * T]

        half[0 : 4 * T, :] = m0[:, 0 : 2 * T]
        half[4 * T : 8 * T, :] = m1[:, 0 : 2 * T]

    fetch(0, step).wait()
    gate_up = jnp.dot(rows_in[0, step], w_out[...], preferred_element_type=F32)
    fetch(1, step).wait()
    back = jnp.dot(rows_in[1, step], w_down[...], preferred_element_type=F32)

    @pl.when(step == 0)
    def _():
        own[:, 0 : 2 * T] = gate_up
        own[:, 2 * T : 3 * T] = back

    for k, ref in ((1, p1), (2, p2), (3, p3)):

        @pl.when(step == k)
        def _():
            ref[:, 0 : 2 * T] = gate_up.astype(BF)
            ref[:, 2 * T : 3 * T] = back.astype(BF)


def forward(ids, tokens, out_grad, mine, theirs, after):
    whole = lambda *shape: pl.BlockSpec(shape, lambda r, ids: (0,) * len(shape))
    part = jax.ShapeDtypeStruct((RB, 3 * T), BF)
    return pl.pallas_call(
        forward_kernel,
        grid_spec=pltpu.PrefetchScalarGridSpec(
            num_scalar_prefetch=1,
            grid=(XS,),
            in_specs=[HBM, HBM] + [whole(4 * T, 3 * T)] * 4 + [ANY],
            out_specs=[whole(RB, 3 * T)] * 4 + [whole(D, 2 * T), whole(8 * T, 2 * T)],
            scratch_shapes=[
                pltpu.VMEM((D, T), BF),
                pltpu.VMEM((2, XS, RB, D), BF),
                pltpu.SemaphoreType.DMA((2, XS)),
            ],
        ),
        out_shape=[
            jax.ShapeDtypeStruct((RB, 3 * T), F32),
            part,
            part,
            part,
            jax.ShapeDtypeStruct((D, 2 * T), BF),
            jax.ShapeDtypeStruct((8 * T, 2 * T), BF),
        ],
        compiler_params=params(56),
        cost_estimate=work(2 * CAP * D * 3 * T, 10),
        name="forward",
    )(ids, tokens, out_grad, *mine, *theirs, after)


def reduce_kernel(own, g1, g2, g3, total):
    total[...] = (
        own[...] + g1[...].astype(F32) + g2[...].astype(F32) + g3[...].astype(F32)
    ).astype(BF)


def reduce_rows(own, got):
    return pl.pallas_call(
        reduce_kernel,
        out_shape=jax.ShapeDtypeStruct((RB, 3 * T), BF),
        in_specs=[VMEM] * 4,
        out_specs=VMEM,
        name="reduce_rows",
    )(own, *got)


def collect_kernel(*refs):
    n = len(refs) - 3
    out, sems = refs[-2], refs[-1]
    copies = [pltpu.make_async_copy(refs[i], out.at[i], sems.at[i]) for i in range(n)]
    for copy in copies:
        copy.start()
    for copy in copies:
        copy.wait()


def collect(arrays, after):
    n = len(arrays)
    return pl.pallas_call(
        collect_kernel,
        out_shape=jax.ShapeDtypeStruct((n,) + arrays[0].shape, arrays[0].dtype),
        in_specs=[ANY] * (n + 1),
        out_specs=ANY,
        scratch_shapes=[pltpu.SemaphoreType.DMA((n,))],
        name="collect",
    )(*arrays, after)


def delta_kernel(ids, s_mine, s_theirs, per_row, out):
    total = s_mine[...].astype(F32) + s_theirs[...].astype(F32)
    gate, up, back = total[:, 0:T], total[:, T : 2 * T], total[:, 2 * T : 3 * T]
    weight = per_row[pl.ds(pl.multiple_of(ids[2] * RB, RB), RB), :][:, 0:1]
    s = jax.nn.sigmoid(gate)
    act = gate * s
    hidden_full = act * up
    delta = back * weight
    out[0:RB, 0:T] = (delta * up * s * (1.0 + gate * (1.0 - s))).astype(BF)
    out[0:RB, T : 2 * T] = (delta * act).astype(BF)
    out[0:RB, 2 * T : 3 * T] = hidden_full.astype(BF)
    router = lax.dot_general(
        jnp.ones((8, T), F32),
        back * hidden_full,
        NT,
        precision=lax.Precision.HIGHEST,
        preferred_element_type=F32,
    )
    router = jnp.concatenate([router, jnp.zeros((8, 2 * T - RB), F32)], axis=1)
    hi, mid, low = (piece.astype(F32) for piece in split3(router))
    row = lax.broadcasted_iota(jnp.int32, (8, 2 * T), 0)
    pieces = jnp.where(row == 0, hi, jnp.where(row == 1, mid, jnp.where(row == 2, low, 0.0)))
    out[RB:MSG, 0 : 2 * T] = jnp.concatenate([pieces, jnp.zeros_like(pieces)], axis=0).astype(BF)
    out[RB:MSG, 2 * T : 3 * T] = jnp.zeros((16, T), BF)


def deltas(ids, s_mine, s_theirs, per_row):
    return pl.pallas_call(
        delta_kernel,
        out_shape=jax.ShapeDtypeStruct((MSG, 3 * T), BF),
        in_specs=[SMEM] + [VMEM] * 3,
        out_specs=VMEM,
        name="deltas",
    )(ids, s_mine, s_theirs, per_row)


def weight_grad_kernel(
    ids,
    tokens,
    out_grad,
    per_row,
    d0,
    d1,
    d2,
    d3,
    a,
    b,
    c,
    keep,
    send,
    flat,
    turned,
    columns_in,
    sems,
):
    step = pl.program_id(0)
    z, core, x = ids[0], ids[1], ids[2]

    def fetch(k, i):
        columns = pl.ds(pl.multiple_of((z ^ far_first(i ^ 4)) * (2 * T), 2 * T), 2 * T)
        source = (tokens, out_grad)[k].at[:, columns]
        return pltpu.make_async_copy(source, columns_in.at[k, i], sems.at[k, i])

    @pl.when(step == 0)
    def _():
        for i in range(Z):
            for k in range(2):
                fetch(k, i).start()
        for r, ref in enumerate((d0, d1, d2, d3)):
            rows = pl.ds(pl.multiple_of((x ^ r) * RB, RB), RB)
            flat[rows, :] = ref[0:RB, :]
        turned[...] = flat[...].astype(F32).T.astype(BF)

    fetch(0, step).wait()
    gate_up = jnp.dot(turned[0 : 2 * T, :], columns_in[0, step], preferred_element_type=F32)
    fetch(1, step).wait()
    scaled = (columns_in[1, step].astype(F32) * per_row[:, 0:1]).astype(BF)
    down = jnp.dot(turned[2 * T : 3 * T, :], scaled, preferred_element_type=F32)
    for rows, value in ((slice(0, 2 * T), gate_up), (slice(2 * T, 3 * T), down)):
        low, high = value[:, 0:T].astype(BF), value[:, T : 2 * T].astype(BF)
        keep[rows, :] = jnp.where(core == 0, low, high)
        send[rows, :] = jnp.where(core == 0, high, low)


def weight_grads(ids, tokens, out_grad, per_row, parts, after):
    whole = lambda *shape: pl.BlockSpec(shape, lambda i, ids: (0,) * len(shape))
    block = pl.BlockSpec((3 * T, T), lambda i, ids: (i, 0))
    return pl.pallas_call(
        weight_grad_kernel,
        grid_spec=pltpu.PrefetchScalarGridSpec(
            num_scalar_prefetch=1,
            grid=(Z,),
            in_specs=[HBM, HBM, whole(CAP, T)] + [whole(MSG, 3 * T)] * 4 + [ANY] * 3,
            out_specs=[block, block],
            scratch_shapes=[
                pltpu.VMEM((CAP, 3 * T), BF),
                pltpu.VMEM((3 * T, CAP), BF),
                pltpu.VMEM((2, Z, CAP, 2 * T), BF),
                pltpu.SemaphoreType.DMA((2, Z)),
            ],
        ),
        out_shape=[jax.ShapeDtypeStruct((Z * 3 * T, T), BF)] * 2,
        compiler_params=params(),
        cost_estimate=work(2 * CAP * D * 3 * T, 10),
        name="weight_grads",
    )(ids, tokens, out_grad, per_row, *parts, *after)


def core_sum_kernel(keep, received, send):
    rows = slice(0, 4 * 3 * T)
    send[...] = (keep[rows, :].astype(F32) + received[rows, :].astype(F32)).astype(BF)


def core_sum(keep, received):
    return pl.pallas_call(
        core_sum_kernel,
        out_shape=jax.ShapeDtypeStruct((4 * 3 * T, T), BF),
        in_specs=[VMEM] * 2,
        out_specs=VMEM,
        name="core_sum",
    )(keep, received)


def rows_kernel(ids, d0, d1, d2, d3, after, rows_out):
    x = ids[2]
    for r, ref in enumerate((d0, d1, d2, d3)):
        rows = pl.ds(pl.multiple_of((x ^ r) * RB, RB), RB)
        rows_out[rows, :] = ref[0:RB, 0 : 2 * T]
        rows_out[CAP + 16 * r : CAP + 16 * (r + 1), :] = ref[RB:MSG, 0 : 2 * T]


def row_order(ids, parts, after):
    return pl.pallas_call(
        rows_kernel,
        out_shape=jax.ShapeDtypeStruct((CAP + XS * 16, 2 * T), BF),
        in_specs=[SMEM] + [VMEM] * 4 + [ANY],
        out_specs=VMEM,
        name="row_order",
    )(ids, *parts, after)


def pair_sum_kernel(keep, received, arrived, y1, y3, own, s4, s2, s6):
    for i, out in enumerate((own, s4, s2, s6)):
        there = slice(i * 3 * T, (i + 1) * 3 * T)
        here = slice((i + 4) * 3 * T, (i + 5) * 3 * T)
        total = keep[here, :].astype(F32) + received[here, :].astype(F32)
        out[...] = (total + arrived[there, :].astype(F32)).astype(out.dtype)


def pair_sum(keep, received, arrived, after):
    part = jax.ShapeDtypeStruct((3 * T, T), BF)
    return pl.pallas_call(
        pair_sum_kernel,
        out_shape=[jax.ShapeDtypeStruct((3 * T, T), F32), part, part, part],
        in_specs=[VMEM] * 3 + [ANY] * 2,
        out_specs=[VMEM] * 4,
        name="pair_sum",
    )(keep, received, arrived, *after)


def last_sum_kernel(own, r4, r2, r6, after, gate, up, down):
    total = own[...] + r4[...].astype(F32) + r2[...].astype(F32) + r6[...].astype(F32)
    gate[...] = total[0:T].T
    up[...] = total[T : 2 * T].T
    down[...] = total[2 * T : 3 * T]


def last_sum(own, r4, r2, r6, after):
    return pl.pallas_call(
        last_sum_kernel,
        out_shape=[jax.ShapeDtypeStruct((T, T), F32)] * 3,
        in_specs=[VMEM] * 4 + [ANY],
        out_specs=[VMEM] * 3,
        name="last_sum",
    )(own, r4, r2, r6, after)


def token_grad_kernel(
    ids, w0, near, far, y0, y1, y2, y3, per_row, after, out, logits_out, w, router
):
    step = pl.program_id(0)
    core, x = ids[1], ids[2]

    @pl.when(step == 0)
    def _():
        for r in range(XS):
            rows = slice(CAP + 16 * r, CAP + 16 * (r + 1))
            terms = []
            for ref in (y0, y1, y2, y3):
                pieces = ref[rows, :].astype(F32)
                terms.append(pieces[0:1] + pieces[1:2] + pieces[2:3])
            total = (terms[0] + terms[1]) + (terms[2] + terms[3])
            router[pl.ds(pl.multiple_of((x ^ r) * RB, RB), RB), :] = turn(total)[0:RB]
        value = router[...] * per_row[:, 1:2]
        at = per_row[:, 2:3].astype(jnp.int32)
        lanes = lax.broadcasted_iota(jnp.int32, (CAP, T), 1)
        upper = jnp.where(lanes == (at >> 7), 1.0, 0.0).T.astype(BF)
        spread = jnp.where(lanes == (at & (T - 1)), value, 0.0)
        total = jnp.zeros((T, T), F32)
        for piece in split3(spread):
            total = total + jnp.dot(upper, piece, preferred_element_type=F32)
        logits_out[...] = total[0 : SEQ // T, :]

    mine = pl.ds(pl.multiple_of(core * T, T), T)
    theirs = pl.ds(pl.multiple_of((1 - core) * T, T), T)
    total = lax.dot_general(y0[0:CAP, :], w0[...], NT, preferred_element_type=F32)
    for j, ref in enumerate((y1, y2, y3)):
        w[j, mine, :] = near[j]
        w[j, theirs, :] = far[j]
        total = total + lax.dot_general(ref[0:CAP, :], w[j], NT, preferred_element_type=F32)
    out[...] = total.astype(BF)


def token_grads(ids, w_own, near, far, rows_by_y, per_row, after):
    whole = lambda *shape: pl.BlockSpec(shape, lambda i, ids: (0,) * len(shape))
    zb = lambda i, ids: ids[0] ^ far_first(i)
    tiles = pl.BlockSpec((3, T, 2 * T), lambda i, ids: (0, i, 0))
    return pl.pallas_call(
        token_grad_kernel,
        grid_spec=pltpu.PrefetchScalarGridSpec(
            num_scalar_prefetch=1,
            grid=(Z,),
            in_specs=[pl.BlockSpec((2 * T, 2 * T), lambda i, ids: (zb(i, ids), 0)), tiles, tiles]
            + [whole(CAP + XS * 16, 2 * T)] * 4
            + [whole(CAP, T), ANY],
            out_specs=[
                pl.BlockSpec((CAP, 2 * T), lambda i, ids: (0, zb(i, ids))),
                whole(SEQ // T, T),
            ],
            scratch_shapes=[pltpu.VMEM((3, 2 * T, 2 * T), BF), pltpu.VMEM((CAP, 1), F32)],
        ),
        out_shape=[
            jax.ShapeDtypeStruct((CAP, D), BF),
            jax.ShapeDtypeStruct((SEQ // T, T), F32),
        ],
        compiler_params=params(),
        cost_estimate=work(2 * CAP * D * 8 * T, 12),
        name="token_grads",
    )(ids, w_own, near, far, *rows_by_y, per_row, after)


def local(
    tokens,
    out_grad,
    router_logits,
    routed_counts,
    routed_positions,
    gate_values,
    up_values,
    down_values,
    gate_scales,
    up_scales,
    down_scales,
):
    z, core, x = lax.axis_index("z"), lax.axis_index("core"), lax.axis_index("x")
    ids = jnp.stack([z, core, x]).astype(jnp.int32)

    scales = (gate_scales.T, up_scales.T, down_scales)
    held = own_tiles(ids, *scales, gate_values, up_values, down_values)
    held = jnp.concatenate([held] + [swap(held, "z", Z, mask) for mask in (4, 2, 6)], axis=0)
    mine = (held, swap(held, "z", Z, 1))
    theirs = tuple(swap(h, "core", CORES, 1) for h in mine)
    per_row = rates(router_logits.reshape(SEQ // T, T), routed_positions[None, :], routed_counts)

    own, p1, p2, p3, w_own, half = forward(ids, tokens, out_grad, mine, theirs, per_row)
    got = [swap(p, "x", XS, r) for r, p in ((1, p1), (2, p2), (3, p3))]
    total = reduce_rows(own, got)
    message = deltas(ids, total, swap(total, "zhi", Z_HI, 1), per_row)
    parts = [message] + [swap(message, "x", XS, r) for r in (1, 2, 3)]

    half = collect([half], total)[0]
    by_y = [swap(half, "row", ROWS, r) for r in (1, 2, 3)]

    keep, send = weight_grads(ids, tokens, out_grad, per_row, parts, by_y)
    received = swap(send, "core", CORES, 1)
    arrived = swap(core_sum(keep, received), "z", Z, 1)

    rows = row_order(ids, parts, keep)
    y1, y2, y3 = (swap(rows, "row", ROWS, r) for r in (1, 2, 3))
    own_sum, s4, s2, s6 = pair_sum(keep, received, arrived, (y1, y3))
    near = collect(by_y, s4)
    far = swap(near, "core", CORES, 1)
    grad_tokens, grad_logits = token_grads(
        ids, w_own, near, far, (rows, y1, y2, y3), per_row, s4
    )
    grad_gate, grad_up, grad_down = last_sum(
        own_sum,
        swap(s4, "z", Z, 4),
        swap(s2, "z", Z, 2),
        swap(s6, "z", Z, 6),
        grad_logits,
    )
    return (grad_tokens, grad_gate, grad_up, grad_down, grad_logits.reshape(SEQ))


def solution(mesh):
    fine = Mesh(mesh.devices.reshape(Z, CORES, ROWS, Z_HI, XS), AXES)
    dp, col = ("z", "core"), ("zhi", "x")
    placed = (
        P(dp, col),
        P(dp, col),
        P(dp),
        P(dp),
        P(dp),
        P(col + dp, "row"),
        P(col + dp, "row"),
        P("row", col + dp),
        P(col, "row"),
        P(col, "row"),
        P("row", col),
    )
    return jax.shard_map(
        local,
        mesh=fine,
        in_specs=placed,
        out_specs=(P(dp, col), P(col + dp, "row"), P(col + dp, "row"), P("row", col + dp), P(dp)),
        check_vma=False,
    )
```

time: 233 us -> 275 us (1.18)
  Pallas kernels: 21.3 us -> 107 us
  waiting for transfers between devices: 50.5 us -> 34.8 us
  other arithmetic: 16.6 us -> 1.52 us
  local copies, waits for them, and re-layouts: 28.4 us -> 13.7 us
    pallas_call x0 -> x8, Pallas kernels: none -> 78.3 us  [the longest x2 65.8 us: collect(): pl.pallas_call(collect_kernel, out_shape=jax.ShapeDtypeStruct((n,) + arra...]
    ppermute x22 -> x25, waiting for transfers between devices: 50.5 us -> 34.8 us  [swap(): return lax.ppermute(value, axis, [(i, i ^ mask) for i in range(size)])]
    scatter-add x1 -> x0, other arithmetic: 6.44 us -> none  [local(): jnp.zeros(router_logits.shape, F32).at[routed_positions].add(logit_delta)]
    pallas_call x1, Pallas kernels: 3.91 us -> 9.52 us  [forward(): pl.pallas_call(forward_kernel, grid_spec=pltpu.PrefetchScalarGridSpec(num...]
    unnamed x42 -> x50, local copies, waits for them, and re-layouts: 17.9 us -> 12.4 us
    gather x2 -> x0, local copies, waits for them, and re-layouts: 5.03 us -> none  [the longest x1 4.46 us: local(): rate = jax.nn.sigmoid(jnp.take(router_logits, routed_positions))]
    add x5 -> x0, other arithmetic: 3.37 us -> none  [the longest x3 3.2 us: local(): sums = sums[:cut] + received.astype(F32)]
    pallas_call x1, Pallas kernels: 4.77 us -> 7.9 us  [weight_grads(): pl.pallas_call(weight_grad_kernel, grid_spec=pltpu.PrefetchScalarGridSpec...]
  transfers between devices with their start and end apart: 22 -> 25, of which waited for: 11 -> 10; matrix products, arithmetic and copies ran while one was open for 11% -> 0% of each run, Pallas kernels for 3% -> 6%
where the time goes in v2:
time: 275 us; the launch traced here: 274 us
  starting transfers between devices  114 us (41%)
  Pallas kernels  107 us (39%)
  waiting for transfers between devices  34.8 us (13%)
  local copies, waits for them, and re-layouts  13.7 us (5%)
    ppermute x25, starting transfers between devices, swap(): return lax.ppermute(value, axis, [(i, i ^ mask) for i in range(size)])  114 us
    pallas_call x2, Pallas kernels, collect(): pl.pallas_call(collect_kernel, out_shape=jax.ShapeDtypeStruct((n,) + arra...  65.8 us
    ppermute x25, waiting for transfers between devices, swap(): return lax.ppermute(value, axis, [(i, i ^ mask) for i in range(size)])  34.8 us
    unnamed x50, local copies, waits for them, and re-layouts  12.4 us
    pallas_call x1, Pallas kernels, forward(): pl.pallas_call(forward_kernel, grid_spec=pltpu.PrefetchScalarGridSpec(num...  9.52 us
    pallas_call x1, Pallas kernels, token_grads(): pl.pallas_call(token_grad_kernel, grid_spec=pltpu.PrefetchScalarGridSpec(...  7.91 us
    pallas_call x1, Pallas kernels, weight_grads(): pl.pallas_call(weight_grad_kernel, grid_spec=pltpu.PrefetchScalarGridSpec...  7.9 us
  transfers between devices with their start and end apart: 25, of which 10 were waited for; matrix products, arithmetic and copies ran while one was open for 0% of the time, Pallas kernels for 6%

profile of v2, /device:TPU:1, one launch (start us, length us, event | category | flops | bytes accessed | tf_op | source)
XLA Modules:
  0.0 273.6 jit_solution(9199509592658313333)
XLA Ops:
  1.2 1.7 own_tiles.1
  2.9 9.6 %collective-permute-start = (bf16[128,384]{1,0:T(8,128)(2,1)}, bf16[128,384]{1,0:T(8,128)(2,1)S(1)}, u32[]{:S(2)}, u32[]{:S(2)}) collective-permute-start(bf16[128,384]{1,0:T(8,128)(2,1)} %own_tiles.1), channel_id=1, source_target_pairs={{0,256},{64,320},{128,384},{192,448},{256,0},{320,64},{384,128},{4... | collective-permute-start | bytes 294920 | tf_op jit(solution)/shard_map/ppermute | solution.py:22
  12.5 4.9 %collective-permute-start.1 = (bf16[128,384]{1,0:T(8,128)(2,1)}, bf16[128,384]{1,0:T(8,128)(2,1)S(1)}, u32[]{:S(2)}, u32[]{:S(2)}) collective-permute-start(bf16[128,384]{1,0:T(8,128)(2,1)} %own_tiles.1), channel_id=1, source_target_pairs={{0,128},{64,192},{128,0},{192,64},{256,384},{320,448},{384,256},{4... | collective-permute-start | bytes 294920 | tf_op jit(solution)/shard_map/ppermute | solution.py:22
  17.4 1.9 collective-permute-start.2
  20.0 8.7 %collective-permute-done.2 = bf16[128,384]{1,0:T(8,128)(2,1)S(1)} collective-permute-done((bf16[128,384]{1,0:T(8,128)(2,1)}, bf16[128,384]{1,0:T(8,128)(2,1)S(1)}, u32[]{:S(2)}, u32[]{:S(2)}) %collective-permute-start.2) | collective-permute-done | bytes 98336 | tf_op jit(solution)/shard_map/ppermute | solution.py:22
  29.7 3.6 %collective-permute-start.3 = (bf16[512,384]{1,0:T(8,128)(2,1)S(1)}, bf16[512,384]{1,0:T(8,128)(2,1)S(1)}, u32[]{:S(2)}, u32[]{:S(2)}) collective-permute-start(bf16[512,384]{1,0:T(8,128)(2,1)S(1)} %pad_maximum_fusion.m0), channel_id=1, source_target_pairs={{0,64},{64,0},{128,192},{192,128},{256,320},{320,256},{384,448},{4... | collective-permute-start | bytes 1179656 | tf_op jit(solution)/shard_map/ppermute | solution.py:22
  33.3 4.6 %collective-permute-start.4 = (bf16[512,384]{1,0:T(8,128)(2,1)S(1)}, bf16[512,384]{1,0:T(8,128)(2,1)S(1)}, u32[]{:S(2)}, u32[]{:S(2)}) collective-permute-start(bf16[512,384]{1,0:T(8,128)(2,1)S(1)} %pad_maximum_fusion.m0), channel_id=1, source_target_pairs={{0,32},{32,0},{1,33},{33,1},{2,34},{34,2},{3,35},{35,3},{4,36},{36... | collective-permute-start | bytes 1179656 | tf_op jit(solution)/shard_map/ppermute | solution.py:22
  37.9 1.4 collective-permute-done.3.m1
  39.3 6.1 %collective-permute-start.5 = (bf16[512,384]{1,0:T(8,128)(2,1)S(1)}, bf16[512,384]{1,0:T(8,128)(2,1)}, u32[]{:S(2)}, u32[]{:S(2)}) collective-permute-start(bf16[512,384]{1,0:T(8,128)(2,1)S(1)} %collective-permute-done.3.m1), channel_id=1, source_target_pairs={{0,32},{32,0},{1,33},{33,1},{2,34},{34,2},{3,35},{35,3},{4,36},{36... | collective-permute-start | bytes 1179656 | tf_op jit(solution)/shard_map/ppermute | solution.py:22
  47.3 2.3 rates.1.after.per_row
  50.4 9.5 %forward.1 = (f32[192,384]{1,0:T(8,128)}, bf16[192,384]{1,0:T(8,128)(2,1)}, bf16[192,384]{1,0:T(8,128)(2,1)}, bf16[192,384]{1,0:T(8,128)(2,1)}, bf16[2048,256]{1,0:T(8,128)(2,1)}, /*index=5*/bf16[1024,256]{1,0:T(8,128)(2,1)}) custom-call(s32[3]{0:T(128)} %pad_add_fusion.ids, bf16[768,2048]{1,0:T(8,128)(2,1)} %tokens.3, bf16[768,2048]{1,0:T(8,128)(2,1)} %out_grad.3, ...), custom_call_target="tpu_custom_call" | custom-call | flops 1207959552 | bytes 10485760 | tf_op jit(solution)/shard_map/forward/pallas_call | solution.py:151
  59.9 3.2 %collective-permute-start.6 = (bf16[192,384]{1,0:T(8,128)(2,1)}, bf16[192,384]{1,0:T(8,128)(2,1)}, u32[]{:S(2)}, u32[]{:S(2)}) collective-permute-start(bf16[192,384]{1,0:T(8,128)(2,1)} %get-tuple-element.25), channel_id=1, source_target_pairs={{0,1},{1,0},{2,3},{3,2},{4,5},{5,4},{6,7},{7,6},{8,9},{9,8},{10,11... | collective-permute-start | bytes 442376 | tf_op jit(solution)/shard_map/ppermute | solution.py:22
  63.2 4.4 %collective-permute-start.7 = (bf16[192,384]{1,0:T(8,128)(2,1)}, bf16[192,384]{1,0:T(8,128)(2,1)}, u32[]{:S(2)}, u32[]{:S(2)}) collective-permute-start(bf16[192,384]{1,0:T(8,128)(2,1)} %get-tuple-element.26), channel_id=1, source_target_pairs={{0,2},{1,3},{2,0},{3,1},{4,6},{5,7},{6,4},{7,5},{8,10},{9,11},{10,... | collective-permute-start | bytes 442376 | tf_op jit(solution)/shard_map/ppermute | solution.py:22
  67.5 2.1 collective-permute-start.8
  69.7 3.4 %collective-permute-done.7.g2 = bf16[192,384]{1,0:T(8,128)(2,1)} collective-permute-done((bf16[192,384]{1,0:T(8,128)(2,1)}, bf16[192,384]{1,0:T(8,128)(2,1)}, u32[]{:S(2)}, u32[]{:S(2)}) %collective-permute-start.7) | collective-permute-done | bytes 147488 | tf_op jit(solution)/shard_map/ppermute | solution.py:22
  73.1 2.7 collective-permute-done.8.g3
  75.8 1.9 reduce_rows.1.refs_1_.s_mine
  77.7 17.0 %collect.2 = bf16[1,1024,256]{2,1,0:T(8,128)(2,1)} custom-call(bf16[1024,256]{1,0:T(8,128)(2,1)} %get-tuple-element.23.refs_0_, bf16[192,384]{1,0:T(8,128)(2,1)} %reduce_rows.1.refs_1_.s_mine), custom_call_target="tpu_custom_call" | custom-call | tf_op jit(solution)/shard_map/collect/pallas_call | solution.py:206
  94.6 4.8 %collective-permute-start.10 = (bf16[1024,256]{1,0:T(8,128)(2,1)}, bf16[1024,256]{1,0:T(8,128)(2,1)}, u32[]{:S(2)}, u32[]{:S(2)}) collective-permute-start(bf16[1024,256]{1,0:T(8,128)(2,1)} %bitcast.8), channel_id=1, source_target_pairs={{0,16},{8,24},{16,0},{24,8},{1,17},{9,25},{17,1},{25,9},{2,18},{10... | collective-permute-start | bytes 1572872 | tf_op jit(solution)/shard_map/ppermute | solution.py:22
  99.5 2.7 collective-permute-start.11
  102.2 1.9 collective-permute-start.9
  104.1 12.0 %collective-permute-start.12 = (bf16[192,384]{1,0:T(8,128)(2,1)}, bf16[192,384]{1,0:T(8,128)(2,1)}, u32[]{:S(2)}, u32[]{:S(2)}) collective-permute-start(bf16[192,384]{1,0:T(8,128)(2,1)} %reduce_rows.1.refs_1_.s_mine), channel_id=1, source_target_pairs={{0,4},{4,0},{1,5},{5,1},{2,6},{6,2},{3,7},{7,3},{8,12},{12,8},{9,1... | collective-permute-start | bytes 442376 | tf_op jit(solution)/shard_map/ppermute | solution.py:22
  116.1 3.1 %collective-permute-done.12.s_theirs = bf16[192,384]{1,0:T(8,128)(2,1)} collective-permute-done((bf16[192,384]{1,0:T(8,128)(2,1)}, bf16[192,384]{1,0:T(8,128)(2,1)}, u32[]{:S(2)}, u32[]{:S(2)}) %collective-permute-start.12) | collective-permute-done | bytes 147488 | tf_op jit(solution)/shard_map/ppermute | solution.py:22
  119.2 2.1 deltas.1.d0
  121.3 2.6 collective-permute-start.13
  123.9 4.0 %collective-permute-start.14 = (bf16[208,384]{1,0:T(8,128)(2,1)}, bf16[208,384]{1,0:T(8,128)(2,1)S(1)}, u32[]{:S(2)}, u32[]{:S(2)}) collective-permute-start(bf16[208,384]{1,0:T(8,128)(2,1)} %deltas.1.d0), channel_id=1, source_target_pairs={{0,2},{1,3},{2,0},{3,1},{4,6},{5,7},{6,4},{7,5},{8,10},{9,11},{10,... | collective-permute-start | bytes 479240 | tf_op jit(solution)/shard_map/ppermute | solution.py:22
  127.9 3.1 %collective-permute-start.15 = (bf16[208,384]{1,0:T(8,128)(2,1)}, bf16[208,384]{1,0:T(8,128)(2,1)S(1)}, u32[]{:S(2)}, u32[]{:S(2)}) collective-permute-start(bf16[208,384]{1,0:T(8,128)(2,1)} %deltas.1.d0), channel_id=1, source_target_pairs={{0,3},{1,2},{2,1},{3,0},{4,7},{5,6},{6,5},{7,4},{8,11},{9,10},{10,... | collective-permute-start | bytes 479240 | tf_op jit(solution)/shard_map/ppermute | solution.py:22
  131.0 2.1 collective-permute-done.14.d2
  133.2 3.6 %collective-permute-done.15.d3 = bf16[208,384]{1,0:T(8,128)(2,1)S(1)} collective-permute-done((bf16[208,384]{1,0:T(8,128)(2,1)}, bf16[208,384]{1,0:T(8,128)(2,1)S(1)}, u32[]{:S(2)}, u32[]{:S(2)}) %collective-permute-start.15) | collective-permute-done | bytes 159776 | tf_op jit(solution)/shard_map/ppermute | solution.py:22
  136.8 1.9 copy-done.1
  139.6 7.9 %weight_grads.1 = (bf16[3072,128]{1,0:T(8,128)(2,1)S(1)}, bf16[3072,128]{1,0:T(8,128)(2,1)}) custom-call(s32[3]{0:T(128)S(1)} %copy-done.15, bf16[768,2048]{1,0:T(8,128)(2,1)S(1)} %copy-done, bf16[768,2048]{1,0:T(8,128)(2,1)S(1)} %copy-done.1, f32[768,128]{1,0:T(8,128)S(1)} %copy-done.3, bf16[208,384]{1,0:T(8,128)(2,1)S(1)} %copy-done.5, ...), custom_call_target="tpu_custom_call" | custom-call | flops 1207959552 | bytes 10485760 | tf_op jit(solution)/shard_map/weight_grads/pallas_call | solution.py:303
  148.5 7.4 %collective-permute-start.16 = (bf16[3072,128]{1,0:T(8,128)(2,1)}, bf16[3072,128]{1,0:T(8,128)(2,1)S(1)}, u32[]{:S(2)}, u32[]{:S(2)}) collective-permute-start(bf16[3072,128]{1,0:T(8,128)(2,1)} %get-tuple-element.29), channel_id=1, source_target_pairs={{0,32},{32,0},{1,33},{33,1},{2,34},{34,2},{3,35},{35,3},{4,36},{36... | collective-permute-start | bytes 2359304 | tf_op jit(solution)/shard_map/ppermute | solution.py:22
  155.8 1.9 row_order.1.y0
  157.8 3.4 %collective-permute-start.18 = (bf16[832,256]{1,0:T(8,128)(2,1)}, bf16[832,256]{1,0:T(8,128)(2,1)S(1)}, u32[]{:S(2)}, u32[]{:S(2)}) collective-permute-start(bf16[832,256]{1,0:T(8,128)(2,1)} %row_order.1.y0), channel_id=1, source_target_pairs={{0,8},{8,0},{16,24},{24,16},{1,9},{9,1},{17,25},{25,17},{2,10},{10... | collective-permute-start | bytes 1277960 | tf_op jit(solution)/shard_map/ppermute | solution.py:22
  161.2 3.8 %collective-permute-start.19 = (bf16[832,256]{1,0:T(8,128)(2,1)}, bf16[832,256]{1,0:T(8,128)(2,1)S(1)}, u32[]{:S(2)}, u32[]{:S(2)}) collective-permute-start(bf16[832,256]{1,0:T(8,128)(2,1)} %row_order.1.y0), channel_id=1, source_target_pairs={{0,24},{8,16},{16,8},{24,0},{1,25},{9,17},{17,9},{25,1},{2,26},{10... | collective-permute-start | bytes 1277960 | tf_op jit(solution)/shard_map/ppermute | solution.py:22
  165.9 2.2 core_sum.1
  168.1 7.3 %collective-permute-start.17 = (bf16[1536,128]{1,0:T(8,128)(2,1)}, bf16[1536,128]{1,0:T(8,128)(2,1)S(1)}, u32[]{:S(2)}, u32[]{:S(2)}) collective-permute-start(bf16[1536,128]{1,0:T(8,128)(2,1)} %core_sum.1), channel_id=1, source_target_pairs={{0,64},{64,0},{128,192},{192,128},{256,320},{320,256},{384,448},{4... | collective-permute-start | bytes 1179656 | tf_op jit(solution)/shard_map/ppermute | solution.py:22
  175.6 9.0 %collective-permute-done.17.arrived = bf16[1536,128]{1,0:T(8,128)(2,1)S(1)} collective-permute-done((bf16[1536,128]{1,0:T(8,128)(2,1)}, bf16[1536,128]{1,0:T(8,128)(2,1)S(1)}, u32[]{:S(2)}, u32[]{:S(2)}) %collective-permute-start.17) | collective-permute-done | bytes 393248 | tf_op jit(solution)/shard_map/ppermute | solution.py:22
  185.4 2.3 pair_sum.1
  187.7 48.8 %collect.3.near = bf16[3,1024,256]{2,1,0:T(8,128)(2,1)} custom-call(bf16[1024,256]{1,0:T(8,128)(2,1)} %collective-permute-done.9.a.refs_0_, bf16[1024,256]{1,0:T(8,128)(2,1)} %collective-permute-done.10.b.refs_1_, bf16[1024,256]{1,0:T(8,128)(2,1)} %collective-permute-done.11.c.refs_2_, bf16[384,128]{1,0:T(8,128)(2,1)} %get-tuple-element.30.refs_3_.after), custom_call_target="tpu_custom_call" | custom-call | tf_op jit(solution)/shard_map/collect/pallas_call | solution.py:206
  236.5 3.0 %collective-permute-start.20 = (bf16[3,1024,256]{2,1,0:T(8,128)(2,1)}, bf16[3,1024,256]{2,1,0:T(8,128)(2,1)S(1)}, u32[]{:S(2)}, u32[]{:S(2)}) collective-permute-start(bf16[3,1024,256]{2,1,0:T(8,128)(2,1)} %collect.3.near), channel_id=1, source_target_pairs={{0,32},{32,0},{1,33},{33,1},{2,34},{34,2},{3,35},{35,3},{4,36},{36... | collective-permute-start | bytes 4718600 | tf_op jit(solution)/shard_map/ppermute | solution.py:22
  239.5 1.9 collective-permute-start.21
  241.5 10.1 %collective-permute-start.22 = (bf16[384,128]{1,0:T(8,128)(2,1)}, bf16[384,128]{1,0:T(8,128)(2,1)S(1)}, u32[]{:S(2)}, u32[]{:S(2)}) collective-permute-start(bf16[384,128]{1,0:T(8,128)(2,1)} %get-tuple-element.30.refs_3_.after), channel_id=1, source_target_pairs={{0,256},{64,320},{128,384},{192,448},{256,0},{320,64},{384,128},{4... | collective-permute-start | bytes 294920 | tf_op jit(solution)/shard_map/ppermute | solution.py:22
  251.5 1.9 collective-permute-start.23
  253.5 4.0 %collective-permute-start.24 = (bf16[384,128]{1,0:T(8,128)(2,1)}, bf16[384,128]{1,0:T(8,128)(2,1)}, u32[]{:S(2)}, u32[]{:S(2)}) collective-permute-start(bf16[384,128]{1,0:T(8,128)(2,1)} %get-tuple-element.34), channel_id=1, source_target_pairs={{0,384},{64,448},{128,256},{192,320},{256,128},{320,192},{384,0},{... | collective-permute-start | bytes 294920 | tf_op jit(solution)/shard_map/ppermute | solution.py:22
  257.5 1.4 copy-done.4
  263.1 7.9 %token_grads.1 = (bf16[768,2048]{1,0:T(8,128)(2,1)}, f32[48,128]{1,0:T(8,128)}) custom-call(s32[3]{0:T(128)S(1)} %copy-done.16, bf16[2048,256]{1,0:T(8,128)(2,1)S(1)} %copy-done.17, bf16[3,1024,256]{2,1,0:T(8,128)(2,1)S(1)} %copy-done.4, bf16[3,1024,256]{2,1,0:T(8,128)(2,1)S(1)} %collective-permute-done.20.far, bf16[832,256]{1,0:T(8,128)(2,1)S(1)} %copy-done.10, ...), custom_call_target="tpu_custom_call" | custom-call | flops 3221225472 | bytes 12582912 | tf_op jit(solution)/shard_map/token_grads/pallas_call | solution.py:433
  271.8 1.9 last_sum.1
  (68 shorter events, 12.7 us)
Async XLA Ops:
  2.9 16.5 %collective-permute-start = (bf16[128,384]{1,0:T(8,128)(2,1)}, bf16[128,384]{1,0:T(8,128)(2,1)S(1)}, u32[]{:S(2)}, u32[]{:S(2)}) collective-permute-start(bf16[128,384]{1,0:T(8,128)(2,1)} %own_tiles.1), channel_id=1, source_target_pairs={{0,256},{64,320},{128,384},{192,448},{256,0},{320,64},{384,128},{4... | collective-permute-start | bytes 294920 | tf_op jit(solution)/shard_map/ppermute | solution.py:22
  12.5 7.5 %collective-permute-start.1 = (bf16[128,384]{1,0:T(8,128)(2,1)}, bf16[128,384]{1,0:T(8,128)(2,1)S(1)}, u32[]{:S(2)}, u32[]{:S(2)}) collective-permute-start(bf16[128,384]{1,0:T(8,128)(2,1)} %own_tiles.1), channel_id=1, source_target_pairs={{0,128},{64,192},{128,0},{192,64},{256,384},{320,448},{384,256},{4... | collective-permute-start | bytes 294920 | tf_op jit(solution)/shard_map/ppermute | solution.py:22
  17.4 11.3 %collective-permute-start.2 = (bf16[128,384]{1,0:T(8,128)(2,1)}, bf16[128,384]{1,0:T(8,128)(2,1)S(1)}, u32[]{:S(2)}, u32[]{:S(2)}) collective-permute-start(bf16[128,384]{1,0:T(8,128)(2,1)} %own_tiles.1), channel_id=1, source_target_pairs={{0,384},{64,448},{128,256},{192,320},{256,128},{320,192},{384,0},{... | collective-permute-start | bytes 294920 | tf_op jit(solution)/shard_map/ppermute | solution.py:22
  29.7 20.7 %copy-start.19 = (bf16[512,384]{1,0:T(8,128)(2,1)}, bf16[512,384]{1,0:T(8,128)(2,1)S(1)}, u32[]{:S(2)}) copy-start(bf16[512,384]{1,0:T(8,128)(2,1)S(1)} %pad_maximum_fusion.m0) | copy-start | bytes 1179652
  29.7 9.6 %collective-permute-start.3 = (bf16[512,384]{1,0:T(8,128)(2,1)S(1)}, bf16[512,384]{1,0:T(8,128)(2,1)S(1)}, u32[]{:S(2)}, u32[]{:S(2)}) collective-permute-start(bf16[512,384]{1,0:T(8,128)(2,1)S(1)} %pad_maximum_fusion.m0), channel_id=1, source_target_pairs={{0,64},{64,0},{128,192},{192,128},{256,320},{320,256},{384,448},{4... | collective-permute-start | bytes 1179656 | tf_op jit(solution)/shard_map/ppermute | solution.py:22
  33.3 16.3 %collective-permute-start.4 = (bf16[512,384]{1,0:T(8,128)(2,1)S(1)}, bf16[512,384]{1,0:T(8,128)(2,1)S(1)}, u32[]{:S(2)}, u32[]{:S(2)}) collective-permute-start(bf16[512,384]{1,0:T(8,128)(2,1)S(1)} %pad_maximum_fusion.m0), channel_id=1, source_target_pairs={{0,32},{32,0},{1,33},{33,1},{2,34},{34,2},{3,35},{35,3},{4,36},{36... | collective-permute-start | bytes 1179656 | tf_op jit(solution)/shard_map/ppermute | solution.py:22
  39.3 10.3 %copy-start.20 = (bf16[512,384]{1,0:T(8,128)(2,1)}, bf16[512,384]{1,0:T(8,128)(2,1)S(1)}, u32[]{:S(2)}) copy-start(bf16[512,384]{1,0:T(8,128)(2,1)S(1)} %collective-permute-done.3.m1) | copy-start | bytes 1179652
  39.3 11.1 %collective-permute-start.5 = (bf16[512,384]{1,0:T(8,128)(2,1)S(1)}, bf16[512,384]{1,0:T(8,128)(2,1)}, u32[]{:S(2)}, u32[]{:S(2)}) collective-permute-start(bf16[512,384]{1,0:T(8,128)(2,1)S(1)} %collective-permute-done.3.m1), channel_id=1, source_target_pairs={{0,32},{32,0},{1,33},{33,1},{2,34},{34,2},{3,35},{35,3},{4,36},{36... | collective-permute-start | bytes 1179656 | tf_op jit(solution)/shard_map/ppermute | solution.py:22
  49.6 87.2 %copy-start.15 = (s32[3]{0:T(128)S(1)}, s32[3]{0:T(128)}, u32[]{:S(2)}) copy-start(s32[3]{0:T(128)} %pad_add_fusion.ids) | copy-start | bytes 40
  49.6 0.7 copy-start.21
  50.4 86.4 %copy-start = (bf16[768,2048]{1,0:T(8,128)(2,1)S(1)}, bf16[768,2048]{1,0:T(8,128)(2,1)}, u32[]{:S(2)}) copy-start(bf16[768,2048]{1,0:T(8,128)(2,1)} %tokens.3) | copy-start | bytes 9437188
  59.9 76.9 %copy-start.3 = (f32[768,128]{1,0:T(8,128)S(1)}, f32[768,128]{1,0:T(8,128)}, u32[]{:S(2)}) copy-start(f32[768,128]{1,0:T(8,128)} %rates.1.after.per_row) | copy-start | bytes 1179652
  59.9 9.7 %collective-permute-start.6 = (bf16[192,384]{1,0:T(8,128)(2,1)}, bf16[192,384]{1,0:T(8,128)(2,1)}, u32[]{:S(2)}, u32[]{:S(2)}) collective-permute-start(bf16[192,384]{1,0:T(8,128)(2,1)} %get-tuple-element.25), channel_id=1, source_target_pairs={{0,1},{1,0},{2,3},{3,2},{4,5},{5,4},{6,7},{7,6},{8,9},{9,8},{10,11... | collective-permute-start | bytes 442376 | tf_op jit(solution)/shard_map/ppermute | solution.py:22
  63.2 9.9 %collective-permute-start.7 = (bf16[192,384]{1,0:T(8,128)(2,1)}, bf16[192,384]{1,0:T(8,128)(2,1)}, u32[]{:S(2)}, u32[]{:S(2)}) collective-permute-start(bf16[192,384]{1,0:T(8,128)(2,1)} %get-tuple-element.26), channel_id=1, source_target_pairs={{0,2},{1,3},{2,0},{3,1},{4,6},{5,7},{6,4},{7,5},{8,10},{9,11},{10,... | collective-permute-start | bytes 442376 | tf_op jit(solution)/shard_map/ppermute | solution.py:22
  67.5 8.2 %collective-permute-start.8 = (bf16[192,384]{1,0:T(8,128)(2,1)}, bf16[192,384]{1,0:T(8,128)(2,1)}, u32[]{:S(2)}, u32[]{:S(2)}) collective-permute-start(bf16[192,384]{1,0:T(8,128)(2,1)} %get-tuple-element.27), channel_id=1, source_target_pairs={{0,3},{1,2},{2,1},{3,0},{4,7},{5,6},{6,5},{7,4},{8,11},{9,10},{10,... | collective-permute-start | bytes 442376 | tf_op jit(solution)/shard_map/ppermute | solution.py:22
  94.6 42.1 %collective-permute-start.10 = (bf16[1024,256]{1,0:T(8,128)(2,1)}, bf16[1024,256]{1,0:T(8,128)(2,1)}, u32[]{:S(2)}, u32[]{:S(2)}) collective-permute-start(bf16[1024,256]{1,0:T(8,128)(2,1)} %bitcast.8), channel_id=1, source_target_pairs={{0,16},{8,24},{16,0},{24,8},{1,17},{9,25},{17,1},{25,9},{2,18},{10... | collective-permute-start | bytes 1572872 | tf_op jit(solution)/shard_map/ppermute | solution.py:22
  99.5 37.3 %collective-permute-start.11 = (bf16[1024,256]{1,0:T(8,128)(2,1)}, bf16[1024,256]{1,0:T(8,128)(2,1)}, u32[]{:S(2)}, u32[]{:S(2)}) collective-permute-start(bf16[1024,256]{1,0:T(8,128)(2,1)} %bitcast.9), channel_id=1, source_target_pairs={{0,24},{8,16},{16,8},{24,0},{1,25},{9,17},{17,9},{25,1},{2,26},{10... | collective-permute-start | bytes 1572872 | tf_op jit(solution)/shard_map/ppermute | solution.py:22
  102.2 34.6 %collective-permute-start.9 = (bf16[1024,256]{1,0:T(8,128)(2,1)}, bf16[1024,256]{1,0:T(8,128)(2,1)}, u32[]{:S(2)}, u32[]{:S(2)}) collective-permute-start(bf16[1024,256]{1,0:T(8,128)(2,1)} %bitcast.10), channel_id=1, source_target_pairs={{0,8},{8,0},{16,24},{24,16},{1,9},{9,1},{17,25},{25,17},{2,10},{10... | collective-permute-start | bytes 1572872 | tf_op jit(solution)/shard_map/ppermute | solution.py:22
  104.1 15.1 %collective-permute-start.12 = (bf16[192,384]{1,0:T(8,128)(2,1)}, bf16[192,384]{1,0:T(8,128)(2,1)}, u32[]{:S(2)}, u32[]{:S(2)}) collective-permute-start(bf16[192,384]{1,0:T(8,128)(2,1)} %reduce_rows.1.refs_1_.s_mine), channel_id=1, source_target_pairs={{0,4},{4,0},{1,5},{5,1},{2,6},{6,2},{3,7},{7,3},{8,12},{12,8},{9,1... | collective-permute-start | bytes 442376 | tf_op jit(solution)/shard_map/ppermute | solution.py:22
  121.3 6.6 %collective-permute-start.13 = (bf16[208,384]{1,0:T(8,128)(2,1)}, bf16[208,384]{1,0:T(8,128)(2,1)S(1)}, u32[]{:S(2)}, u32[]{:S(2)}) collective-permute-start(bf16[208,384]{1,0:T(8,128)(2,1)} %deltas.1.d0), channel_id=1, source_target_pairs={{0,1},{1,0},{2,3},{3,2},{4,5},{5,4},{6,7},{7,6},{8,9},{9,8},{10,11... | collective-permute-start | bytes 479240 | tf_op jit(solution)/shard_map/ppermute | solution.py:22
  123.9 9.3 %collective-permute-start.14 = (bf16[208,384]{1,0:T(8,128)(2,1)}, bf16[208,384]{1,0:T(8,128)(2,1)S(1)}, u32[]{:S(2)}, u32[]{:S(2)}) collective-permute-start(bf16[208,384]{1,0:T(8,128)(2,1)} %deltas.1.d0), channel_id=1, source_target_pairs={{0,2},{1,3},{2,0},{3,1},{4,6},{5,7},{6,4},{7,5},{8,10},{9,11},{10,... | collective-permute-start | bytes 479240 | tf_op jit(solution)/shard_map/ppermute | solution.py:22
  127.9 19.6 %copy-start.6 = (bf16[208,384]{1,0:T(8,128)(2,1)}, bf16[208,384]{1,0:T(8,128)(2,1)S(1)}, u32[]{:S(2)}) copy-start(bf16[208,384]{1,0:T(8,128)(2,1)S(1)} %collective-permute-done.13.d1) | copy-start | bytes 479236
  127.9 8.8 %collective-permute-start.15 = (bf16[208,384]{1,0:T(8,128)(2,1)}, bf16[208,384]{1,0:T(8,128)(2,1)S(1)}, u32[]{:S(2)}, u32[]{:S(2)}) collective-permute-start(bf16[208,384]{1,0:T(8,128)(2,1)} %deltas.1.d0), channel_id=1, source_target_pairs={{0,3},{1,2},{2,1},{3,0},{4,7},{5,6},{6,5},{7,4},{8,11},{9,10},{10,... | collective-permute-start | bytes 479240 | tf_op jit(solution)/shard_map/ppermute | solution.py:22
  133.2 14.4 %copy-start.7 = (bf16[208,384]{1,0:T(8,128)(2,1)}, bf16[208,384]{1,0:T(8,128)(2,1)S(1)}, u32[]{:S(2)}) copy-start(bf16[208,384]{1,0:T(8,128)(2,1)S(1)} %collective-permute-done.14.d2) | copy-start | bytes 479236
  136.8 10.8 %copy-start.8 = (bf16[208,384]{1,0:T(8,128)(2,1)}, bf16[208,384]{1,0:T(8,128)(2,1)S(1)}, u32[]{:S(2)}) copy-start(bf16[208,384]{1,0:T(8,128)(2,1)S(1)} %collective-permute-done.15.d3) | copy-start | bytes 479236
  136.8 1.9 copy-start.1
  138.7 0.9 copy-start.5
  147.6 0.9 copy-start.2
  148.5 16.6 %collective-permute-start.16 = (bf16[3072,128]{1,0:T(8,128)(2,1)}, bf16[3072,128]{1,0:T(8,128)(2,1)S(1)}, u32[]{:S(2)}, u32[]{:S(2)}) collective-permute-start(bf16[3072,128]{1,0:T(8,128)(2,1)} %get-tuple-element.29), channel_id=1, source_target_pairs={{0,32},{32,0},{1,33},{33,1},{2,34},{34,2},{3,35},{35,3},{4,36},{36... | collective-permute-start | bytes 2359304 | tf_op jit(solution)/shard_map/ppermute | solution.py:22
  157.8 17.7 %collective-permute-start.18 = (bf16[832,256]{1,0:T(8,128)(2,1)}, bf16[832,256]{1,0:T(8,128)(2,1)S(1)}, u32[]{:S(2)}, u32[]{:S(2)}) collective-permute-start(bf16[832,256]{1,0:T(8,128)(2,1)} %row_order.1.y0), channel_id=1, source_target_pairs={{0,8},{8,0},{16,24},{24,16},{1,9},{9,1},{17,25},{25,17},{2,10},{10... | collective-permute-start | bytes 1277960 | tf_op jit(solution)/shard_map/ppermute | solution.py:22
  161.2 14.4 %collective-permute-start.19 = (bf16[832,256]{1,0:T(8,128)(2,1)}, bf16[832,256]{1,0:T(8,128)(2,1)S(1)}, u32[]{:S(2)}, u32[]{:S(2)}) collective-permute-start(bf16[832,256]{1,0:T(8,128)(2,1)} %row_order.1.y0), channel_id=1, source_target_pairs={{0,24},{8,16},{16,8},{24,0},{1,25},{9,17},{17,9},{25,1},{2,26},{10... | collective-permute-start | bytes 1277960 | tf_op jit(solution)/shard_map/ppermute | solution.py:22
  165.0 0.9 copy-start.18
  168.1 71.4 %copy-start.9 = (bf16[832,256]{1,0:T(8,128)(2,1)S(1)}, bf16[832,256]{1,0:T(8,128)(2,1)}, u32[]{:S(2)}) copy-start(bf16[832,256]{1,0:T(8,128)(2,1)} %row_order.1.y0) | copy-start | bytes 1277956
  168.1 89.3 %copy-start.16 = (s32[3]{0:T(128)S(1)}, s32[3]{0:T(128)}, u32[]{:S(2)}) copy-start(s32[3]{0:T(128)} %pad_add_fusion.ids) | copy-start | bytes 40
  168.1 16.5 %collective-permute-start.17 = (bf16[1536,128]{1,0:T(8,128)(2,1)}, bf16[1536,128]{1,0:T(8,128)(2,1)S(1)}, u32[]{:S(2)}, u32[]{:S(2)}) collective-permute-start(bf16[1536,128]{1,0:T(8,128)(2,1)} %core_sum.1), channel_id=1, source_target_pairs={{0,64},{64,0},{128,192},{192,128},{256,320},{320,256},{384,448},{4... | collective-permute-start | bytes 1179656 | tf_op jit(solution)/shard_map/ppermute | solution.py:22
  175.5 9.1 %copy-start.11 = (bf16[832,256]{1,0:T(8,128)(2,1)}, bf16[832,256]{1,0:T(8,128)(2,1)S(1)}, u32[]{:S(2)}) copy-start(bf16[832,256]{1,0:T(8,128)(2,1)S(1)} %collective-permute-done.18.y1) | copy-start | bytes 1277956
  175.6 9.0 %copy-start.13 = (bf16[832,256]{1,0:T(8,128)(2,1)}, bf16[832,256]{1,0:T(8,128)(2,1)S(1)}, u32[]{:S(2)}) copy-start(bf16[832,256]{1,0:T(8,128)(2,1)S(1)} %collective-permute-done.19.y3) | copy-start | bytes 1277956
  184.7 0.8 copy-start.22
  236.5 21.0 %collective-permute-start.20 = (bf16[3,1024,256]{2,1,0:T(8,128)(2,1)}, bf16[3,1024,256]{2,1,0:T(8,128)(2,1)S(1)}, u32[]{:S(2)}, u32[]{:S(2)}) collective-permute-start(bf16[3,1024,256]{2,1,0:T(8,128)(2,1)} %collect.3.near), channel_id=1, source_target_pairs={{0,32},{32,0},{1,33},{33,1},{2,34},{34,2},{3,35},{35,3},{4,36},{36... | collective-permute-start | bytes 4718600 | tf_op jit(solution)/shard_map/ppermute | solution.py:22
  239.5 17.9 %collective-permute-start.21 = (bf16[832,256]{1,0:T(8,128)(2,1)S(1)}, bf16[832,256]{1,0:T(8,128)(2,1)S(1)}, u32[]{:S(2)}, u32[]{:S(2)}) collective-permute-start(bf16[832,256]{1,0:T(8,128)(2,1)S(1)} %copy-done.9), channel_id=1, source_target_pairs={{0,16},{8,24},{16,0},{24,8},{1,17},{9,25},{17,1},{25,9},{2,18},{10... | collective-permute-start | bytes 1277960 | tf_op jit(solution)/shard_map/ppermute | solution.py:22
  241.5 29.6 %collective-permute-start.22 = (bf16[384,128]{1,0:T(8,128)(2,1)}, bf16[384,128]{1,0:T(8,128)(2,1)S(1)}, u32[]{:S(2)}, u32[]{:S(2)}) collective-permute-start(bf16[384,128]{1,0:T(8,128)(2,1)} %get-tuple-element.30.refs_3_.after), channel_id=1, source_target_pairs={{0,256},{64,320},{128,384},{192,448},{256,0},{320,64},{384,128},{4... | collective-permute-start | bytes 294920 | tf_op jit(solution)/shard_map/ppermute | solution.py:22
  251.5 19.5 %collective-permute-start.23 = (bf16[384,128]{1,0:T(8,128)(2,1)}, bf16[384,128]{1,0:T(8,128)(2,1)S(1)}, u32[]{:S(2)}, u32[]{:S(2)}) collective-permute-start(bf16[384,128]{1,0:T(8,128)(2,1)} %get-tuple-element.33), channel_id=1, source_target_pairs={{0,128},{64,192},{128,0},{192,64},{256,384},{320,448},{384,256},{4... | collective-permute-start | bytes 294920 | tf_op jit(solution)/shard_map/ppermute | solution.py:22
  253.5 17.6 %collective-permute-start.24 = (bf16[384,128]{1,0:T(8,128)(2,1)}, bf16[384,128]{1,0:T(8,128)(2,1)}, u32[]{:S(2)}, u32[]{:S(2)}) collective-permute-start(bf16[384,128]{1,0:T(8,128)(2,1)} %get-tuple-element.34), channel_id=1, source_target_pairs={{0,384},{64,448},{128,256},{192,320},{256,128},{320,192},{384,0},{... | collective-permute-start | bytes 294920 | tf_op jit(solution)/shard_map/ppermute | solution.py:22
  257.5 1.4 copy-start.4
  258.9 1.0 copy-start.10
  259.9 1.0 copy-start.12
  260.9 1.0 copy-start.14
  261.9 1.2 copy-start.17
  (2 other events, 1.3 us)

commit v3 on v2

--- a/solution.py
+++ b/solution.py
@@ -33,7 +33,7 @@
     return hi, mid, (rest - mid.astype(F32)).astype(BF)
 
 
-def params(mib=24):
+def params(mib=44):
     return pltpu.CompilerParams(
         dimension_semantics=("arbitrary",), vmem_limit_bytes=mib * 1024 * 1024
     )
@@ -101,21 +101,12 @@
     )(ids, gate_scales, up_scales, down_scales, gate, up, down)
 
 
-def forward_kernel(
-    ids, tokens, out_grad, m0, m1, t0, t1, after, own, p1, p2, p3, w_out, half, w_down, rows_in, sems
-):
+def forward_kernel(ids, tokens, out_grad, m0, m1, t0, t1, own, p1, p2, p3, w_out, w_down):
     step = pl.program_id(0)
-    z, core, x = ids[0], ids[1], ids[2]
-
-    def fetch(k, r):
-        source = (tokens, out_grad)[k].at[pl.ds(pl.multiple_of((x ^ r) * RB, RB), RB), :]
-        return pltpu.make_async_copy(source, rows_in.at[k, r], sems.at[k, r])
+    z, core = ids[0], ids[1]
 
     @pl.when(step == 0)
     def _():
-        for r in range(XS):
-            for k in range(2):
-                fetch(k, r).start()
         for i in range(Z):
             base = (z ^ far_first(i)) * (2 * T)
             for pair, side in (((m0, m1), core), ((t0, t1), 1 - core)):
@@ -124,13 +115,8 @@
                 w_out[rows, :] = ref[j * T : (j + 1) * T, 0 : 2 * T]
                 w_down[rows, :] = ref[j * T : (j + 1) * T, 2 * T : 3 * T]
 
-        half[0 : 4 * T, :] = m0[:, 0 : 2 * T]
-        half[4 * T : 8 * T, :] = m1[:, 0 : 2 * T]
-
-    fetch(0, step).wait()
-    gate_up = jnp.dot(rows_in[0, step], w_out[...], preferred_element_type=F32)
-    fetch(1, step).wait()
-    back = jnp.dot(rows_in[1, step], w_down[...], preferred_element_type=F32)
+    gate_up = jnp.dot(tokens[...], w_out[...], preferred_element_type=F32)
+    back = jnp.dot(out_grad[...], w_down[...], preferred_element_type=F32)
 
     @pl.when(step == 0)
     def _():
@@ -145,21 +131,18 @@
             ref[:, 2 * T : 3 * T] = back.astype(BF)
 
 
-def forward(ids, tokens, out_grad, mine, theirs, after):
+def forward(ids, tokens, out_grad, mine, theirs):
     whole = lambda *shape: pl.BlockSpec(shape, lambda r, ids: (0,) * len(shape))
+    rows = pl.BlockSpec((RB, D), lambda r, ids: (ids[2] ^ r, 0))
     part = jax.ShapeDtypeStruct((RB, 3 * T), BF)
     return pl.pallas_call(
         forward_kernel,
         grid_spec=pltpu.PrefetchScalarGridSpec(
             num_scalar_prefetch=1,
             grid=(XS,),
-            in_specs=[HBM, HBM] + [whole(4 * T, 3 * T)] * 4 + [ANY],
-            out_specs=[whole(RB, 3 * T)] * 4 + [whole(D, 2 * T), whole(8 * T, 2 * T)],
-            scratch_shapes=[
-                pltpu.VMEM((D, T), BF),
-                pltpu.VMEM((2, XS, RB, D), BF),
-                pltpu.SemaphoreType.DMA((2, XS)),
-            ],
+            in_specs=[rows, rows] + [whole(4 * T, 3 * T)] * 4,
+            out_specs=[whole(RB, 3 * T)] * 4 + [whole(D, 2 * T)],
+            scratch_shapes=[pltpu.VMEM((D, T), BF)],
         ),
         out_shape=[
             jax.ShapeDtypeStruct((RB, 3 * T), F32),
@@ -167,12 +150,11 @@
             part,
             part,
             jax.ShapeDtypeStruct((D, 2 * T), BF),
-            jax.ShapeDtypeStruct((8 * T, 2 * T), BF),
         ],
-        compiler_params=params(56),
+        compiler_params=params(),
         cost_estimate=work(2 * CAP * D * 3 * T, 10),
         name="forward",
-    )(ids, tokens, out_grad, *mine, *theirs, after)
+    )(ids, tokens, out_grad, *mine, *theirs)
 
 
 def reduce_kernel(own, g1, g2, g3, total):
@@ -189,28 +171,6 @@
         out_specs=VMEM,
         name="reduce_rows",
     )(own, *got)
-
-
-def collect_kernel(*refs):
-    n = len(refs) - 3
-    out, sems = refs[-2], refs[-1]
-    copies = [pltpu.make_async_copy(refs[i], out.at[i], sems.at[i]) for i in range(n)]
-    for copy in copies:
-        copy.start()
-    for copy in copies:
-        copy.wait()
-
-
-def collect(arrays, after):
-    n = len(arrays)
-    return pl.pallas_call(
-        collect_kernel,
-        out_shape=jax.ShapeDtypeStruct((n,) + arrays[0].shape, arrays[0].dtype),
-        in_specs=[ANY] * (n + 1),
-        out_specs=ANY,
-        scratch_shapes=[pltpu.SemaphoreType.DMA((n,))],
-        name="collect",
-    )(*arrays, after)
 
 
 def delta_kernel(ids, s_mine, s_theirs, per_row, out):
@@ -249,47 +209,19 @@
     )(ids, s_mine, s_theirs, per_row)
 
 
-def weight_grad_kernel(
-    ids,
-    tokens,
-    out_grad,
-    per_row,
-    d0,
-    d1,
-    d2,
-    d3,
-    a,
-    b,
-    c,
-    keep,
-    send,
-    flat,
-    turned,
-    columns_in,
-    sems,
-):
+def weight_grad_kernel(ids, tokens, out_grad, per_row, d0, d1, d2, d3, keep, send, flat, turned):
     step = pl.program_id(0)
-    z, core, x = ids[0], ids[1], ids[2]
-
-    def fetch(k, i):
-        columns = pl.ds(pl.multiple_of((z ^ far_first(i ^ 4)) * (2 * T), 2 * T), 2 * T)
-        source = (tokens, out_grad)[k].at[:, columns]
-        return pltpu.make_async_copy(source, columns_in.at[k, i], sems.at[k, i])
+    core, x = ids[1], ids[2]
 
     @pl.when(step == 0)
     def _():
-        for i in range(Z):
-            for k in range(2):
-                fetch(k, i).start()
         for r, ref in enumerate((d0, d1, d2, d3)):
             rows = pl.ds(pl.multiple_of((x ^ r) * RB, RB), RB)
             flat[rows, :] = ref[0:RB, :]
         turned[...] = flat[...].astype(F32).T.astype(BF)
 
-    fetch(0, step).wait()
-    gate_up = jnp.dot(turned[0 : 2 * T, :], columns_in[0, step], preferred_element_type=F32)
-    fetch(1, step).wait()
-    scaled = (columns_in[1, step].astype(F32) * per_row[:, 0:1]).astype(BF)
+    scaled = (out_grad[...].astype(F32) * per_row[:, 0:1]).astype(BF)
+    gate_up = jnp.dot(turned[0 : 2 * T, :], tokens[...], preferred_element_type=F32)
     down = jnp.dot(turned[2 * T : 3 * T, :], scaled, preferred_element_type=F32)
     for rows, value in ((slice(0, 2 * T), gate_up), (slice(2 * T, 3 * T), down)):
         low, high = value[:, 0:T].astype(BF), value[:, T : 2 * T].astype(BF)
@@ -297,28 +229,24 @@
         send[rows, :] = jnp.where(core == 0, high, low)
 
 
-def weight_grads(ids, tokens, out_grad, per_row, parts, after):
+def weight_grads(ids, tokens, out_grad, per_row, parts):
     whole = lambda *shape: pl.BlockSpec(shape, lambda i, ids: (0,) * len(shape))
+    columns = pl.BlockSpec((CAP, 2 * T), lambda i, ids: (0, ids[0] ^ far_first(i ^ 4)))
     block = pl.BlockSpec((3 * T, T), lambda i, ids: (i, 0))
     return pl.pallas_call(
         weight_grad_kernel,
         grid_spec=pltpu.PrefetchScalarGridSpec(
             num_scalar_prefetch=1,
             grid=(Z,),
-            in_specs=[HBM, HBM, whole(CAP, T)] + [whole(MSG, 3 * T)] * 4 + [ANY] * 3,
+            in_specs=[columns, columns, whole(CAP, T)] + [whole(MSG, 3 * T)] * 4,
             out_specs=[block, block],
-            scratch_shapes=[
-                pltpu.VMEM((CAP, 3 * T), BF),
-                pltpu.VMEM((3 * T, CAP), BF),
-                pltpu.VMEM((2, Z, CAP, 2 * T), BF),
-                pltpu.SemaphoreType.DMA((2, Z)),
-            ],
+            scratch_shapes=[pltpu.VMEM((CAP, 3 * T), BF), pltpu.VMEM((3 * T, CAP), BF)],
         ),
         out_shape=[jax.ShapeDtypeStruct((Z * 3 * T, T), BF)] * 2,
         compiler_params=params(),
         cost_estimate=work(2 * CAP * D * 3 * T, 10),
         name="weight_grads",
-    )(ids, tokens, out_grad, per_row, *parts, *after)
+    )(ids, tokens, out_grad, per_row, *parts)
 
 
 def core_sum_kernel(keep, received, send):
@@ -354,7 +282,7 @@
     )(ids, *parts, after)
 
 
-def pair_sum_kernel(keep, received, arrived, y1, y3, own, s4, s2, s6):
+def pair_sum_kernel(keep, received, arrived, own, s4, s2, s6):
     for i, out in enumerate((own, s4, s2, s6)):
         there = slice(i * 3 * T, (i + 1) * 3 * T)
         here = slice((i + 4) * 3 * T, (i + 5) * 3 * T)
@@ -362,15 +290,15 @@
         out[...] = (total + arrived[there, :].astype(F32)).astype(out.dtype)
 
 
-def pair_sum(keep, received, arrived, after):
+def pair_sum(keep, received, arrived):
     part = jax.ShapeDtypeStruct((3 * T, T), BF)
     return pl.pallas_call(
         pair_sum_kernel,
         out_shape=[jax.ShapeDtypeStruct((3 * T, T), F32), part, part, part],
-        in_specs=[VMEM] * 3 + [ANY] * 2,
+        in_specs=[VMEM] * 3,
         out_specs=[VMEM] * 4,
         name="pair_sum",
-    )(keep, received, arrived, *after)
+    )(keep, received, arrived)
 
 
 def last_sum_kernel(own, r4, r2, r6, after, gate, up, down):
@@ -391,18 +319,18 @@
 
 
 def token_grad_kernel(
-    ids, w0, near, far, y0, y1, y2, y3, per_row, after, out, logits_out, w, router
+    ids, weights, rows_by_y, per_row, after, out, logits_out, router
 ):
     step = pl.program_id(0)
-    core, x = ids[1], ids[2]
+    x = ids[2]
 
     @pl.when(step == 0)
     def _():
         for r in range(XS):
             rows = slice(CAP + 16 * r, CAP + 16 * (r + 1))
             terms = []
-            for ref in (y0, y1, y2, y3):
-                pieces = ref[rows, :].astype(F32)
+            for j in range(ROWS):
+                pieces = rows_by_y[j, rows, :].astype(F32)
                 terms.append(pieces[0:1] + pieces[1:2] + pieces[2:3])
             total = (terms[0] + terms[1]) + (terms[2] + terms[3])
             router[pl.ds(pl.multiple_of((x ^ r) * RB, RB), RB), :] = turn(total)[0:RB]
@@ -416,33 +344,32 @@
             total = total + jnp.dot(upper, piece, preferred_element_type=F32)
         logits_out[...] = total[0 : SEQ // T, :]
 
-    mine = pl.ds(pl.multiple_of(core * T, T), T)
-    theirs = pl.ds(pl.multiple_of((1 - core) * T, T), T)
-    total = lax.dot_general(y0[0:CAP, :], w0[...], NT, preferred_element_type=F32)
-    for j, ref in enumerate((y1, y2, y3)):
-        w[j, mine, :] = near[j]
-        w[j, theirs, :] = far[j]
-        total = total + lax.dot_general(ref[0:CAP, :], w[j], NT, preferred_element_type=F32)
+    total = jnp.zeros((CAP, 2 * T), F32)
+    for j in range(ROWS):
+        total += lax.dot_general(
+            rows_by_y[j, 0:CAP, :], weights[j], NT, preferred_element_type=F32
+        )
     out[...] = total.astype(BF)
 
 
-def token_grads(ids, w_own, near, far, rows_by_y, per_row, after):
+def token_grads(ids, weights, rows_by_y, per_row, after):
     whole = lambda *shape: pl.BlockSpec(shape, lambda i, ids: (0,) * len(shape))
-    zb = lambda i, ids: ids[0] ^ far_first(i)
-    tiles = pl.BlockSpec((3, T, 2 * T), lambda i, ids: (0, i, 0))
     return pl.pallas_call(
         token_grad_kernel,
         grid_spec=pltpu.PrefetchScalarGridSpec(
             num_scalar_prefetch=1,
             grid=(Z,),
-            in_specs=[pl.BlockSpec((2 * T, 2 * T), lambda i, ids: (zb(i, ids), 0)), tiles, tiles]
-            + [whole(CAP + XS * 16, 2 * T)] * 4
-            + [whole(CAP, T), ANY],
+            in_specs=[
+                pl.BlockSpec((ROWS, 2 * T, 2 * T), lambda i, ids: (0, i, 0)),
+                whole(ROWS, CAP + XS * 16, 2 * T),
+                whole(CAP, T),
+                ANY,
+            ],
             out_specs=[
-                pl.BlockSpec((CAP, 2 * T), lambda i, ids: (0, zb(i, ids))),
+                pl.BlockSpec((CAP, 2 * T), lambda i, ids: (0, i)),
                 whole(SEQ // T, T),
             ],
-            scratch_shapes=[pltpu.VMEM((3, 2 * T, 2 * T), BF), pltpu.VMEM((CAP, 1), F32)],
+            scratch_shapes=[pltpu.VMEM((CAP, 1), F32)],
         ),
         out_shape=[
             jax.ShapeDtypeStruct((CAP, D), BF),
@@ -451,7 +378,7 @@
         compiler_params=params(),
         cost_estimate=work(2 * CAP * D * 8 * T, 12),
         name="token_grads",
-    )(ids, w_own, near, far, *rows_by_y, per_row, after)
+    )(ids, weights, rows_by_y, per_row, after)
 
 
 def local(
@@ -477,27 +404,21 @@
     theirs = tuple(swap(h, "core", CORES, 1) for h in mine)
     per_row = rates(router_logits.reshape(SEQ // T, T), routed_positions[None, :], routed_counts)
 
-    own, p1, p2, p3, w_own, half = forward(ids, tokens, out_grad, mine, theirs, per_row)
+    own, p1, p2, p3, w_own = forward(ids, tokens, out_grad, mine, theirs)
     got = [swap(p, "x", XS, r) for r, p in ((1, p1), (2, p2), (3, p3))]
     total = reduce_rows(own, got)
     message = deltas(ids, total, swap(total, "zhi", Z_HI, 1), per_row)
     parts = [message] + [swap(message, "x", XS, r) for r in (1, 2, 3)]
 
-    half = collect([half], total)[0]
-    by_y = [swap(half, "row", ROWS, r) for r in (1, 2, 3)]
-
-    keep, send = weight_grads(ids, tokens, out_grad, per_row, parts, by_y)
+    weights = lax.all_gather(w_own, "row")
+
+    keep, send = weight_grads(ids, tokens, out_grad, per_row, parts)
     received = swap(send, "core", CORES, 1)
     arrived = swap(core_sum(keep, received), "z", Z, 1)
 
-    rows = row_order(ids, parts, keep)
-    y1, y2, y3 = (swap(rows, "row", ROWS, r) for r in (1, 2, 3))
-    own_sum, s4, s2, s6 = pair_sum(keep, received, arrived, (y1, y3))
-    near = collect(by_y, s4)
-    far = swap(near, "core", CORES, 1)
-    grad_tokens, grad_logits = token_grads(
-        ids, w_own, near, far, (rows, y1, y2, y3), per_row, s4
-    )
+    rows_by_y = lax.all_gather(row_order(ids, parts, keep), "row")
+    own_sum, s4, s2, s6 = pair_sum(keep, received, arrived)
+    grad_tokens, grad_logits = token_grads(ids, weights, rows_by_y, per_row, s4)
     grad_gate, grad_up, grad_down = last_sum(
         own_sum,
         swap(s4, "z", Z, 4),

time: 275 us -> 253 us (0.920)
  Pallas kernels: 107 us -> 32.3 us
  waiting for transfers between devices: 34.8 us -> 89.4 us
  starting transfers between devices: 114 us -> 92.8 us
  between operations: 1.77 us -> 15 us
  local copies, waits for them, and re-layouts: 13.7 us -> 20.6 us
    pallas_call x2 -> x0, Pallas kernels: 65.8 us -> none  [collect(): pl.pallas_call(collect_kernel, out_shape=jax.ShapeDtypeStruct((n,) + arra...]
    all_gather x0 -> x2, waiting for transfers between devices: none -> 56 us  [the longest x1 56 us: local(): weights = lax.all_gather(w_own, 'row')]
    ppermute x25 -> x18, starting transfers between devices: 114 us -> 92.7 us  [swap(): return lax.ppermute(value, axis, [(i, i ^ mask) for i in range(size)])]
    unnamed x50 -> x62, local copies, waits for them, and re-layouts: 12.4 us -> 20 us
    pallas_call x1, Pallas kernels: 9.52 us -> 3.13 us  [forward(): pl.pallas_call(forward_kernel, grid_spec=pltpu.PrefetchScalarGridSpec(num...]
    pallas_call x1, Pallas kernels: 7.9 us -> 4.92 us  [weight_grads(): pl.pallas_call(weight_grad_kernel, grid_spec=pltpu.PrefetchScalarGridSpec...]
    ppermute x25 -> x18, waiting for transfers between devices: 34.8 us -> 32.7 us  [swap(): return lax.ppermute(value, axis, [(i, i ^ mask) for i in range(size)])]
  transfers between devices with their start and end apart: 25 -> 20, of which waited for: 10 -> 11; matrix products, arithmetic and copies ran while one was open for 0% -> 0% of each run, Pallas kernels for 6% -> 6%
where the time goes in v3:
time: 253 us; the launch traced here: 252 us
  starting transfers between devices  92.8 us (37%)
  waiting for transfers between devices  89.4 us (35%)
  Pallas kernels  32.3 us (13%)
  local copies, waits for them, and re-layouts  20.6 us (8%)
  between operations  15 us (6%)
    ppermute x18, starting transfers between devices, swap(): return lax.ppermute(value, axis, [(i, i ^ mask) for i in range(size)])  92.7 us
    all_gather x1, waiting for transfers between devices, local(): weights = lax.all_gather(w_own, 'row')  56 us
    ppermute x18, waiting for transfers between devices, swap(): return lax.ppermute(value, axis, [(i, i ^ mask) for i in range(size)])  32.7 us
    unnamed x62, local copies, waits for them, and re-layouts  20 us
    pallas_call x1, Pallas kernels, token_grads(): pl.pallas_call(token_grad_kernel, grid_spec=pltpu.PrefetchScalarGridSpec(...  7.8 us
  transfers between devices with their start and end apart: 20, of which 11 were waited for; matrix products, arithmetic and copies ran while one was open for 0% of the time, Pallas kernels for 6%

profile of v3, /device:TPU:1, one launch (start us, length us, event | category | flops | bytes accessed | tf_op | source)
XLA Modules:
  0.0 251.7 jit_solution(6238498621387609504)
XLA Ops:
  7.8 1.7 own_tiles.1
  9.5 12.3 %collective-permute-start.2 = (bf16[128,384]{1,0:T(8,128)(2,1)}, bf16[128,384]{1,0:T(8,128)(2,1)S(1)}, u32[]{:S(2)}, u32[]{:S(2)}) collective-permute-start(bf16[128,384]{1,0:T(8,128)(2,1)} %own_tiles.1), channel_id=1, source_target_pairs={{0,384},{64,448},{128,256},{192,320},{256,128},{320,192},{384,0},{... | collective-permute-start | bytes 294920 | tf_op jit(solution)/shard_map/ppermute | solution.py:22
  21.8 1.9 collective-permute-start.1
  23.8 2.2 collective-permute-start
  26.0 2.6 %collective-permute-done.1 = bf16[128,384]{1,0:T(8,128)(2,1)S(1)} collective-permute-done((bf16[128,384]{1,0:T(8,128)(2,1)}, bf16[128,384]{1,0:T(8,128)(2,1)S(1)}, u32[]{:S(2)}, u32[]{:S(2)}) %collective-permute-start.1) | collective-permute-done | bytes 98336 | tf_op jit(solution)/shard_map/ppermute | solution.py:22
  28.6 4.6 %collective-permute-done = bf16[128,384]{1,0:T(8,128)(2,1)S(1)} collective-permute-done((bf16[128,384]{1,0:T(8,128)(2,1)}, bf16[128,384]{1,0:T(8,128)(2,1)S(1)}, u32[]{:S(2)}, u32[]{:S(2)}) %collective-permute-start) | collective-permute-done | bytes 98336 | tf_op jit(solution)/shard_map/ppermute | solution.py:22
  33.2 1.0 pad_maximum_fusion.m0
  34.2 8.3 %collective-permute-start.3 = (bf16[512,384]{1,0:T(8,128)(2,1)S(1)}, bf16[512,384]{1,0:T(8,128)(2,1)S(1)}, u32[]{:S(2)}, u32[]{:S(2)}) collective-permute-start(bf16[512,384]{1,0:T(8,128)(2,1)S(1)} %pad_maximum_fusion.m0), channel_id=1, source_target_pairs={{0,64},{64,0},{128,192},{192,128},{256,320},{320,256},{384,448},{4... | collective-permute-start | bytes 1179656 | tf_op jit(solution)/shard_map/ppermute | solution.py:22
  42.5 3.9 %collective-permute-start.4 = (bf16[512,384]{1,0:T(8,128)(2,1)S(1)}, bf16[512,384]{1,0:T(8,128)(2,1)S(1)}, u32[]{:S(2)}, u32[]{:S(2)}) collective-permute-start(bf16[512,384]{1,0:T(8,128)(2,1)S(1)} %pad_maximum_fusion.m0), channel_id=1, source_target_pairs={{0,32},{32,0},{1,33},{33,1},{2,34},{34,2},{3,35},{35,3},{4,36},{36... | collective-permute-start | bytes 1179656 | tf_op jit(solution)/shard_map/ppermute | solution.py:22
  46.4 2.7 %collective-permute-done.3.m1 = bf16[512,384]{1,0:T(8,128)(2,1)S(1)} collective-permute-done((bf16[512,384]{1,0:T(8,128)(2,1)S(1)}, bf16[512,384]{1,0:T(8,128)(2,1)S(1)}, u32[]{:S(2)}, u32[]{:S(2)}) %collective-permute-start.3) | collective-permute-done | bytes 393248 | tf_op jit(solution)/shard_map/ppermute | solution.py:22
  49.1 5.3 %collective-permute-start.5 = (bf16[512,384]{1,0:T(8,128)(2,1)S(1)}, bf16[512,384]{1,0:T(8,128)(2,1)S(1)}, u32[]{:S(2)}, u32[]{:S(2)}) collective-permute-start(bf16[512,384]{1,0:T(8,128)(2,1)S(1)} %collective-permute-done.3.m1), channel_id=1, source_target_pairs={{0,32},{32,0},{1,33},{33,1},{2,34},{34,2},{3,35},{35,3},{4,36},{36... | collective-permute-start | bytes 1179656 | tf_op jit(solution)/shard_map/ppermute | solution.py:22
  54.5 1.3 collective-permute-done.5.t1
  55.8 1.9 copy-done
  57.7 1.9 copy-done.2
  60.2 3.1 %forward.1 = (f32[192,384]{1,0:T(8,128)S(1)}, bf16[192,384]{1,0:T(8,128)(2,1)S(1)}, bf16[192,384]{1,0:T(8,128)(2,1)S(1)}, bf16[192,384]{1,0:T(8,128)(2,1)S(1)}, bf16[2048,256]{1,0:T(8,128)(2,1)S(1)}) custom-call(s32[3]{0:T(128)S(1)} %copy-done.13, bf16[768,2048]{1,0:T(8,128)(2,1)S(1)} %copy-done, bf16[768,2048]{1,0:T(8,128)(2,1)S(1)} %copy-done.2, ...), custom_call_target="tpu_custom_call" | custom-call | flops 1207959552 | bytes 10485760 | tf_op jit(solution)/shard_map/forward/pallas_call | solution.py:138
  63.4 1.0 copy-done.8
  65.0 3.1 %collective-permute-start.6 = (bf16[192,384]{1,0:T(8,128)(2,1)S(1)}, bf16[192,384]{1,0:T(8,128)(2,1)S(1)}, u32[]{:S(2)}, u32[]{:S(2)}) collective-permute-start(bf16[192,384]{1,0:T(8,128)(2,1)S(1)} %get-tuple-element.23), channel_id=1, source_target_pairs={{0,1},{1,0},{2,3},{3,2},{4,5},{5,4},{6,7},{7,6},{8,9},{9,8},{10,11... | collective-permute-start | bytes 442376 | tf_op jit(solution)/shard_map/ppermute | solution.py:22
  68.2 4.4 %collective-permute-start.7 = (bf16[192,384]{1,0:T(8,128)(2,1)S(1)}, bf16[192,384]{1,0:T(8,128)(2,1)S(1)}, u32[]{:S(2)}, u32[]{:S(2)}) collective-permute-start(bf16[192,384]{1,0:T(8,128)(2,1)S(1)} %get-tuple-element.24), channel_id=1, source_target_pairs={{0,2},{1,3},{2,0},{3,1},{4,6},{5,7},{6,4},{7,5},{8,10},{9,11},{10,... | collective-permute-start | bytes 442376 | tf_op jit(solution)/shard_map/ppermute | solution.py:22
  72.5 2.1 collective-permute-start.8
  74.7 2.8 %collective-permute-done.7.g2 = bf16[192,384]{1,0:T(8,128)(2,1)S(1)} collective-permute-done((bf16[192,384]{1,0:T(8,128)(2,1)S(1)}, bf16[192,384]{1,0:T(8,128)(2,1)S(1)}, u32[]{:S(2)}, u32[]{:S(2)}) %collective-permute-start.7) | collective-permute-done | bytes 147488 | tf_op jit(solution)/shard_map/ppermute | solution.py:22
  77.5 2.6 %collective-permute-done.8.g3 = bf16[192,384]{1,0:T(8,128)(2,1)S(1)} collective-permute-done((bf16[192,384]{1,0:T(8,128)(2,1)S(1)}, bf16[192,384]{1,0:T(8,128)(2,1)S(1)}, u32[]{:S(2)}, u32[]{:S(2)}) %collective-permute-start.8) | collective-permute-done | bytes 147488 | tf_op jit(solution)/shard_map/ppermute | solution.py:22
  80.7 1.9 reduce_rows.1.s_mine
  82.6 11.6 %collective-permute-start.9 = (bf16[192,384]{1,0:T(8,128)(2,1)}, bf16[192,384]{1,0:T(8,128)(2,1)S(1)}, u32[]{:S(2)}, u32[]{:S(2)}) collective-permute-start(bf16[192,384]{1,0:T(8,128)(2,1)} %reduce_rows.1.s_mine), channel_id=1, source_target_pairs={{0,4},{4,0},{1,5},{5,1},{2,6},{6,2},{3,7},{7,3},{8,12},{12,8},{9,1... | collective-permute-start | bytes 442376 | tf_op jit(solution)/shard_map/ppermute | solution.py:22
  95.4 2.3 rates.1.per_row
  98.4 2.1 deltas.1.d0
  100.5 3.5 %collective-permute-start.12 = (bf16[208,384]{1,0:T(8,128)(2,1)}, bf16[208,384]{1,0:T(8,128)(2,1)S(1)}, u32[]{:S(2)}, u32[]{:S(2)}) collective-permute-start(bf16[208,384]{1,0:T(8,128)(2,1)} %deltas.1.d0), channel_id=1, source_target_pairs={{0,3},{1,2},{2,1},{3,0},{4,7},{5,6},{6,5},{7,4},{8,11},{9,10},{10,... | collective-permute-start | bytes 479240 | tf_op jit(solution)/shard_map/ppermute | solution.py:22
  104.0 3.8 %collective-permute-start.11 = (bf16[208,384]{1,0:T(8,128)(2,1)}, bf16[208,384]{1,0:T(8,128)(2,1)S(1)}, u32[]{:S(2)}, u32[]{:S(2)}) collective-permute-start(bf16[208,384]{1,0:T(8,128)(2,1)} %deltas.1.d0), channel_id=1, source_target_pairs={{0,2},{1,3},{2,0},{3,1},{4,6},{5,7},{6,4},{7,5},{8,10},{9,11},{10,... | collective-permute-start | bytes 479240 | tf_op jit(solution)/shard_map/ppermute | solution.py:22
  107.8 1.9 collective-permute-start.10
  109.8 2.0 collective-permute-done.11.d2
  111.8 2.5 %collective-permute-done.10.d1 = bf16[208,384]{1,0:T(8,128)(2,1)S(1)} collective-permute-done((bf16[208,384]{1,0:T(8,128)(2,1)}, bf16[208,384]{1,0:T(8,128)(2,1)S(1)}, u32[]{:S(2)}, u32[]{:S(2)}) %collective-permute-start.10) | collective-permute-done | bytes 159776 | tf_op jit(solution)/shard_map/ppermute | solution.py:22
  114.4 1.9 copy-done.3
  116.3 1.0 copy-done.5
  118.2 4.9 %weight_grads.1 = (bf16[3072,128]{1,0:T(8,128)(2,1)S(1)}, bf16[3072,128]{1,0:T(8,128)(2,1)S(1)}) custom-call(s32[3]{0:T(128)S(1)} %copy-done.14, bf16[768,2048]{1,0:T(8,128)(2,1)S(1)} %copy-done.1, bf16[768,2048]{1,0:T(8,128)(2,1)S(1)} %copy-done.3, f32[768,128]{1,0:T(8,128)S(1)} %copy-done.5, bf16[208,384]{1,0:T(8,128)(2,1)S(1)} %copy-done.7, ...), custom_call_target="tpu_custom_call" | custom-call | flops 1207959552 | bytes 10485760 | tf_op jit(solution)/shard_map/weight_grads/pallas_call | solution.py:236
  124.9 2.1 row_order.1
  127.8 5.9 %collective-permute-start.13 = (bf16[3072,128]{1,0:T(8,128)(2,1)S(1)}, bf16[3072,128]{1,0:T(8,128)(2,1)S(1)}, u32[]{:S(2)}, u32[]{:S(2)}) collective-permute-start(bf16[3072,128]{1,0:T(8,128)(2,1)S(1)} %copy-done.19), channel_id=1, source_target_pairs={{0,32},{32,0},{1,33},{33,1},{2,34},{34,2},{3,35},{35,3},{4,36},{36... | collective-permute-start | bytes 2359304 | tf_op jit(solution)/shard_map/ppermute | solution.py:22
  133.7 1.9 collective-permute-done.13.received
  136.5 2.2 core_sum.1
  138.8 9.2 %collective-permute-start.14 = (bf16[1536,128]{1,0:T(8,128)(2,1)}, bf16[1536,128]{1,0:T(8,128)(2,1)S(1)}, u32[]{:S(2)}, u32[]{:S(2)}) collective-permute-start(bf16[1536,128]{1,0:T(8,128)(2,1)} %core_sum.1), channel_id=1, source_target_pairs={{0,64},{64,0},{128,192},{192,128},{256,320},{320,256},{384,448},{4... | collective-permute-start | bytes 1179656 | tf_op jit(solution)/shard_map/ppermute | solution.py:22
  148.0 9.5 %collective-permute-done.14.arrived = bf16[1536,128]{1,0:T(8,128)(2,1)S(1)} collective-permute-done((bf16[1536,128]{1,0:T(8,128)(2,1)}, bf16[1536,128]{1,0:T(8,128)(2,1)S(1)}, u32[]{:S(2)}, u32[]{:S(2)}) %collective-permute-start.14) | collective-permute-done | bytes 393248 | tf_op jit(solution)/shard_map/ppermute | solution.py:22
  158.3 2.3 pair_sum.1
  160.6 2.0 collective-permute-start.16
  162.6 9.1 %collective-permute-start.17 = (bf16[384,128]{1,0:T(8,128)(2,1)}, bf16[384,128]{1,0:T(8,128)(2,1)S(1)}, u32[]{:S(2)}, u32[]{:S(2)}) collective-permute-start(bf16[384,128]{1,0:T(8,128)(2,1)} %get-tuple-element.32), channel_id=1, source_target_pairs={{0,384},{64,448},{128,256},{192,320},{256,128},{320,192},{384,0},{... | collective-permute-start | bytes 294920 | tf_op jit(solution)/shard_map/ppermute | solution.py:22
  171.7 2.2 collective-permute-start.15
  173.9 56.0 %all-gather.5.cloned.1.call-done = bf16[8192,256]{1,0:T(8,128)(2,1)} async-done(((bf16[2048,256]{1,0:T(8,128)(2,1)}), bf16[8192,256]{1,0:T(8,128)(2,1)}) %all-gather.5.cloned.1.call-update) | async-done | bytes 4194320 | tf_op jit(solution)/shard_map/all_gather | solution.py:413
  229.9 2.2 copy-done.16
  232.1 1.5 copy-done.17
  234.4 7.8 %token_grads.1 = (bf16[768,2048]{1,0:T(8,128)(2,1)}, f32[48,128]{1,0:T(8,128)}) custom-call(s32[3]{0:T(128)S(1)} %copy-done.15, bf16[4,2048,256]{2,1,0:T(8,128)(2,1)S(1)} %bitcast.9, bf16[4,832,256]{2,1,0:T(8,128)(2,1)S(1)} %bitcast.10, f32[768,128]{1,0:T(8,128)S(1)} %copy-done.6, bf16[384,128]{1,0:T(8,128)(2,1)S(1)} %copy-done.20), custom_call_target="tpu_custom_call" | custom-call | flops 3221225472 | bytes 12582912 | tf_op jit(solution)/shard_map/token_grads/pallas_call | solution.py:357
  243.0 1.9 last_sum.1
  (70 shorter events, 10.7 us)
Async XLA Ops:
  7.2 166.8 %all-gather.7.cloned.1.call-start = ((), (), s32[]{:S(2)}) async-start(), calls=%async_computation.1 | async-start | bytes 2129920 | tf_op jit(solution)/shard_map/all_gather | solution.py:419
  9.5 16.5 %collective-permute-start.2 = (bf16[128,384]{1,0:T(8,128)(2,1)}, bf16[128,384]{1,0:T(8,128)(2,1)S(1)}, u32[]{:S(2)}, u32[]{:S(2)}) collective-permute-start(bf16[128,384]{1,0:T(8,128)(2,1)} %own_tiles.1), channel_id=1, source_target_pairs={{0,384},{64,448},{128,256},{192,320},{256,128},{320,192},{384,0},{... | collective-permute-start | bytes 294920 | tf_op jit(solution)/shard_map/ppermute | solution.py:22
  21.8 6.8 %collective-permute-start.1 = (bf16[128,384]{1,0:T(8,128)(2,1)}, bf16[128,384]{1,0:T(8,128)(2,1)S(1)}, u32[]{:S(2)}, u32[]{:S(2)}) collective-permute-start(bf16[128,384]{1,0:T(8,128)(2,1)} %own_tiles.1), channel_id=1, source_target_pairs={{0,128},{64,192},{128,0},{192,64},{256,384},{320,448},{384,256},{4... | collective-permute-start | bytes 294920 | tf_op jit(solution)/shard_map/ppermute | solution.py:22
  23.8 9.5 %collective-permute-start = (bf16[128,384]{1,0:T(8,128)(2,1)}, bf16[128,384]{1,0:T(8,128)(2,1)S(1)}, u32[]{:S(2)}, u32[]{:S(2)}) collective-permute-start(bf16[128,384]{1,0:T(8,128)(2,1)} %own_tiles.1), channel_id=1, source_target_pairs={{0,256},{64,320},{128,384},{192,448},{256,0},{320,64},{384,128},{4... | collective-permute-start | bytes 294920 | tf_op jit(solution)/shard_map/ppermute | solution.py:22
  33.2 61.6 %copy-start.30 = (s32[768]{0:T(1024)S(1)}, s32[768]{0:T(1024)}, u32[]{:S(2)}) copy-start(s32[768]{0:T(1024)} %param.15) | copy-start | bytes 9220
  33.2 81.1 %copy-start.14 = (s32[3]{0:T(128)S(1)}, s32[3]{0:T(128)}, u32[]{:S(2)}) copy-start(s32[3]{0:T(128)} %pad_add_fusion.ids) | copy-start | bytes 40
  34.2 14.9 %collective-permute-start.3 = (bf16[512,384]{1,0:T(8,128)(2,1)S(1)}, bf16[512,384]{1,0:T(8,128)(2,1)S(1)}, u32[]{:S(2)}, u32[]{:S(2)}) collective-permute-start(bf16[512,384]{1,0:T(8,128)(2,1)S(1)} %pad_maximum_fusion.m0), channel_id=1, source_target_pairs={{0,64},{64,0},{128,192},{192,128},{256,320},{320,256},{384,448},{4... | collective-permute-start | bytes 1179656 | tf_op jit(solution)/shard_map/ppermute | solution.py:22
  42.5 12.0 %collective-permute-start.4 = (bf16[512,384]{1,0:T(8,128)(2,1)S(1)}, bf16[512,384]{1,0:T(8,128)(2,1)S(1)}, u32[]{:S(2)}, u32[]{:S(2)}) collective-permute-start(bf16[512,384]{1,0:T(8,128)(2,1)S(1)} %pad_maximum_fusion.m0), channel_id=1, source_target_pairs={{0,32},{32,0},{1,33},{33,1},{2,34},{34,2},{3,35},{35,3},{4,36},{36... | collective-permute-start | bytes 1179656 | tf_op jit(solution)/shard_map/ppermute | solution.py:22
  49.1 6.6 %collective-permute-start.5 = (bf16[512,384]{1,0:T(8,128)(2,1)S(1)}, bf16[512,384]{1,0:T(8,128)(2,1)S(1)}, u32[]{:S(2)}, u32[]{:S(2)}) collective-permute-start(bf16[512,384]{1,0:T(8,128)(2,1)S(1)} %collective-permute-done.3.m1), channel_id=1, source_target_pairs={{0,32},{32,0},{1,33},{33,1},{2,34},{34,2},{3,35},{35,3},{4,36},{36... | collective-permute-start | bytes 1179656 | tf_op jit(solution)/shard_map/ppermute | solution.py:22
  55.8 1.9 copy-start
  57.7 1.9 copy-start.2
  60.2 54.2 %copy-start.1 = (bf16[768,2048]{1,0:T(8,128)(2,1)S(1)}, bf16[768,2048]{1,0:T(8,128)(2,1)}, u32[]{:S(2)}) copy-start(bf16[768,2048]{1,0:T(8,128)(2,1)} %tokens.3) | copy-start | bytes 9437188
  63.3 1.0 copy-start.8
  64.3 0.7 copy-start.12
  65.0 9.6 %collective-permute-start.6 = (bf16[192,384]{1,0:T(8,128)(2,1)S(1)}, bf16[192,384]{1,0:T(8,128)(2,1)S(1)}, u32[]{:S(2)}, u32[]{:S(2)}) collective-permute-start(bf16[192,384]{1,0:T(8,128)(2,1)S(1)} %get-tuple-element.23), channel_id=1, source_target_pairs={{0,1},{1,0},{2,3},{3,2},{4,5},{5,4},{6,7},{7,6},{8,9},{9,8},{10,11... | collective-permute-start | bytes 442376 | tf_op jit(solution)/shard_map/ppermute | solution.py:22
  68.2 9.3 %collective-permute-start.7 = (bf16[192,384]{1,0:T(8,128)(2,1)S(1)}, bf16[192,384]{1,0:T(8,128)(2,1)S(1)}, u32[]{:S(2)}, u32[]{:S(2)}) collective-permute-start(bf16[192,384]{1,0:T(8,128)(2,1)S(1)} %get-tuple-element.24), channel_id=1, source_target_pairs={{0,2},{1,3},{2,0},{3,1},{4,6},{5,7},{6,4},{7,5},{8,10},{9,11},{10,... | collective-permute-start | bytes 442376 | tf_op jit(solution)/shard_map/ppermute | solution.py:22
  72.5 7.5 %collective-permute-start.8 = (bf16[192,384]{1,0:T(8,128)(2,1)S(1)}, bf16[192,384]{1,0:T(8,128)(2,1)S(1)}, u32[]{:S(2)}, u32[]{:S(2)}) collective-permute-start(bf16[192,384]{1,0:T(8,128)(2,1)S(1)} %get-tuple-element.25), channel_id=1, source_target_pairs={{0,3},{1,2},{2,1},{3,0},{4,7},{5,6},{6,5},{7,4},{8,11},{9,10},{10,... | collective-permute-start | bytes 442376 | tf_op jit(solution)/shard_map/ppermute | solution.py:22
  74.6 6.1 %copy-start.23 = (bf16[192,384]{1,0:T(8,128)(2,1)}, bf16[192,384]{1,0:T(8,128)(2,1)S(1)}, u32[]{:S(2)}) copy-start(bf16[192,384]{1,0:T(8,128)(2,1)S(1)} %collective-permute-done.6.g1) | copy-start | bytes 442372
  77.5 3.2 %copy-start.24 = (bf16[192,384]{1,0:T(8,128)(2,1)}, bf16[192,384]{1,0:T(8,128)(2,1)S(1)}, u32[]{:S(2)}) copy-start(bf16[192,384]{1,0:T(8,128)(2,1)S(1)} %collective-permute-done.7.g2) | copy-start | bytes 442372
  82.6 15.1 %collective-permute-start.9 = (bf16[192,384]{1,0:T(8,128)(2,1)}, bf16[192,384]{1,0:T(8,128)(2,1)S(1)}, u32[]{:S(2)}, u32[]{:S(2)}) collective-permute-start(bf16[192,384]{1,0:T(8,128)(2,1)} %reduce_rows.1.s_mine), channel_id=1, source_target_pairs={{0,4},{4,0},{1,5},{5,1},{2,6},{6,2},{3,7},{7,3},{8,12},{12,8},{9,1... | collective-permute-start | bytes 442376 | tf_op jit(solution)/shard_map/ppermute | solution.py:22
  97.7 0.7 copy-start.26
  100.5 9.3 %collective-permute-start.12 = (bf16[208,384]{1,0:T(8,128)(2,1)}, bf16[208,384]{1,0:T(8,128)(2,1)S(1)}, u32[]{:S(2)}, u32[]{:S(2)}) collective-permute-start(bf16[208,384]{1,0:T(8,128)(2,1)} %deltas.1.d0), channel_id=1, source_target_pairs={{0,3},{1,2},{2,1},{3,0},{4,7},{5,6},{6,5},{7,4},{8,11},{9,10},{10,... | collective-permute-start | bytes 479240 | tf_op jit(solution)/shard_map/ppermute | solution.py:22
  104.0 7.8 %collective-permute-start.11 = (bf16[208,384]{1,0:T(8,128)(2,1)}, bf16[208,384]{1,0:T(8,128)(2,1)S(1)}, u32[]{:S(2)}, u32[]{:S(2)}) collective-permute-start(bf16[208,384]{1,0:T(8,128)(2,1)} %deltas.1.d0), channel_id=1, source_target_pairs={{0,2},{1,3},{2,0},{3,1},{4,6},{5,7},{6,4},{7,5},{8,10},{9,11},{10,... | collective-permute-start | bytes 479240 | tf_op jit(solution)/shard_map/ppermute | solution.py:22
  107.8 6.5 %collective-permute-start.10 = (bf16[208,384]{1,0:T(8,128)(2,1)}, bf16[208,384]{1,0:T(8,128)(2,1)S(1)}, u32[]{:S(2)}, u32[]{:S(2)}) collective-permute-start(bf16[208,384]{1,0:T(8,128)(2,1)} %deltas.1.d0), channel_id=1, source_target_pairs={{0,1},{1,0},{2,3},{3,2},{4,5},{5,4},{6,7},{7,6},{8,9},{9,8},{10,11... | collective-permute-start | bytes 479240 | tf_op jit(solution)/shard_map/ppermute | solution.py:22
  109.8 13.3 %copy-start.9 = (bf16[208,384]{1,0:T(8,128)(2,1)}, bf16[208,384]{1,0:T(8,128)(2,1)S(1)}, u32[]{:S(2)}) copy-start(bf16[208,384]{1,0:T(8,128)(2,1)S(1)} %collective-permute-done.12.d3) | copy-start | bytes 479236
  111.8 11.3 %copy-start.10 = (bf16[208,384]{1,0:T(8,128)(2,1)}, bf16[208,384]{1,0:T(8,128)(2,1)S(1)}, u32[]{:S(2)}) copy-start(bf16[208,384]{1,0:T(8,128)(2,1)S(1)} %collective-permute-done.11.d2) | copy-start | bytes 479236
  114.4 1.9 copy-start.3
  116.3 1.0 copy-start.5
  117.3 0.9 copy-start.7
  118.2 5.0 %copy-start.11 = (bf16[208,384]{1,0:T(8,128)(2,1)}, bf16[208,384]{1,0:T(8,128)(2,1)S(1)}, u32[]{:S(2)}) copy-start(bf16[208,384]{1,0:T(8,128)(2,1)S(1)} %collective-permute-done.10.d1) | copy-start | bytes 479236
  123.1 0.9 copy-start.4
  124.0 0.9 copy-start.18
  124.9 2.9 %copy-start.19 = (bf16[3072,128]{1,0:T(8,128)(2,1)S(1)}, bf16[3072,128]{1,0:T(8,128)(2,1)}, u32[]{:S(2)}) copy-start(bf16[3072,128]{1,0:T(8,128)(2,1)} %copy-done.18) | copy-start | bytes 2359300
  127.0 102.9 %copy-start.6 = (f32[768,128]{1,0:T(8,128)S(1)}, f32[768,128]{1,0:T(8,128)}, u32[]{:S(2)}) copy-start(f32[768,128]{1,0:T(8,128)} %rates.1.per_row) | copy-start | bytes 1179652
  127.0 102.9 %copy-start.15 = (s32[3]{0:T(128)S(1)}, s32[3]{0:T(128)}, u32[]{:S(2)}) copy-start(s32[3]{0:T(128)} %pad_add_fusion.ids) | copy-start | bytes 40
  127.0 102.9 %all-gather.5.cloned.1.call-start = ((), (), s32[]{:S(2)}) async-start(), calls=%async_computation | async-start | bytes 5242880 | tf_op jit(solution)/shard_map/all_gather | solution.py:413
  127.8 7.8 %collective-permute-start.13 = (bf16[3072,128]{1,0:T(8,128)(2,1)S(1)}, bf16[3072,128]{1,0:T(8,128)(2,1)S(1)}, u32[]{:S(2)}, u32[]{:S(2)}) collective-permute-start(bf16[3072,128]{1,0:T(8,128)(2,1)S(1)} %copy-done.19), channel_id=1, source_target_pairs={{0,32},{32,0},{1,33},{33,1},{2,34},{34,2},{3,35},{35,3},{4,36},{36... | collective-permute-start | bytes 2359304 | tf_op jit(solution)/shard_map/ppermute | solution.py:22
  135.6 0.9 copy-start.21
  138.8 18.7 %collective-permute-start.14 = (bf16[1536,128]{1,0:T(8,128)(2,1)}, bf16[1536,128]{1,0:T(8,128)(2,1)S(1)}, u32[]{:S(2)}, u32[]{:S(2)}) collective-permute-start(bf16[1536,128]{1,0:T(8,128)(2,1)} %core_sum.1), channel_id=1, source_target_pairs={{0,64},{64,0},{128,192},{192,128},{256,320},{320,256},{384,448},{4... | collective-permute-start | bytes 1179656 | tf_op jit(solution)/shard_map/ppermute | solution.py:22
  157.5 0.8 copy-start.22
  160.6 81.7 %collective-permute-start.16 = (bf16[384,128]{1,0:T(8,128)(2,1)}, bf16[384,128]{1,0:T(8,128)(2,1)S(1)}, u32[]{:S(2)}, u32[]{:S(2)}) collective-permute-start(bf16[384,128]{1,0:T(8,128)(2,1)} %get-tuple-element.31), channel_id=1, source_target_pairs={{0,128},{64,192},{128,0},{192,64},{256,384},{320,448},{384,256},{4... | collective-permute-start | bytes 294920 | tf_op jit(solution)/shard_map/ppermute | solution.py:22
  162.6 79.7 %collective-permute-start.17 = (bf16[384,128]{1,0:T(8,128)(2,1)}, bf16[384,128]{1,0:T(8,128)(2,1)S(1)}, u32[]{:S(2)}, u32[]{:S(2)}) collective-permute-start(bf16[384,128]{1,0:T(8,128)(2,1)} %get-tuple-element.32), channel_id=1, source_target_pairs={{0,384},{64,448},{128,256},{192,320},{256,128},{320,192},{384,0},{... | collective-permute-start | bytes 294920 | tf_op jit(solution)/shard_map/ppermute | solution.py:22
  171.7 70.6 %collective-permute-start.15 = (bf16[384,128]{1,0:T(8,128)(2,1)}, bf16[384,128]{1,0:T(8,128)(2,1)S(1)}, u32[]{:S(2)}, u32[]{:S(2)}) collective-permute-start(bf16[384,128]{1,0:T(8,128)(2,1)} %get-tuple-element.28.after), channel_id=1, source_target_pairs={{0,256},{64,320},{128,384},{192,448},{256,0},{320,64},{384,128},{4... | collective-permute-start | bytes 294920 | tf_op jit(solution)/shard_map/ppermute | solution.py:22
  229.9 2.2 copy-start.16
  232.1 1.5 copy-start.17
  233.6 0.9 copy-start.20
  242.3 0.7 copy-start.28
  242.3 0.7 copy-start.29
  (3 other events, 1.9 us)
Sparse Core Ops, SparseCore 0:
  127.2 44.0 all-gather.6
  173.9 55.9 all-gather.4

commit v4 on v3

--- a/solution.py
+++ b/solution.py
@@ -157,22 +157,6 @@
     )(ids, tokens, out_grad, *mine, *theirs)
 
 
-def reduce_kernel(own, g1, g2, g3, total):
-    total[...] = (
-        own[...] + g1[...].astype(F32) + g2[...].astype(F32) + g3[...].astype(F32)
-    ).astype(BF)
-
-
-def reduce_rows(own, got):
-    return pl.pallas_call(
-        reduce_kernel,
-        out_shape=jax.ShapeDtypeStruct((RB, 3 * T), BF),
-        in_specs=[VMEM] * 4,
-        out_specs=VMEM,
-        name="reduce_rows",
-    )(own, *got)
-
-
 def delta_kernel(ids, s_mine, s_theirs, per_row, out):
     total = s_mine[...].astype(F32) + s_theirs[...].astype(F32)
     gate, up, back = total[:, 0:T], total[:, T : 2 * T], total[:, 2 * T : 3 * T]
@@ -209,7 +193,9 @@
     )(ids, s_mine, s_theirs, per_row)
 
 
-def weight_grad_kernel(ids, tokens, out_grad, per_row, d0, d1, d2, d3, keep, send, flat, turned):
+def weight_grad_kernel(
+    ids, tokens, out_grad, per_row, d0, d1, d2, d3, after, keep, send, rows_out, flat, turned
+):
     step = pl.program_id(0)
     core, x = ids[1], ids[2]
 
@@ -218,6 +204,8 @@
         for r, ref in enumerate((d0, d1, d2, d3)):
             rows = pl.ds(pl.multiple_of((x ^ r) * RB, RB), RB)
             flat[rows, :] = ref[0:RB, :]
+            rows_out[rows, :] = ref[0:RB, 0 : 2 * T]
+            rows_out[CAP + 16 * r : CAP + 16 * (r + 1), :] = ref[RB:MSG, 0 : 2 * T]
         turned[...] = flat[...].astype(F32).T.astype(BF)
 
     scaled = (out_grad[...].astype(F32) * per_row[:, 0:1]).astype(BF)
@@ -229,7 +217,7 @@
         send[rows, :] = jnp.where(core == 0, high, low)
 
 
-def weight_grads(ids, tokens, out_grad, per_row, parts):
+def weight_grads(ids, tokens, out_grad, per_row, parts, after):
     whole = lambda *shape: pl.BlockSpec(shape, lambda i, ids: (0,) * len(shape))
     columns = pl.BlockSpec((CAP, 2 * T), lambda i, ids: (0, ids[0] ^ far_first(i ^ 4)))
     block = pl.BlockSpec((3 * T, T), lambda i, ids: (i, 0))
@@ -238,67 +226,19 @@
         grid_spec=pltpu.PrefetchScalarGridSpec(
             num_scalar_prefetch=1,
             grid=(Z,),
-            in_specs=[columns, columns, whole(CAP, T)] + [whole(MSG, 3 * T)] * 4,
-            out_specs=[block, block],
+            in_specs=[columns, columns, whole(CAP, T)] + [whole(MSG, 3 * T)] * 4 + [whole(16, T)],
+            out_specs=[block, block, whole(CAP + XS * 16, 2 * T)],
             scratch_shapes=[pltpu.VMEM((CAP, 3 * T), BF), pltpu.VMEM((3 * T, CAP), BF)],
         ),
-        out_shape=[jax.ShapeDtypeStruct((Z * 3 * T, T), BF)] * 2,
+        out_shape=[
+            jax.ShapeDtypeStruct((Z * 3 * T, T), BF),
+            jax.ShapeDtypeStruct((Z * 3 * T, T), BF),
+            jax.ShapeDtypeStruct((CAP + XS * 16, 2 * T), BF),
+        ],
         compiler_params=params(),
         cost_estimate=work(2 * CAP * D * 3 * T, 10),
         name="weight_grads",
-    )(ids, tokens, out_grad, per_row, *parts)
-
-
-def core_sum_kernel(keep, received, send):
-    rows = slice(0, 4 * 3 * T)
-    send[...] = (keep[rows, :].astype(F32) + received[rows, :].astype(F32)).astype(BF)
-
-
-def core_sum(keep, received):
-    return pl.pallas_call(
-        core_sum_kernel,
-        out_shape=jax.ShapeDtypeStruct((4 * 3 * T, T), BF),
-        in_specs=[VMEM] * 2,
-        out_specs=VMEM,
-        name="core_sum",
-    )(keep, received)
-
-
-def rows_kernel(ids, d0, d1, d2, d3, after, rows_out):
-    x = ids[2]
-    for r, ref in enumerate((d0, d1, d2, d3)):
-        rows = pl.ds(pl.multiple_of((x ^ r) * RB, RB), RB)
-        rows_out[rows, :] = ref[0:RB, 0 : 2 * T]
-        rows_out[CAP + 16 * r : CAP + 16 * (r + 1), :] = ref[RB:MSG, 0 : 2 * T]
-
-
-def row_order(ids, parts, after):
-    return pl.pallas_call(
-        rows_kernel,
-        out_shape=jax.ShapeDtypeStruct((CAP + XS * 16, 2 * T), BF),
-        in_specs=[SMEM] + [VMEM] * 4 + [ANY],
-        out_specs=VMEM,
-        name="row_order",
-    )(ids, *parts, after)
-
-
-def pair_sum_kernel(keep, received, arrived, own, s4, s2, s6):
-    for i, out in enumerate((own, s4, s2, s6)):
-        there = slice(i * 3 * T, (i + 1) * 3 * T)
-        here = slice((i + 4) * 3 * T, (i + 5) * 3 * T)
-        total = keep[here, :].astype(F32) + received[here, :].astype(F32)
-        out[...] = (total + arrived[there, :].astype(F32)).astype(out.dtype)
-
-
-def pair_sum(keep, received, arrived):
-    part = jax.ShapeDtypeStruct((3 * T, T), BF)
-    return pl.pallas_call(
-        pair_sum_kernel,
-        out_shape=[jax.ShapeDtypeStruct((3 * T, T), F32), part, part, part],
-        in_specs=[VMEM] * 3,
-        out_specs=[VMEM] * 4,
-        name="pair_sum",
-    )(keep, received, arrived)
+    )(ids, tokens, out_grad, per_row, *parts, after)
 
 
 def last_sum_kernel(own, r4, r2, r6, after, gate, up, down):
@@ -406,18 +346,25 @@
 
     own, p1, p2, p3, w_own = forward(ids, tokens, out_grad, mine, theirs)
     got = [swap(p, "x", XS, r) for r, p in ((1, p1), (2, p2), (3, p3))]
-    total = reduce_rows(own, got)
+    total = own
+    for g in got:
+        total = total + g.astype(F32)
+    total = total.astype(BF)
     message = deltas(ids, total, swap(total, "zhi", Z_HI, 1), per_row)
     parts = [message] + [swap(message, "x", XS, r) for r in (1, 2, 3)]
 
     weights = lax.all_gather(w_own, "row")
 
-    keep, send = weight_grads(ids, tokens, out_grad, per_row, parts)
-    received = swap(send, "core", CORES, 1)
-    arrived = swap(core_sum(keep, received), "z", Z, 1)
-
-    rows_by_y = lax.all_gather(row_order(ids, parts, keep), "row")
-    own_sum, s4, s2, s6 = pair_sum(keep, received, arrived)
+    keep, send, rows = weight_grads(
+        ids, tokens, out_grad, per_row, parts, weights[0, 0:16, 0:T]
+    )
+    sums = keep.astype(F32) + swap(send, "core", CORES, 1).astype(F32)
+    near, rest = sums[0 : 4 * 3 * T].astype(BF), sums[4 * 3 * T :]
+    sums = rest + swap(near, "z", Z, 1).astype(F32)
+    own_sum, *others = (sums[i * 3 * T : (i + 1) * 3 * T] for i in range(4))
+    s4, s2, s6 = (other.astype(BF) for other in others)
+
+    rows_by_y = lax.all_gather(rows, "row")
     grad_tokens, grad_logits = token_grads(ids, weights, rows_by_y, per_row, s4)
     grad_gate, grad_up, grad_down = last_sum(
         own_sum,

time: 253 us -> 196 us (0.77)
  waiting for transfers between devices: 89.4 us -> 46.3 us
  starting transfers between devices: 92.8 us -> 84.3 us
  Pallas kernels: 32.3 us -> 25.6 us
    all_gather x1, waiting for transfers between devices: 56 us -> 13.2 us  [local(): weights = lax.all_gather(w_own, 'row')]
    ppermute x18, starting transfers between devices: 92.7 us -> 84.2 us  [swap(): return lax.ppermute(value, axis, [(i, i ^ mask) for i in range(size)])]
    pallas_call x4 -> x0, Pallas kernels: 8.5 us -> none  [the longest x1 2.3 us: pair_sum(): pl.pallas_call(pair_sum_kernel, out_shape=[jax.ShapeDtypeStruct((3 * T, T...]
    all_gather x1, waiting for transfers between devices: 0.02 us -> 5.06 us  [local(): rows_by_y = lax.all_gather(rows, 'row')]
    ppermute x18, waiting for transfers between devices: 32.7 us -> 27.9 us  [swap(): return lax.ppermute(value, axis, [(i, i ^ mask) for i in range(size)])]
    unnamed x62 -> x44, local copies, waits for them, and re-layouts: 20 us -> 17.8 us
  transfers between devices with their start and end apart: 20 -> 20, of which waited for: 11 -> 10; matrix products, arithmetic and copies ran while one was open for 0% -> 2% of each run, Pallas kernels for 6% -> 6%
where the time goes in v4:
time: 196 us; the launch traced here: 195 us
  starting transfers between devices  84.3 us (43%)
  waiting for transfers between devices  46.3 us (24%)
  Pallas kernels  25.6 us (13%)
  local copies, waits for them, and re-layouts  19.8 us (10%)
  between operations  15 us (8%)
  other arithmetic  3.71 us (2%)
    ppermute x18, starting transfers between devices, swap(): return lax.ppermute(value, axis, [(i, i ^ mask) for i in range(size)])  84.2 us
    ppermute x18, waiting for transfers between devices, swap(): return lax.ppermute(value, axis, [(i, i ^ mask) for i in range(size)])  27.9 us
    unnamed x44, local copies, waits for them, and re-layouts  17.8 us
    all_gather x1, waiting for transfers between devices, local(): weights = lax.all_gather(w_own, 'row')  13.2 us
    pallas_call x1, Pallas kernels, token_grads(): pl.pallas_call(token_grad_kernel, grid_spec=pltpu.PrefetchScalarGridSpec(...  7.8 us
    pallas_call x1, Pallas kernels, weight_grads(): pl.pallas_call(weight_grad_kernel, grid_spec=pltpu.PrefetchScalarGridSpec...  6.73 us
    all_gather x1, waiting for transfers between devices, local(): rows_by_y = lax.all_gather(rows, 'row')  5.06 us
  transfers between devices with their start and end apart: 20, of which 10 were waited for; matrix products, arithmetic and copies ran while one was open for 2% of the time, Pallas kernels for 6%

profile of v4, /device:TPU:1, one launch (start us, length us, event | category | flops | bytes accessed | tf_op | source)
XLA Modules:
  0.0 194.7 jit_solution(10480258621599258279)
XLA Ops:
  7.8 1.7 own_tiles.1
  9.5 12.3 %collective-permute-start.2 = (bf16[128,384]{1,0:T(8,128)(2,1)}, bf16[128,384]{1,0:T(8,128)(2,1)S(1)}, u32[]{:S(2)}, u32[]{:S(2)}) collective-permute-start(bf16[128,384]{1,0:T(8,128)(2,1)} %own_tiles.1), channel_id=1, source_target_pairs={{0,384},{64,448},{128,256},{192,320},{256,128},{320,192},{384,0},{... | collective-permute-start | bytes 294920 | tf_op jit(solution)/shard_map/ppermute | solution.py:22
  21.8 1.9 collective-permute-start.1
  23.8 2.2 %collective-permute-start = (bf16[128,384]{1,0:T(8,128)(2,1)}, bf16[128,384]{1,0:T(8,128)(2,1)S(1)}, u32[]{:S(2)}, u32[]{:S(2)}) collective-permute-start(bf16[128,384]{1,0:T(8,128)(2,1)} %own_tiles.1), channel_id=1, source_target_pairs={{0,256},{64,320},{128,384},{192,448},{256,0},{320,64},{384,128},{4... | collective-permute-start | bytes 294920 | tf_op jit(solution)/shard_map/ppermute | solution.py:22
  26.0 2.6 %collective-permute-done.1 = bf16[128,384]{1,0:T(8,128)(2,1)S(1)} collective-permute-done((bf16[128,384]{1,0:T(8,128)(2,1)}, bf16[128,384]{1,0:T(8,128)(2,1)S(1)}, u32[]{:S(2)}, u32[]{:S(2)}) %collective-permute-start.1) | collective-permute-done | bytes 98336 | tf_op jit(solution)/shard_map/ppermute | solution.py:22
  28.6 4.6 %collective-permute-done = bf16[128,384]{1,0:T(8,128)(2,1)S(1)} collective-permute-done((bf16[128,384]{1,0:T(8,128)(2,1)}, bf16[128,384]{1,0:T(8,128)(2,1)S(1)}, u32[]{:S(2)}, u32[]{:S(2)}) %collective-permute-start) | collective-permute-done | bytes 98336 | tf_op jit(solution)/shard_map/ppermute | solution.py:22
  33.2 0.9 pad_maximum_fusion.m0
  34.2 8.3 %collective-permute-start.3 = (bf16[512,384]{1,0:T(8,128)(2,1)S(1)}, bf16[512,384]{1,0:T(8,128)(2,1)S(1)}, u32[]{:S(2)}, u32[]{:S(2)}) collective-permute-start(bf16[512,384]{1,0:T(8,128)(2,1)S(1)} %pad_maximum_fusion.m0), channel_id=1, source_target_pairs={{0,64},{64,0},{128,192},{192,128},{256,320},{320,256},{384,448},{4... | collective-permute-start | bytes 1179656 | tf_op jit(solution)/shard_map/ppermute | solution.py:22
  42.5 3.9 %collective-permute-start.4 = (bf16[512,384]{1,0:T(8,128)(2,1)S(1)}, bf16[512,384]{1,0:T(8,128)(2,1)S(1)}, u32[]{:S(2)}, u32[]{:S(2)}) collective-permute-start(bf16[512,384]{1,0:T(8,128)(2,1)S(1)} %pad_maximum_fusion.m0), channel_id=1, source_target_pairs={{0,32},{32,0},{1,33},{33,1},{2,34},{34,2},{3,35},{35,3},{4,36},{36... | collective-permute-start | bytes 1179656 | tf_op jit(solution)/shard_map/ppermute | solution.py:22
  46.4 2.7 %collective-permute-done.3.m1 = bf16[512,384]{1,0:T(8,128)(2,1)S(1)} collective-permute-done((bf16[512,384]{1,0:T(8,128)(2,1)S(1)}, bf16[512,384]{1,0:T(8,128)(2,1)S(1)}, u32[]{:S(2)}, u32[]{:S(2)}) %collective-permute-start.3) | collective-permute-done | bytes 393248 | tf_op jit(solution)/shard_map/ppermute | solution.py:22
  49.1 5.3 %collective-permute-start.5 = (bf16[512,384]{1,0:T(8,128)(2,1)S(1)}, bf16[512,384]{1,0:T(8,128)(2,1)S(1)}, u32[]{:S(2)}, u32[]{:S(2)}) collective-permute-start(bf16[512,384]{1,0:T(8,128)(2,1)S(1)} %collective-permute-done.3.m1), channel_id=1, source_target_pairs={{0,32},{32,0},{1,33},{33,1},{2,34},{34,2},{3,35},{35,3},{4,36},{36... | collective-permute-start | bytes 1179656 | tf_op jit(solution)/shard_map/ppermute | solution.py:22
  54.4 1.3 collective-permute-done.5.t1
  55.7 1.9 copy-done
  57.6 1.9 copy-done.2
  60.2 3.2 %forward.1 = (f32[192,384]{1,0:T(8,128)S(1)}, bf16[192,384]{1,0:T(8,128)(2,1)S(1)}, bf16[192,384]{1,0:T(8,128)(2,1)S(1)}, bf16[192,384]{1,0:T(8,128)(2,1)S(1)}, bf16[2048,256]{1,0:T(8,128)(2,1)S(1)}) custom-call(s32[3]{0:T(128)S(1)} %copy-done.10, bf16[768,2048]{1,0:T(8,128)(2,1)S(1)} %copy-done, bf16[768,2048]{1,0:T(8,128)(2,1)S(1)} %copy-done.2, ...), custom_call_target="tpu_custom_call" | custom-call | flops 1207959552 | bytes 10485760 | tf_op jit(solution)/shard_map/forward/pallas_call | solution.py:138
  63.4 1.0 copy-done.6
  66.4 3.4 %collective-permute-start.6 = (bf16[192,384]{1,0:T(8,128)(2,1)}, bf16[192,384]{1,0:T(8,128)(2,1)S(1)}, u32[]{:S(2)}, u32[]{:S(2)}) collective-permute-start(bf16[192,384]{1,0:T(8,128)(2,1)} %copy-done.16), channel_id=1, source_target_pairs={{0,1},{1,0},{2,3},{3,2},{4,5},{5,4},{6,7},{7,6},{8,9},{9,8},{10,11... | collective-permute-start | bytes 442376 | tf_op jit(solution)/shard_map/ppermute | solution.py:22
  69.8 4.4 %collective-permute-start.7 = (bf16[192,384]{1,0:T(8,128)(2,1)}, bf16[192,384]{1,0:T(8,128)(2,1)S(1)}, u32[]{:S(2)}, u32[]{:S(2)}) collective-permute-start(bf16[192,384]{1,0:T(8,128)(2,1)} %copy-done.15), channel_id=1, source_target_pairs={{0,2},{1,3},{2,0},{3,1},{4,6},{5,7},{6,4},{7,5},{8,10},{9,11},{10,... | collective-permute-start | bytes 442376 | tf_op jit(solution)/shard_map/ppermute | solution.py:22
  74.2 2.1 %collective-permute-start.8 = (bf16[192,384]{1,0:T(8,128)(2,1)}, bf16[192,384]{1,0:T(8,128)(2,1)S(1)}, u32[]{:S(2)}, u32[]{:S(2)}) collective-permute-start(bf16[192,384]{1,0:T(8,128)(2,1)} %copy-done.14), channel_id=1, source_target_pairs={{0,3},{1,2},{2,1},{3,0},{4,7},{5,6},{6,5},{7,4},{8,11},{9,10},{10,... | collective-permute-start | bytes 442376 | tf_op jit(solution)/shard_map/ppermute | solution.py:22
  76.3 3.0 %collective-permute-done.7 = bf16[192,384]{1,0:T(8,128)(2,1)S(1)} collective-permute-done((bf16[192,384]{1,0:T(8,128)(2,1)}, bf16[192,384]{1,0:T(8,128)(2,1)S(1)}, u32[]{:S(2)}, u32[]{:S(2)}) %collective-permute-start.7) | collective-permute-done | bytes 147488 | tf_op jit(solution)/shard_map/ppermute | solution.py:22
  79.3 2.6 %collective-permute-done.8 = bf16[192,384]{1,0:T(8,128)(2,1)S(1)} collective-permute-done((bf16[192,384]{1,0:T(8,128)(2,1)}, bf16[192,384]{1,0:T(8,128)(2,1)S(1)}, u32[]{:S(2)}, u32[]{:S(2)}) %collective-permute-start.8) | collective-permute-done | bytes 147488 | tf_op jit(solution)/shard_map/ppermute | solution.py:22
  81.9 0.7 add_convert_fusion.s_mine
  82.6 11.6 %collective-permute-start.9 = (bf16[192,384]{1,0:T(8,128)(2,1)}, bf16[192,384]{1,0:T(8,128)(2,1)S(1)}, u32[]{:S(2)}, u32[]{:S(2)}) collective-permute-start(bf16[192,384]{1,0:T(8,128)(2,1)} %add_convert_fusion.s_mine), channel_id=1, source_target_pairs={{0,4},{4,0},{1,5},{5,1},{2,6},{6,2},{3,7},{7,3},{8,12},{12,8},{9,1... | collective-permute-start | bytes 442376 | tf_op jit(solution)/shard_map/ppermute | solution.py:22
  95.5 2.3 %rates.1.per_row = f32[768,128]{1,0:T(8,128)} custom-call(f32[48,128]{1,0:T(8,128)} %bitcast.15, s32[1,768]{1,0:T(1,128)} %broadcast_in_dim.3.positions, s32[1]{0:T(128)S(6)} %copy.16.counts), custom_call_target="tpu_custom_call" | custom-call | tf_op jit(solution)/shard_map/rates/pallas_call | solution.py:74
  98.4 2.1 %deltas.1.d0 = bf16[208,384]{1,0:T(8,128)(2,1)} custom-call(s32[3]{0:T(128)} %pad_add_fusion.ids, bf16[192,384]{1,0:T(8,128)(2,1)} %add_convert_fusion.s_mine, bf16[192,384]{1,0:T(8,128)(2,1)} %copy-done.17, f32[768,128]{1,0:T(8,128)} %rates.1.per_row), custom_call_target="tpu_custom_call" | custom-call | tf_op jit(solution)/shard_map/deltas/pallas_call | solution.py:187
  100.5 3.5 %collective-permute-start.12 = (bf16[208,384]{1,0:T(8,128)(2,1)}, bf16[208,384]{1,0:T(8,128)(2,1)S(1)}, u32[]{:S(2)}, u32[]{:S(2)}) collective-permute-start(bf16[208,384]{1,0:T(8,128)(2,1)} %deltas.1.d0), channel_id=1, source_target_pairs={{0,3},{1,2},{2,1},{3,0},{4,7},{5,6},{6,5},{7,4},{8,11},{9,10},{10,... | collective-permute-start | bytes 479240 | tf_op jit(solution)/shard_map/ppermute | solution.py:22
  104.0 3.8 %collective-permute-start.11 = (bf16[208,384]{1,0:T(8,128)(2,1)}, bf16[208,384]{1,0:T(8,128)(2,1)S(1)}, u32[]{:S(2)}, u32[]{:S(2)}) collective-permute-start(bf16[208,384]{1,0:T(8,128)(2,1)} %deltas.1.d0), channel_id=1, source_target_pairs={{0,2},{1,3},{2,0},{3,1},{4,6},{5,7},{6,4},{7,5},{8,10},{9,11},{10,... | collective-permute-start | bytes 479240 | tf_op jit(solution)/shard_map/ppermute | solution.py:22
  107.9 1.9 collective-permute-start.10
  109.8 13.2 %all-gather.5.cloned.1.call-done = bf16[8192,256]{1,0:T(8,128)(2,1)} async-done(((bf16[2048,256]{1,0:T(8,128)(2,1)}), bf16[8192,256]{1,0:T(8,128)(2,1)}) %all-gather.5.cloned.1.call-update) | async-done | bytes 4194320 | tf_op jit(solution)/shard_map/all_gather | solution.py:356
  123.8 1.9 copy-done.3
  125.7 1.0 copy-done.4
  126.7 0.9 copy-done.8
  127.6 6.7 %weight_grads.1 = (bf16[3072,128]{1,0:T(8,128)(2,1)S(1)}, bf16[3072,128]{1,0:T(8,128)(2,1)}, bf16[832,256]{1,0:T(8,128)(2,1)S(1)}) custom-call(s32[3]{0:T(128)S(1)} %copy-done.11, bf16[768,2048]{1,0:T(8,128)(2,1)S(1)} %copy-done.1, bf16[768,2048]{1,0:T(8,128)(2,1)S(1)} %copy-done.3, f32[768,128]{1,0:T(8,128)S(1)} %copy-done.4, ...), custom_call_target="tpu_custom_call" | custom-call | flops 1207959552 | bytes 10485760 | tf_op jit(solution)/shard_map/weight_grads/pallas_call | solution.py:224
  134.3 0.9 copy-done.7
  135.2 0.7 copy-done.9
  135.9 2.6 %collective-permute-start.13 = (bf16[3072,128]{1,0:T(8,128)(2,1)}, bf16[3072,128]{1,0:T(8,128)(2,1)S(1)}, u32[]{:S(2)}, u32[]{:S(2)}) collective-permute-start(bf16[3072,128]{1,0:T(8,128)(2,1)} %get-tuple-element.25), channel_id=1, source_target_pairs={{0,32},{32,0},{1,33},{33,1},{2,34},{34,2},{3,35},{35,3},{4,36},{36... | collective-permute-start | bytes 2359304 | tf_op jit(solution)/shard_map/ppermute | solution.py:22
  138.5 2.1 %collective-permute-done.13 = bf16[3072,128]{1,0:T(8,128)(2,1)S(1)} collective-permute-done((bf16[3072,128]{1,0:T(8,128)(2,1)}, bf16[3072,128]{1,0:T(8,128)(2,1)S(1)}, u32[]{:S(2)}, u32[]{:S(2)}) %collective-permute-start.13) | collective-permute-done | bytes 786464 | tf_op jit(solution)/shard_map/ppermute | solution.py:22
  140.6 1.3 convert_add_fusion
  142.0 3.5 %collective-permute-start.14 = (bf16[1536,128]{1,0:T(8,128)(2,1)S(1)}, bf16[1536,128]{1,0:T(8,128)(2,1)S(1)}, u32[]{:S(2)}, u32[]{:S(2)}) collective-permute-start(bf16[1536,128]{1,0:T(8,128)(2,1)S(1)} %slice.42), channel_id=1, source_target_pairs={{0,64},{64,0},{128,192},{192,128},{256,320},{320,256},{384,448},{4... | collective-permute-start | bytes 1179656 | tf_op jit(solution)/shard_map/ppermute | solution.py:22
  145.5 8.9 %collective-permute-done.14 = bf16[1536,128]{1,0:T(8,128)(2,1)S(1)} collective-permute-done((bf16[1536,128]{1,0:T(8,128)(2,1)S(1)}, bf16[1536,128]{1,0:T(8,128)(2,1)S(1)}, u32[]{:S(2)}, u32[]{:S(2)}) %collective-permute-start.14) | collective-permute-done | bytes 393248 | tf_op jit(solution)/shard_map/ppermute | solution.py:22
  154.5 9.5 %collective-permute-start.17 = (bf16[384,128]{1,0:T(8,128)(2,1)S(1)}, bf16[384,128]{1,0:T(8,128)(2,1)S(1)}, u32[]{:S(2)}, u32[]{:S(2)}) collective-permute-start(bf16[384,128]{1,0:T(8,128)(2,1)S(1)} %get-tuple-element.33), channel_id=1, source_target_pairs={{0,384},{64,448},{128,256},{192,320},{256,128},{320,192},{384,0},{... | collective-permute-start | bytes 294920 | tf_op jit(solution)/shard_map/ppermute | solution.py:22
  164.0 1.9 collective-permute-start.16
  165.9 2.2 %collective-permute-start.15 = (bf16[384,128]{1,0:T(8,128)(2,1)S(1)}, bf16[384,128]{1,0:T(8,128)(2,1)S(1)}, u32[]{:S(2)}, u32[]{:S(2)}) collective-permute-start(bf16[384,128]{1,0:T(8,128)(2,1)S(1)} %get-tuple-element.35.after), channel_id=1, source_target_pairs={{0,256},{64,320},{128,384},{192,448},{256,0},{320,64},{384,128},{4... | collective-permute-start | bytes 294920 | tf_op jit(solution)/shard_map/ppermute | solution.py:22
  168.8 5.1 %all-gather.7.cloned.1.call-done = bf16[3328,256]{1,0:T(8,128)(2,1)} async-done(((bf16[832,256]{1,0:T(8,128)(2,1)}), bf16[3328,256]{1,0:T(8,128)(2,1)}) %all-gather.7.cloned.1.call-update) | async-done | bytes 1703952 | tf_op jit(solution)/shard_map/all_gather | solution.py:367
  173.9 2.2 %copy-done.12 = bf16[8192,256]{1,0:T(8,128)(2,1)S(1)} copy-done((bf16[8192,256]{1,0:T(8,128)(2,1)S(1)}, bf16[8192,256]{1,0:T(8,128)(2,1)}, u32[]{:S(2)}) %copy-start.12) | copy-done | bytes 4194328
  176.1 1.5 copy-done.13
  177.5 7.8 %token_grads.1 = (bf16[768,2048]{1,0:T(8,128)(2,1)}, f32[48,128]{1,0:T(8,128)}) custom-call(s32[3]{0:T(128)S(1)} %copy-done.11, bf16[4,2048,256]{2,1,0:T(8,128)(2,1)S(1)} %bitcast.12, bf16[4,832,256]{2,1,0:T(8,128)(2,1)S(1)} %bitcast.13, f32[768,128]{1,0:T(8,128)S(1)} %copy-done.5, bf16[384,128]{1,0:T(8,128)(2,1)S(1)} %get-tuple-element.35.after), custom_call_target="tpu_custom_call" | custom-call | flops 3221225472 | bytes 12582912 | tf_op jit(solution)/shard_map/token_grads/pallas_call | solution.py:297
  186.0 1.9 last_sum.1
  (55 shorter events, 6.9 us)
Async XLA Ops:
  7.2 115.9 %all-gather.5.cloned.1.call-start = ((), (), s32[]{:S(2)}) async-start(), calls=%async_computation | async-start | bytes 5242880 | tf_op jit(solution)/shard_map/all_gather | solution.py:356
  9.5 16.5 %collective-permute-start.2 = (bf16[128,384]{1,0:T(8,128)(2,1)}, bf16[128,384]{1,0:T(8,128)(2,1)S(1)}, u32[]{:S(2)}, u32[]{:S(2)}) collective-permute-start(bf16[128,384]{1,0:T(8,128)(2,1)} %own_tiles.1), channel_id=1, source_target_pairs={{0,384},{64,448},{128,256},{192,320},{256,128},{320,192},{384,0},{... | collective-permute-start | bytes 294920 | tf_op jit(solution)/shard_map/ppermute | solution.py:22
  21.8 6.8 %collective-permute-start.1 = (bf16[128,384]{1,0:T(8,128)(2,1)}, bf16[128,384]{1,0:T(8,128)(2,1)S(1)}, u32[]{:S(2)}, u32[]{:S(2)}) collective-permute-start(bf16[128,384]{1,0:T(8,128)(2,1)} %own_tiles.1), channel_id=1, source_target_pairs={{0,128},{64,192},{128,0},{192,64},{256,384},{320,448},{384,256},{4... | collective-permute-start | bytes 294920 | tf_op jit(solution)/shard_map/ppermute | solution.py:22
  23.8 9.5 %collective-permute-start = (bf16[128,384]{1,0:T(8,128)(2,1)}, bf16[128,384]{1,0:T(8,128)(2,1)S(1)}, u32[]{:S(2)}, u32[]{:S(2)}) collective-permute-start(bf16[128,384]{1,0:T(8,128)(2,1)} %own_tiles.1), channel_id=1, source_target_pairs={{0,256},{64,320},{128,384},{192,448},{256,0},{320,64},{384,128},{4... | collective-permute-start | bytes 294920 | tf_op jit(solution)/shard_map/ppermute | solution.py:22
  34.2 14.9 %collective-permute-start.3 = (bf16[512,384]{1,0:T(8,128)(2,1)S(1)}, bf16[512,384]{1,0:T(8,128)(2,1)S(1)}, u32[]{:S(2)}, u32[]{:S(2)}) collective-permute-start(bf16[512,384]{1,0:T(8,128)(2,1)S(1)} %pad_maximum_fusion.m0), channel_id=1, source_target_pairs={{0,64},{64,0},{128,192},{192,128},{256,320},{320,256},{384,448},{4... | collective-permute-start | bytes 1179656 | tf_op jit(solution)/shard_map/ppermute | solution.py:22
  42.5 12.0 %collective-permute-start.4 = (bf16[512,384]{1,0:T(8,128)(2,1)S(1)}, bf16[512,384]{1,0:T(8,128)(2,1)S(1)}, u32[]{:S(2)}, u32[]{:S(2)}) collective-permute-start(bf16[512,384]{1,0:T(8,128)(2,1)S(1)} %pad_maximum_fusion.m0), channel_id=1, source_target_pairs={{0,32},{32,0},{1,33},{33,1},{2,34},{34,2},{3,35},{35,3},{4,36},{36... | collective-permute-start | bytes 1179656 | tf_op jit(solution)/shard_map/ppermute | solution.py:22
  49.1 6.6 %collective-permute-start.5 = (bf16[512,384]{1,0:T(8,128)(2,1)S(1)}, bf16[512,384]{1,0:T(8,128)(2,1)S(1)}, u32[]{:S(2)}, u32[]{:S(2)}) collective-permute-start(bf16[512,384]{1,0:T(8,128)(2,1)S(1)} %collective-permute-done.3.m1), channel_id=1, source_target_pairs={{0,32},{32,0},{1,33},{33,1},{2,34},{34,2},{3,35},{35,3},{4,36},{36... | collective-permute-start | bytes 1179656 | tf_op jit(solution)/shard_map/ppermute | solution.py:22
  55.7 1.9 copy-start
  57.6 1.9 copy-start.2
  59.5 0.7 copy-start.10
  60.2 34.7 %copy-start.21 = (s32[768]{0:T(1024)S(1)}, s32[768]{0:T(1024)}, u32[]{:S(2)}) copy-start(s32[768]{0:T(1024)} %param.15) | copy-start | bytes 9220
  63.3 1.0 copy-start.6
  64.3 0.7 copy-start.14
  65.0 0.7 copy-start.15
  65.7 0.7 copy-start.16
  66.3 57.4 %copy-start.1 = (bf16[768,2048]{1,0:T(8,128)(2,1)S(1)}, bf16[768,2048]{1,0:T(8,128)(2,1)}, u32[]{:S(2)}) copy-start(bf16[768,2048]{1,0:T(8,128)(2,1)} %tokens.3) | copy-start | bytes 9437188
  66.3 57.4 %copy-start.11 = (s32[3]{0:T(128)S(1)}, s32[3]{0:T(128)}, u32[]{:S(2)}) copy-start(s32[3]{0:T(128)} %pad_add_fusion.ids) | copy-start | bytes 40
  66.4 107.5 %all-gather.7.cloned.1.call-start = ((), (), s32[]{:S(2)}) async-start(), calls=%async_computation.1 | async-start | bytes 2129920 | tf_op jit(solution)/shard_map/all_gather | solution.py:367
  66.4 9.9 %collective-permute-start.6 = (bf16[192,384]{1,0:T(8,128)(2,1)}, bf16[192,384]{1,0:T(8,128)(2,1)S(1)}, u32[]{:S(2)}, u32[]{:S(2)}) collective-permute-start(bf16[192,384]{1,0:T(8,128)(2,1)} %copy-done.16), channel_id=1, source_target_pairs={{0,1},{1,0},{2,3},{3,2},{4,5},{5,4},{6,7},{7,6},{8,9},{9,8},{10,11... | collective-permute-start | bytes 442376 | tf_op jit(solution)/shard_map/ppermute | solution.py:22
  69.8 9.5 %collective-permute-start.7 = (bf16[192,384]{1,0:T(8,128)(2,1)}, bf16[192,384]{1,0:T(8,128)(2,1)S(1)}, u32[]{:S(2)}, u32[]{:S(2)}) collective-permute-start(bf16[192,384]{1,0:T(8,128)(2,1)} %copy-done.15), channel_id=1, source_target_pairs={{0,2},{1,3},{2,0},{3,1},{4,6},{5,7},{6,4},{7,5},{8,10},{9,11},{10,... | collective-permute-start | bytes 442376 | tf_op jit(solution)/shard_map/ppermute | solution.py:22
  74.2 7.7 %collective-permute-start.8 = (bf16[192,384]{1,0:T(8,128)(2,1)}, bf16[192,384]{1,0:T(8,128)(2,1)S(1)}, u32[]{:S(2)}, u32[]{:S(2)}) collective-permute-start(bf16[192,384]{1,0:T(8,128)(2,1)} %copy-done.14), channel_id=1, source_target_pairs={{0,3},{1,2},{2,1},{3,0},{4,7},{5,6},{6,5},{7,4},{8,11},{9,10},{10,... | collective-permute-start | bytes 442376 | tf_op jit(solution)/shard_map/ppermute | solution.py:22
  82.6 15.1 %collective-permute-start.9 = (bf16[192,384]{1,0:T(8,128)(2,1)}, bf16[192,384]{1,0:T(8,128)(2,1)S(1)}, u32[]{:S(2)}, u32[]{:S(2)}) collective-permute-start(bf16[192,384]{1,0:T(8,128)(2,1)} %add_convert_fusion.s_mine), channel_id=1, source_target_pairs={{0,4},{4,0},{1,5},{5,1},{2,6},{6,2},{3,7},{7,3},{8,12},{12,8},{9,1... | collective-permute-start | bytes 442376 | tf_op jit(solution)/shard_map/ppermute | solution.py:22
  97.8 0.7 copy-start.17
  100.5 23.2 %collective-permute-start.12 = (bf16[208,384]{1,0:T(8,128)(2,1)}, bf16[208,384]{1,0:T(8,128)(2,1)S(1)}, u32[]{:S(2)}, u32[]{:S(2)}) collective-permute-start(bf16[208,384]{1,0:T(8,128)(2,1)} %deltas.1.d0), channel_id=1, source_target_pairs={{0,3},{1,2},{2,1},{3,0},{4,7},{5,6},{6,5},{7,4},{8,11},{9,10},{10,... | collective-permute-start | bytes 479240 | tf_op jit(solution)/shard_map/ppermute | solution.py:22
  104.0 19.7 %collective-permute-start.11 = (bf16[208,384]{1,0:T(8,128)(2,1)}, bf16[208,384]{1,0:T(8,128)(2,1)S(1)}, u32[]{:S(2)}, u32[]{:S(2)}) collective-permute-start(bf16[208,384]{1,0:T(8,128)(2,1)} %deltas.1.d0), channel_id=1, source_target_pairs={{0,2},{1,3},{2,0},{3,1},{4,6},{5,7},{6,4},{7,5},{8,10},{9,11},{10,... | collective-permute-start | bytes 479240 | tf_op jit(solution)/shard_map/ppermute | solution.py:22
  107.9 15.9 %collective-permute-start.10 = (bf16[208,384]{1,0:T(8,128)(2,1)}, bf16[208,384]{1,0:T(8,128)(2,1)}, u32[]{:S(2)}, u32[]{:S(2)}) collective-permute-start(bf16[208,384]{1,0:T(8,128)(2,1)} %deltas.1.d0), channel_id=1, source_target_pairs={{0,1},{1,0},{2,3},{3,2},{4,5},{5,4},{6,7},{7,6},{8,9},{9,8},{10,11... | collective-permute-start | bytes 479240 | tf_op jit(solution)/shard_map/ppermute | solution.py:22
  123.8 1.9 copy-start.3
  125.7 1.0 copy-start.4
  126.7 0.9 copy-start.8
  134.3 0.9 copy-start.7
  135.2 0.7 copy-start.9
  135.9 4.7 %collective-permute-start.13 = (bf16[3072,128]{1,0:T(8,128)(2,1)}, bf16[3072,128]{1,0:T(8,128)(2,1)S(1)}, u32[]{:S(2)}, u32[]{:S(2)}) collective-permute-start(bf16[3072,128]{1,0:T(8,128)(2,1)} %get-tuple-element.25), channel_id=1, source_target_pairs={{0,32},{32,0},{1,33},{33,1},{2,34},{34,2},{3,35},{35,3},{4,36},{36... | collective-permute-start | bytes 2359304 | tf_op jit(solution)/shard_map/ppermute | solution.py:22
  142.0 31.9 %copy-start.5 = (f32[768,128]{1,0:T(8,128)S(1)}, f32[768,128]{1,0:T(8,128)}, u32[]{:S(2)}) copy-start(f32[768,128]{1,0:T(8,128)} %rates.1.per_row) | copy-start | bytes 1179652
  142.0 12.4 %collective-permute-start.14 = (bf16[1536,128]{1,0:T(8,128)(2,1)S(1)}, bf16[1536,128]{1,0:T(8,128)(2,1)S(1)}, u32[]{:S(2)}, u32[]{:S(2)}) collective-permute-start(bf16[1536,128]{1,0:T(8,128)(2,1)S(1)} %slice.42), channel_id=1, source_target_pairs={{0,64},{64,0},{128,192},{192,128},{256,320},{320,256},{384,448},{4... | collective-permute-start | bytes 1179656 | tf_op jit(solution)/shard_map/ppermute | solution.py:22
  154.5 30.8 %collective-permute-start.17 = (bf16[384,128]{1,0:T(8,128)(2,1)S(1)}, bf16[384,128]{1,0:T(8,128)(2,1)S(1)}, u32[]{:S(2)}, u32[]{:S(2)}) collective-permute-start(bf16[384,128]{1,0:T(8,128)(2,1)S(1)} %get-tuple-element.33), channel_id=1, source_target_pairs={{0,384},{64,448},{128,256},{192,320},{256,128},{320,192},{384,0},{... | collective-permute-start | bytes 294920 | tf_op jit(solution)/shard_map/ppermute | solution.py:22
  164.0 21.3 %collective-permute-start.16 = (bf16[384,128]{1,0:T(8,128)(2,1)S(1)}, bf16[384,128]{1,0:T(8,128)(2,1)S(1)}, u32[]{:S(2)}, u32[]{:S(2)}) collective-permute-start(bf16[384,128]{1,0:T(8,128)(2,1)S(1)} %get-tuple-element.34), channel_id=1, source_target_pairs={{0,128},{64,192},{128,0},{192,64},{256,384},{320,448},{384,256},{4... | collective-permute-start | bytes 294920 | tf_op jit(solution)/shard_map/ppermute | solution.py:22
  165.9 19.4 %collective-permute-start.15 = (bf16[384,128]{1,0:T(8,128)(2,1)S(1)}, bf16[384,128]{1,0:T(8,128)(2,1)S(1)}, u32[]{:S(2)}, u32[]{:S(2)}) collective-permute-start(bf16[384,128]{1,0:T(8,128)(2,1)S(1)} %get-tuple-element.35.after), channel_id=1, source_target_pairs={{0,256},{64,320},{128,384},{192,448},{256,0},{320,64},{384,128},{4... | collective-permute-start | bytes 294920 | tf_op jit(solution)/shard_map/ppermute | solution.py:22
  173.9 2.2 %copy-start.12 = (bf16[8192,256]{1,0:T(8,128)(2,1)S(1)}, bf16[8192,256]{1,0:T(8,128)(2,1)}, u32[]{:S(2)}) copy-start(bf16[8192,256]{1,0:T(8,128)(2,1)} %all-gather.5.cloned.1.call-done) | copy-start | bytes 12582916
  176.1 1.5 copy-start.13
  185.3 0.6 copy-start.18
  185.3 0.7 copy-start.19
  185.3 0.7 copy-start.20
Sparse Core Ops, SparseCore 0:
  66.5 56.5 all-gather.4
  138.7 35.1 all-gather.6

commit v5 on v3

--- a/solution.py
+++ b/solution.py
@@ -13,6 +13,7 @@
 SEQ = 6144
 D = 2048
 RB = CAP // XS
+PAD = 192
 MSG = RB + 16
 AXES = ("z", "core", "row", "zhi", "x")
 NT = (((1,), (1,)), ((), ()))
@@ -33,10 +34,8 @@
     return hi, mid, (rest - mid.astype(F32)).astype(BF)
 
 
-def params(mib=44):
-    return pltpu.CompilerParams(
-        dimension_semantics=("arbitrary",), vmem_limit_bytes=mib * 1024 * 1024
-    )
+def params(mib=20):
+    return pltpu.CompilerParams(vmem_limit_bytes=mib * 1024 * 1024)
 
 
 def work(flops, mib):
@@ -47,6 +46,10 @@
 SMEM = pl.BlockSpec(memory_space=pltpu.SMEM)
 ANY = pl.BlockSpec(memory_space=pl.ANY)
 HBM = pl.BlockSpec(memory_space=pltpu.HBM)
+
+
+def in_hbm(*arrays):
+    return tuple(pltpu.with_memory_space_constraint(array, pltpu.HBM) for array in arrays)
 
 
 def turn(row):
@@ -76,6 +79,7 @@
         out_shape=jax.ShapeDtypeStruct((CAP, T), F32),
         in_specs=[VMEM, VMEM, SMEM],
         out_specs=VMEM,
+        compiler_params=params(8),
         name="rates",
     )(logits, positions, counts)
 
@@ -97,11 +101,51 @@
         out_shape=jax.ShapeDtypeStruct((T, 3 * T), BF),
         in_specs=[SMEM] + [VMEM] * 6,
         out_specs=VMEM,
+        compiler_params=params(8),
         name="own_tiles",
-    )(ids, gate_scales, up_scales, down_scales, gate, up, down)
-
-
-def forward_kernel(ids, tokens, out_grad, m0, m1, t0, t1, own, p1, p2, p3, w_out, w_down):
+    )(ids, *in_hbm(gate_scales, up_scales, down_scales, gate, up, down))
+
+
+def load_kernel(tokens, out_grad, tokens_out, out_grad_out, sems):
+    copies = (
+        pltpu.make_async_copy(tokens, tokens_out, sems.at[0]),
+        pltpu.make_async_copy(out_grad, out_grad_out, sems.at[1]),
+    )
+    for copy in copies:
+        copy.start()
+    for copy in copies:
+        copy.wait()
+
+
+def load(tokens, out_grad):
+    return pl.pallas_call(
+        load_kernel,
+        out_shape=[pltpu.VMEM((CAP, D), BF)] * 2,
+        in_specs=[ANY] * 2,
+        out_specs=[ANY] * 2,
+        scratch_shapes=[pltpu.SemaphoreType.DMA((2,))],
+        compiler_params=params(1),
+        name="load",
+    )(*in_hbm(tokens, out_grad))
+
+
+def join_kernel(a, b, c, d, tokens, out_grad, out):
+    for i, ref in enumerate((a, b, c, d)):
+        out[i * T : (i + 1) * T, :] = ref[...]
+
+
+def join(blocks, tokens, out_grad):
+    return pl.pallas_call(
+        join_kernel,
+        out_shape=jax.ShapeDtypeStruct((4 * T, 3 * T), BF),
+        in_specs=[VMEM] * 4 + [ANY] * 2,
+        out_specs=VMEM,
+        compiler_params=params(8),
+        name="join",
+    )(*blocks, tokens, out_grad)
+
+
+def forward_kernel(ids, tokens, out_grad, m0, m1, t0, t1, own, p1, p2, p3, w_both, w_down):
     step = pl.program_id(0)
     z, core = ids[0], ids[1]
 
@@ -112,10 +156,10 @@
             for pair, side in (((m0, m1), core), ((t0, t1), 1 - core)):
                 ref, j = pair[i // 4], i % 4
                 rows = pl.ds(pl.multiple_of(base + side * T, T), T)
-                w_out[rows, :] = ref[j * T : (j + 1) * T, 0 : 2 * T]
+                w_both[rows, :] = ref[j * T : (j + 1) * T, 0 : 2 * T]
                 w_down[rows, :] = ref[j * T : (j + 1) * T, 2 * T : 3 * T]
 
-    gate_up = jnp.dot(tokens[...], w_out[...], preferred_element_type=F32)
+    gate_up = jnp.dot(tokens[...], w_both[...], preferred_element_type=F32)
     back = jnp.dot(out_grad[...], w_down[...], preferred_element_type=F32)
 
     @pl.when(step == 0)
@@ -134,7 +178,7 @@
 def forward(ids, tokens, out_grad, mine, theirs):
     whole = lambda *shape: pl.BlockSpec(shape, lambda r, ids: (0,) * len(shape))
     rows = pl.BlockSpec((RB, D), lambda r, ids: (ids[2] ^ r, 0))
-    part = jax.ShapeDtypeStruct((RB, 3 * T), BF)
+    part = pltpu.HBM((RB, 3 * T), BF)
     return pl.pallas_call(
         forward_kernel,
         grid_spec=pltpu.PrefetchScalarGridSpec(
@@ -149,28 +193,12 @@
             part,
             part,
             part,
-            jax.ShapeDtypeStruct((D, 2 * T), BF),
+            pltpu.HBM((D, 2 * T), BF),
         ],
         compiler_params=params(),
         cost_estimate=work(2 * CAP * D * 3 * T, 10),
         name="forward",
     )(ids, tokens, out_grad, *mine, *theirs)
-
-
-def reduce_kernel(own, g1, g2, g3, total):
-    total[...] = (
-        own[...] + g1[...].astype(F32) + g2[...].astype(F32) + g3[...].astype(F32)
-    ).astype(BF)
-
-
-def reduce_rows(own, got):
-    return pl.pallas_call(
-        reduce_kernel,
-        out_shape=jax.ShapeDtypeStruct((RB, 3 * T), BF),
-        in_specs=[VMEM] * 4,
-        out_specs=VMEM,
-        name="reduce_rows",
-    )(own, *got)
 
 
 def delta_kernel(ids, s_mine, s_theirs, per_row, out):
@@ -205,11 +233,14 @@
         out_shape=jax.ShapeDtypeStruct((MSG, 3 * T), BF),
         in_specs=[SMEM] + [VMEM] * 3,
         out_specs=VMEM,
+        compiler_params=params(8),
         name="deltas",
     )(ids, s_mine, s_theirs, per_row)
 
 
-def weight_grad_kernel(ids, tokens, out_grad, per_row, d0, d1, d2, d3, keep, send, flat, turned):
+def weight_grad_kernel(
+    ids, tokens, out_grad, per_row, d0, d1, d2, d3, keep, send, flat, turned
+):
     step = pl.program_id(0)
     core, x = ids[1], ids[2]
 
@@ -242,34 +273,22 @@
             out_specs=[block, block],
             scratch_shapes=[pltpu.VMEM((CAP, 3 * T), BF), pltpu.VMEM((3 * T, CAP), BF)],
         ),
-        out_shape=[jax.ShapeDtypeStruct((Z * 3 * T, T), BF)] * 2,
+        out_shape=[
+            jax.ShapeDtypeStruct((Z * 3 * T, T), BF),
+            jax.ShapeDtypeStruct((Z * 3 * T, T), BF),
+        ],
         compiler_params=params(),
         cost_estimate=work(2 * CAP * D * 3 * T, 10),
         name="weight_grads",
     )(ids, tokens, out_grad, per_row, *parts)
 
 
-def core_sum_kernel(keep, received, send):
-    rows = slice(0, 4 * 3 * T)
-    send[...] = (keep[rows, :].astype(F32) + received[rows, :].astype(F32)).astype(BF)
-
-
-def core_sum(keep, received):
-    return pl.pallas_call(
-        core_sum_kernel,
-        out_shape=jax.ShapeDtypeStruct((4 * 3 * T, T), BF),
-        in_specs=[VMEM] * 2,
-        out_specs=VMEM,
-        name="core_sum",
-    )(keep, received)
-
-
-def rows_kernel(ids, d0, d1, d2, d3, after, rows_out):
+def rows_kernel(ids, d0, d1, d2, d3, after, out):
     x = ids[2]
     for r, ref in enumerate((d0, d1, d2, d3)):
         rows = pl.ds(pl.multiple_of((x ^ r) * RB, RB), RB)
-        rows_out[rows, :] = ref[0:RB, 0 : 2 * T]
-        rows_out[CAP + 16 * r : CAP + 16 * (r + 1), :] = ref[RB:MSG, 0 : 2 * T]
+        out[rows, :] = ref[0:RB, 0 : 2 * T]
+        out[CAP + 16 * r : CAP + 16 * (r + 1), :] = ref[RB:MSG, 0 : 2 * T]
 
 
 def row_order(ids, parts, after):
@@ -278,8 +297,26 @@
         out_shape=jax.ShapeDtypeStruct((CAP + XS * 16, 2 * T), BF),
         in_specs=[SMEM] + [VMEM] * 4 + [ANY],
         out_specs=VMEM,
+        compiler_params=params(8),
         name="row_order",
     )(ids, *parts, after)
+
+
+def core_sum_kernel(keep, received, send):
+    rows = slice(0, 4 * 3 * T)
+    send[rows, :] = (keep[rows, :].astype(F32) + received[rows, :].astype(F32)).astype(BF)
+    send[4 * 3 * T :, :] = jnp.zeros((PAD, T), BF)
+
+
+def core_sum(keep, received):
+    return pl.pallas_call(
+        core_sum_kernel,
+        out_shape=jax.ShapeDtypeStruct((4 * 3 * T + PAD, T), BF),
+        in_specs=[VMEM] * 2,
+        out_specs=VMEM,
+        compiler_params=params(8),
+        name="core_sum",
+    )(keep, received)
 
 
 def pair_sum_kernel(keep, received, arrived, own, s4, s2, s6):
@@ -297,6 +334,7 @@
         out_shape=[jax.ShapeDtypeStruct((3 * T, T), F32), part, part, part],
         in_specs=[VMEM] * 3,
         out_specs=[VMEM] * 4,
+        compiler_params=params(8),
         name="pair_sum",
     )(keep, received, arrived)
 
@@ -314,26 +352,30 @@
         out_shape=[jax.ShapeDtypeStruct((T, T), F32)] * 3,
         in_specs=[VMEM] * 4 + [ANY],
         out_specs=[VMEM] * 3,
+        compiler_params=params(8),
         name="last_sum",
-    )(own, r4, r2, r6, after)
+    )(own, r4, r2, r6, *in_hbm(after))
 
 
 def token_grad_kernel(
-    ids, weights, rows_by_y, per_row, after, out, logits_out, router
+    ids, weights, y0, y1, y2, y3, per_row, after, out, logits_out, router, flat, w
 ):
     step = pl.program_id(0)
-    x = ids[2]
+    x, y = ids[2], ids[3]
+    rows_by_y = (y0, y1, y2, y3)
 
     @pl.when(step == 0)
     def _():
+        for j in range(ROWS):
+            flat[:, j * 2 * T : (j + 1) * 2 * T] = rows_by_y[j][0:CAP, :]
         for r in range(XS):
-            rows = slice(CAP + 16 * r, CAP + 16 * (r + 1))
+            place = pl.ds(pl.multiple_of((x ^ r) * RB, RB), RB)
             terms = []
             for j in range(ROWS):
-                pieces = rows_by_y[j, rows, :].astype(F32)
+                pieces = rows_by_y[j][CAP + 16 * r : CAP + 16 * (r + 1), :].astype(F32)
                 terms.append(pieces[0:1] + pieces[1:2] + pieces[2:3])
             total = (terms[0] + terms[1]) + (terms[2] + terms[3])
-            router[pl.ds(pl.multiple_of((x ^ r) * RB, RB), RB), :] = turn(total)[0:RB]
+            router[place, :] = turn(total)[0:RB]
         value = router[...] * per_row[:, 1:2]
         at = per_row[:, 2:3].astype(jnp.int32)
         lanes = lax.broadcasted_iota(jnp.int32, (CAP, T), 1)
@@ -344,12 +386,9 @@
             total = total + jnp.dot(upper, piece, preferred_element_type=F32)
         logits_out[...] = total[0 : SEQ // T, :]
 
-    total = jnp.zeros((CAP, 2 * T), F32)
     for j in range(ROWS):
-        total += lax.dot_general(
-            rows_by_y[j, 0:CAP, :], weights[j], NT, preferred_element_type=F32
-        )
-    out[...] = total.astype(BF)
+        w[:, j * 2 * T : (j + 1) * 2 * T] = weights[y ^ j]
+    out[...] = lax.dot_general(flat[...], w[...], NT, preferred_element_type=F32).astype(BF)
 
 
 def token_grads(ids, weights, rows_by_y, per_row, after):
@@ -361,15 +400,18 @@
             grid=(Z,),
             in_specs=[
                 pl.BlockSpec((ROWS, 2 * T, 2 * T), lambda i, ids: (0, i, 0)),
-                whole(ROWS, CAP + XS * 16, 2 * T),
-                whole(CAP, T),
-                ANY,
-            ],
+            ]
+            + [whole(CAP + XS * 16, 2 * T)] * 4
+            + [whole(CAP, T), ANY],
             out_specs=[
                 pl.BlockSpec((CAP, 2 * T), lambda i, ids: (0, i)),
                 whole(SEQ // T, T),
             ],
-            scratch_shapes=[pltpu.VMEM((CAP, 1), F32)],
+            scratch_shapes=[
+                pltpu.VMEM((CAP, 1), F32),
+                pltpu.VMEM((CAP, 8 * T), BF),
+                pltpu.VMEM((2 * T, 8 * T), BF),
+            ],
         ),
         out_shape=[
             jax.ShapeDtypeStruct((CAP, D), BF),
@@ -378,7 +420,7 @@
         compiler_params=params(),
         cost_estimate=work(2 * CAP * D * 8 * T, 12),
         name="token_grads",
-    )(ids, weights, rows_by_y, per_row, after)
+    )(ids, weights, *rows_by_y, per_row, after)
 
 
 def local(
@@ -394,19 +436,22 @@
     up_scales,
     down_scales,
 ):
-    z, core, x = lax.axis_index("z"), lax.axis_index("core"), lax.axis_index("x")
-    ids = jnp.stack([z, core, x]).astype(jnp.int32)
+    ids = jnp.stack([lax.axis_index(axis) for axis in ("z", "core", "x", "row")]).astype(jnp.int32)
 
     scales = (gate_scales.T, up_scales.T, down_scales)
     held = own_tiles(ids, *scales, gate_values, up_values, down_values)
-    held = jnp.concatenate([held] + [swap(held, "z", Z, mask) for mask in (4, 2, 6)], axis=0)
+    tokens, out_grad = load(tokens, out_grad)
+    held = join([held] + [swap(held, "z", Z, mask) for mask in (4, 2, 6)], tokens, out_grad)
     mine = (held, swap(held, "z", Z, 1))
     theirs = tuple(swap(h, "core", CORES, 1) for h in mine)
     per_row = rates(router_logits.reshape(SEQ // T, T), routed_positions[None, :], routed_counts)
 
     own, p1, p2, p3, w_own = forward(ids, tokens, out_grad, mine, theirs)
     got = [swap(p, "x", XS, r) for r, p in ((1, p1), (2, p2), (3, p3))]
-    total = reduce_rows(own, got)
+    total = own
+    for g in got:
+        total = total + g.astype(F32)
+    total = total.astype(BF)
     message = deltas(ids, total, swap(total, "zhi", Z_HI, 1), per_row)
     parts = [message] + [swap(message, "x", XS, r) for r in (1, 2, 3)]
 
@@ -414,11 +459,15 @@
 
     keep, send = weight_grads(ids, tokens, out_grad, per_row, parts)
     received = swap(send, "core", CORES, 1)
-    arrived = swap(core_sum(keep, received), "z", Z, 1)
-
-    rows_by_y = lax.all_gather(row_order(ids, parts, keep), "row")
+    sent = core_sum(keep, received)
+    arrived = swap(sent, "z", Z, 1)
+
+    rows = row_order(ids, parts, sent)
+    y1, y2, y3 = (swap(rows, "row", ROWS, r) for r in (1, 2, 3))
     own_sum, s4, s2, s6 = pair_sum(keep, received, arrived)
-    grad_tokens, grad_logits = token_grads(ids, weights, rows_by_y, per_row, s4)
+    grad_tokens, grad_logits = token_grads(
+        ids, weights, (rows, y1, y2, y3), per_row, s4
+    )
     grad_gate, grad_up, grad_down = last_sum(
         own_sum,
         swap(s4, "z", Z, 4),

time: 253 us -> 176 us (0.70)
  waiting for transfers between devices: 89.4 us -> 26.8 us
  local copies, waits for them, and re-layouts: 20.6 us -> 4.87 us
  starting transfers between devices: 92.8 us -> 102 us
  Pallas kernels: 32.3 us -> 24.3 us
    all_gather x1, waiting for transfers between devices: 56 us -> 0.01 us  [local(): weights = lax.all_gather(w_own, 'row')]
    unnamed x62 -> x10, local copies, waits for them, and re-layouts: 20 us -> 4.87 us
    ppermute x18 -> x21, starting transfers between devices: 92.7 us -> 101 us  [swap(): return lax.ppermute(value, axis, [(i, i ^ mask) for i in range(size)])]
    ppermute x18 -> x21, waiting for transfers between devices: 32.7 us -> 26.8 us  [swap(): return lax.ppermute(value, axis, [(i, i ^ mask) for i in range(size)])]
  transfers between devices with their start and end apart: 20 -> 22, of which waited for: 11 -> 10; matrix products, arithmetic and copies ran while one was open for 0% -> 0% of each run, Pallas kernels for 6% -> 10%
where the time goes in v5:
time: 176 us; the launch traced here: 173 us
  starting transfers between devices  102 us (58%)
  waiting for transfers between devices  26.8 us (15%)
  Pallas kernels  24.3 us (14%)
  between operations  15 us (9%)
  local copies, waits for them, and re-layouts  4.87 us (3%)
    ppermute x21, starting transfers between devices, swap(): return lax.ppermute(value, axis, [(i, i ^ mask) for i in range(size)])  101 us
    ppermute x21, waiting for transfers between devices, swap(): return lax.ppermute(value, axis, [(i, i ^ mask) for i in range(size)])  26.8 us
    pallas_call x1, Pallas kernels, token_grads(): pl.pallas_call(token_grad_kernel, grid_spec=pltpu.PrefetchScalarGridSpec(...  7.97 us
    unnamed x10, local copies, waits for them, and re-layouts  4.87 us
    pallas_call x1, Pallas kernels, weight_grads(): pl.pallas_call(weight_grad_kernel, grid_spec=pltpu.PrefetchScalarGridSpec...  4.87 us
    pallas_call x1, Pallas kernels, forward(): pl.pallas_call(forward_kernel, grid_spec=pltpu.PrefetchScalarGridSpec(num...  4.36 us
  transfers between devices with their start and end apart: 22, of which 10 were waited for; matrix products, arithmetic and copies ran while one was open for 0% of the time, Pallas kernels for 10%

profile of v5, /device:TPU:1, one launch (start us, length us, event | category | flops | bytes accessed | tf_op | source)
XLA Modules:
  0.0 172.7 jit_solution(13723030845743618905)
XLA Ops:
  7.2 0.0 all-gather.3.cloned.1.call-start
  7.2 0.1 pad_add_fusion.ids
  7.3 1.0 own_tiles.1.a
  8.3 9.6 %collective-permute-start = (bf16[128,384]{1,0:T(8,128)(2,1)S(1)}, bf16[128,384]{1,0:T(8,128)(2,1)S(1)}, u32[]{:S(2)}, u32[]{:S(2)}) collective-permute-start(bf16[128,384]{1,0:T(8,128)(2,1)S(1)} %own_tiles.1.a), channel_id=1, source_target_pairs={{0,256},{64,320},{128,384},{192,448},{256,0},{320,64},{384,128},{4... | collective-permute-start | bytes 294920 | tf_op jit(solution)/shard_map/ppermute | solution.py:23
  18.0 4.9 %collective-permute-start.1 = (bf16[128,384]{1,0:T(8,128)(2,1)S(1)}, bf16[128,384]{1,0:T(8,128)(2,1)S(1)}, u32[]{:S(2)}, u32[]{:S(2)}) collective-permute-start(bf16[128,384]{1,0:T(8,128)(2,1)S(1)} %own_tiles.1.a), channel_id=1, source_target_pairs={{0,128},{64,192},{128,0},{192,64},{256,384},{320,448},{384,256},{4... | collective-permute-start | bytes 294920 | tf_op jit(solution)/shard_map/ppermute | solution.py:23
  22.9 1.9 %collective-permute-start.2 = (bf16[128,384]{1,0:T(8,128)(2,1)S(1)}, bf16[128,384]{1,0:T(8,128)(2,1)S(1)}, u32[]{:S(2)}, u32[]{:S(2)}) collective-permute-start(bf16[128,384]{1,0:T(8,128)(2,1)S(1)} %own_tiles.1.a), channel_id=1, source_target_pairs={{0,384},{64,448},{128,256},{192,320},{256,128},{320,192},{384,0},{... | collective-permute-start | bytes 294920 | tf_op jit(solution)/shard_map/ppermute | solution.py:23
  24.8 2.9 %load.1 = (bf16[768,2048]{1,0:T(8,128)(2,1)S(1)}, bf16[768,2048]{1,0:T(8,128)(2,1)S(1)}) custom-call(bf16[768,2048]{1,0:T(8,128)(2,1)} %tokens.1, bf16[768,2048]{1,0:T(8,128)(2,1)} %out_grad.1), custom_call_target="tpu_custom_call" | custom-call | tf_op jit(solution)/shard_map/load/pallas_call | solution.py:121
  27.7 6.2 %collective-permute-done.2.d = bf16[128,384]{1,0:T(8,128)(2,1)S(1)} collective-permute-done((bf16[128,384]{1,0:T(8,128)(2,1)S(1)}, bf16[128,384]{1,0:T(8,128)(2,1)S(1)}, u32[]{:S(2)}, u32[]{:S(2)}) %collective-permute-start.2) | collective-permute-done | bytes 98336 | tf_op jit(solution)/shard_map/ppermute | solution.py:23
  34.0 3.6 %collective-permute-start.3 = (bf16[512,384]{1,0:T(8,128)(2,1)S(1)}, bf16[512,384]{1,0:T(8,128)(2,1)S(1)}, u32[]{:S(2)}, u32[]{:S(2)}) collective-permute-start(bf16[512,384]{1,0:T(8,128)(2,1)S(1)} %join.1.m0), channel_id=1, source_target_pairs={{0,64},{64,0},{128,192},{192,128},{256,320},{320,256},{384,448},{4... | collective-permute-start | bytes 1179656 | tf_op jit(solution)/shard_map/ppermute | solution.py:23
  37.6 4.6 %collective-permute-start.4 = (bf16[512,384]{1,0:T(8,128)(2,1)S(1)}, bf16[512,384]{1,0:T(8,128)(2,1)S(1)}, u32[]{:S(2)}, u32[]{:S(2)}) collective-permute-start(bf16[512,384]{1,0:T(8,128)(2,1)S(1)} %join.1.m0), channel_id=1, source_target_pairs={{0,32},{32,0},{1,33},{33,1},{2,34},{34,2},{3,35},{35,3},{4,36},{36... | collective-permute-start | bytes 1179656 | tf_op jit(solution)/shard_map/ppermute | solution.py:23
  42.2 1.4 collective-permute-done.3.m1
  43.6 6.1 %collective-permute-start.5 = (bf16[512,384]{1,0:T(8,128)(2,1)S(1)}, bf16[512,384]{1,0:T(8,128)(2,1)S(1)}, u32[]{:S(2)}, u32[]{:S(2)}) collective-permute-start(bf16[512,384]{1,0:T(8,128)(2,1)S(1)} %collective-permute-done.3.m1), channel_id=1, source_target_pairs={{0,32},{32,0},{1,33},{33,1},{2,34},{34,2},{3,35},{35,3},{4,36},{36... | collective-permute-start | bytes 1179656 | tf_op jit(solution)/shard_map/ppermute | solution.py:23
  49.7 1.3 collective-permute-done.5.t1
  51.1 4.4 %forward.1 = (f32[192,384]{1,0:T(8,128)S(1)}, bf16[192,384]{1,0:T(8,128)(2,1)}, bf16[192,384]{1,0:T(8,128)(2,1)}, bf16[192,384]{1,0:T(8,128)(2,1)}, bf16[2048,256]{1,0:T(8,128)(2,1)}) custom-call(s32[4]{0:T(128)S(1)} %pad_add_fusion.ids, bf16[768,2048]{1,0:T(8,128)(2,1)S(1)} %get-tuple-element.23.tokens, bf16[768,2048]{1,0:T(8,128)(2,1)S(1)} %get-tuple-element.24.out_grad, ...), custom_call_target="tpu_custom_call" | custom-call | flops 1207959552 | bytes 10485760 | tf_op jit(solution)/shard_map/forward/pallas_call | solution.py:182
  55.5 3.1 %collective-permute-start.6 = (bf16[192,384]{1,0:T(8,128)(2,1)}, bf16[192,384]{1,0:T(8,128)(2,1)S(1)}, u32[]{:S(2)}, u32[]{:S(2)}) collective-permute-start(bf16[192,384]{1,0:T(8,128)(2,1)} %get-tuple-element.27), channel_id=1, source_target_pairs={{0,1},{1,0},{2,3},{3,2},{4,5},{5,4},{6,7},{7,6},{8,9},{9,8},{10,11... | collective-permute-start | bytes 442376 | tf_op jit(solution)/shard_map/ppermute | solution.py:23
  58.6 4.4 %collective-permute-start.7 = (bf16[192,384]{1,0:T(8,128)(2,1)}, bf16[192,384]{1,0:T(8,128)(2,1)S(1)}, u32[]{:S(2)}, u32[]{:S(2)}) collective-permute-start(bf16[192,384]{1,0:T(8,128)(2,1)} %get-tuple-element.28), channel_id=1, source_target_pairs={{0,2},{1,3},{2,0},{3,1},{4,6},{5,7},{6,4},{7,5},{8,10},{9,11},{10,... | collective-permute-start | bytes 442376 | tf_op jit(solution)/shard_map/ppermute | solution.py:23
  62.9 2.1 %collective-permute-start.8 = (bf16[192,384]{1,0:T(8,128)(2,1)}, bf16[192,384]{1,0:T(8,128)(2,1)S(1)}, u32[]{:S(2)}, u32[]{:S(2)}) collective-permute-start(bf16[192,384]{1,0:T(8,128)(2,1)} %get-tuple-element.29), channel_id=1, source_target_pairs={{0,3},{1,2},{2,1},{3,0},{4,7},{5,6},{6,5},{7,4},{8,11},{9,10},{10,... | collective-permute-start | bytes 442376 | tf_op jit(solution)/shard_map/ppermute | solution.py:23
  65.1 3.0 %collective-permute-done.7 = bf16[192,384]{1,0:T(8,128)(2,1)S(1)} collective-permute-done((bf16[192,384]{1,0:T(8,128)(2,1)}, bf16[192,384]{1,0:T(8,128)(2,1)S(1)}, u32[]{:S(2)}, u32[]{:S(2)}) %collective-permute-start.7) | collective-permute-done | bytes 147488 | tf_op jit(solution)/shard_map/ppermute | solution.py:23
  68.1 2.6 %collective-permute-done.8 = bf16[192,384]{1,0:T(8,128)(2,1)S(1)} collective-permute-done((bf16[192,384]{1,0:T(8,128)(2,1)}, bf16[192,384]{1,0:T(8,128)(2,1)S(1)}, u32[]{:S(2)}, u32[]{:S(2)}) %collective-permute-start.8) | collective-permute-done | bytes 147488 | tf_op jit(solution)/shard_map/ppermute | solution.py:23
  70.7 0.1 add_convert_fusion.s_mine
  70.7 12.0 %collective-permute-start.9 = (bf16[192,384]{1,0:T(8,128)(2,1)S(1)}, bf16[192,384]{1,0:T(8,128)(2,1)S(1)}, u32[]{:S(2)}, u32[]{:S(2)}) collective-permute-start(bf16[192,384]{1,0:T(8,128)(2,1)S(1)} %add_convert_fusion.s_mine), channel_id=1, source_target_pairs={{0,4},{4,0},{1,5},{5,1},{2,6},{6,2},{3,7},{7,3},{8,12},{12,8},{9,1... | collective-permute-start | bytes 442376 | tf_op jit(solution)/shard_map/ppermute | solution.py:23
  83.4 0.7 copy-done.2
  84.1 0.8 rates.1.per_row
  84.9 0.6 collective-permute-done.9.s_theirs
  85.5 0.8 deltas.1.d0
  86.3 3.1 %collective-permute-start.10 = (bf16[208,384]{1,0:T(8,128)(2,1)S(1)}, bf16[208,384]{1,0:T(8,128)(2,1)S(1)}, u32[]{:S(2)}, u32[]{:S(2)}) collective-permute-start(bf16[208,384]{1,0:T(8,128)(2,1)S(1)} %deltas.1.d0), channel_id=1, source_target_pairs={{0,1},{1,0},{2,3},{3,2},{4,5},{5,4},{6,7},{7,6},{8,9},{9,8},{10,11... | collective-permute-start | bytes 479240 | tf_op jit(solution)/shard_map/ppermute | solution.py:23
  89.4 4.4 %collective-permute-start.11 = (bf16[208,384]{1,0:T(8,128)(2,1)S(1)}, bf16[208,384]{1,0:T(8,128)(2,1)S(1)}, u32[]{:S(2)}, u32[]{:S(2)}) collective-permute-start(bf16[208,384]{1,0:T(8,128)(2,1)S(1)} %deltas.1.d0), channel_id=1, source_target_pairs={{0,2},{1,3},{2,0},{3,1},{4,6},{5,7},{6,4},{7,5},{8,10},{9,11},{10,... | collective-permute-start | bytes 479240 | tf_op jit(solution)/shard_map/ppermute | solution.py:23
  93.8 2.2 %collective-permute-start.12 = (bf16[208,384]{1,0:T(8,128)(2,1)S(1)}, bf16[208,384]{1,0:T(8,128)(2,1)S(1)}, u32[]{:S(2)}, u32[]{:S(2)}) collective-permute-start(bf16[208,384]{1,0:T(8,128)(2,1)S(1)} %deltas.1.d0), channel_id=1, source_target_pairs={{0,3},{1,2},{2,1},{3,0},{4,7},{5,6},{6,5},{7,4},{8,11},{9,10},{10,... | collective-permute-start | bytes 479240 | tf_op jit(solution)/shard_map/ppermute | solution.py:23
  96.0 2.7 %collective-permute-done.11.d2 = bf16[208,384]{1,0:T(8,128)(2,1)S(1)} collective-permute-done((bf16[208,384]{1,0:T(8,128)(2,1)S(1)}, bf16[208,384]{1,0:T(8,128)(2,1)S(1)}, u32[]{:S(2)}, u32[]{:S(2)}) %collective-permute-start.11) | collective-permute-done | bytes 159776 | tf_op jit(solution)/shard_map/ppermute | solution.py:23
  98.7 3.3 %collective-permute-done.12.d3 = bf16[208,384]{1,0:T(8,128)(2,1)S(1)} collective-permute-done((bf16[208,384]{1,0:T(8,128)(2,1)S(1)}, bf16[208,384]{1,0:T(8,128)(2,1)S(1)}, u32[]{:S(2)}, u32[]{:S(2)}) %collective-permute-start.12) | collective-permute-done | bytes 159776 | tf_op jit(solution)/shard_map/ppermute | solution.py:23
  102.1 1.9 %copy-done.1 = bf16[768,2048]{1,0:T(8,128)(2,1)S(1)} copy-done((bf16[768,2048]{1,0:T(8,128)(2,1)S(1)}, bf16[768,2048]{1,0:T(8,128)(2,1)}, u32[]{:S(2)}) %copy-start.1) | copy-done | bytes 3145752
  104.0 4.9 %weight_grads.1 = (bf16[3072,128]{1,0:T(8,128)(2,1)S(1)}, bf16[3072,128]{1,0:T(8,128)(2,1)S(1)}) custom-call(s32[4]{0:T(128)S(1)} %pad_add_fusion.ids, bf16[768,2048]{1,0:T(8,128)(2,1)S(1)} %get-tuple-element.23.tokens, bf16[768,2048]{1,0:T(8,128)(2,1)S(1)} %copy-done.1, f32[768,128]{1,0:T(8,128)S(1)} %rates.1.per_row, bf16[208,384]{1,0:T(8,128)(2,1)S(1)} %deltas.1.d0, ...), custom_call_target="tpu_custom_call" | custom-call | flops 1207959552 | bytes 10485760 | tf_op jit(solution)/shard_map/weight_grads/pallas_call | solution.py:267
  108.9 4.1 %collective-permute-start.13 = (bf16[3072,128]{1,0:T(8,128)(2,1)S(1)}, bf16[3072,128]{1,0:T(8,128)(2,1)S(1)}, u32[]{:S(2)}, u32[]{:S(2)}) collective-permute-start(bf16[3072,128]{1,0:T(8,128)(2,1)S(1)} %get-tuple-element.31), channel_id=1, source_target_pairs={{0,32},{32,0},{1,33},{33,1},{2,34},{34,2},{3,35},{35,3},{4,36},{36... | collective-permute-start | bytes 2359304 | tf_op jit(solution)/shard_map/ppermute | solution.py:23
  113.0 1.9 %collective-permute-done.13.received = bf16[3072,128]{1,0:T(8,128)(2,1)S(1)} collective-permute-done((bf16[3072,128]{1,0:T(8,128)(2,1)S(1)}, bf16[3072,128]{1,0:T(8,128)(2,1)S(1)}, u32[]{:S(2)}, u32[]{:S(2)}) %collective-permute-start.13) | collective-permute-done | bytes 786464 | tf_op jit(solution)/shard_map/ppermute | solution.py:23
  114.9 0.1 core_sum.1.after
  115.0 9.2 %collective-permute-start.17 = (bf16[1728,128]{1,0:T(8,128)(2,1)S(1)}, bf16[1728,128]{1,0:T(8,128)(2,1)S(1)}, u32[]{:S(2)}, u32[]{:S(2)}) collective-permute-start(bf16[1728,128]{1,0:T(8,128)(2,1)S(1)} %core_sum.1.after), channel_id=1, source_target_pairs={{0,64},{64,0},{128,192},{192,128},{256,320},{320,256},{384,448},{4... | collective-permute-start | bytes 1327112 | tf_op jit(solution)/shard_map/ppermute | solution.py:23
  124.2 0.6 row_order.1.y0
  124.7 3.2 %collective-permute-start.14 = (bf16[832,256]{1,0:T(8,128)(2,1)S(1)}, bf16[832,256]{1,0:T(8,128)(2,1)S(1)}, u32[]{:S(2)}, u32[]{:S(2)}) collective-permute-start(bf16[832,256]{1,0:T(8,128)(2,1)S(1)} %row_order.1.y0), channel_id=1, source_target_pairs={{0,8},{8,0},{16,24},{24,16},{1,9},{9,1},{17,25},{25,17},{2,10},{10... | collective-permute-start | bytes 1277960 | tf_op jit(solution)/shard_map/ppermute | solution.py:23
  128.0 4.5 %collective-permute-start.15 = (bf16[832,256]{1,0:T(8,128)(2,1)S(1)}, bf16[832,256]{1,0:T(8,128)(2,1)S(1)}, u32[]{:S(2)}, u32[]{:S(2)}) collective-permute-start(bf16[832,256]{1,0:T(8,128)(2,1)S(1)} %row_order.1.y0), channel_id=1, source_target_pairs={{0,16},{8,24},{16,0},{24,8},{1,17},{9,25},{17,1},{25,9},{2,18},{10... | collective-permute-start | bytes 1277960 | tf_op jit(solution)/shard_map/ppermute | solution.py:23
  132.5 1.9 %collective-permute-start.16 = (bf16[832,256]{1,0:T(8,128)(2,1)S(1)}, bf16[832,256]{1,0:T(8,128)(2,1)S(1)}, u32[]{:S(2)}, u32[]{:S(2)}) collective-permute-start(bf16[832,256]{1,0:T(8,128)(2,1)S(1)} %row_order.1.y0), channel_id=1, source_target_pairs={{0,24},{8,16},{16,8},{24,0},{1,25},{9,17},{17,9},{25,1},{2,26},{10... | collective-permute-start | bytes 1277960 | tf_op jit(solution)/shard_map/ppermute | solution.py:23
  134.4 0.1 pair_sum.1
  134.6 10.6 %collective-permute-start.18 = (bf16[384,128]{1,0:T(8,128)(2,1)S(1)}, bf16[384,128]{1,0:T(8,128)(2,1)S(1)}, u32[]{:S(2)}, u32[]{:S(2)}) collective-permute-start(bf16[384,128]{1,0:T(8,128)(2,1)S(1)} %get-tuple-element.32.after), channel_id=1, source_target_pairs={{0,256},{64,320},{128,384},{192,448},{256,0},{320,64},{384,128},{4... | collective-permute-start | bytes 294920 | tf_op jit(solution)/shard_map/ppermute | solution.py:23
  145.2 1.9 %collective-permute-start.19 = (bf16[384,128]{1,0:T(8,128)(2,1)S(1)}, bf16[384,128]{1,0:T(8,128)(2,1)S(1)}, u32[]{:S(2)}, u32[]{:S(2)}) collective-permute-start(bf16[384,128]{1,0:T(8,128)(2,1)S(1)} %get-tuple-element.35), channel_id=1, source_target_pairs={{0,128},{64,192},{128,0},{192,64},{256,384},{320,448},{384,256},{4... | collective-permute-start | bytes 294920 | tf_op jit(solution)/shard_map/ppermute | solution.py:23
  147.2 4.0 %collective-permute-start.20 = (bf16[384,128]{1,0:T(8,128)(2,1)S(1)}, bf16[384,128]{1,0:T(8,128)(2,1)S(1)}, u32[]{:S(2)}, u32[]{:S(2)}) collective-permute-start(bf16[384,128]{1,0:T(8,128)(2,1)S(1)} %get-tuple-element.36), channel_id=1, source_target_pairs={{0,384},{64,448},{128,256},{192,320},{256,128},{320,192},{384,0},{... | collective-permute-start | bytes 294920 | tf_op jit(solution)/shard_map/ppermute | solution.py:23
  151.2 3.7 %collective-permute-done.16.y3 = bf16[832,256]{1,0:T(8,128)(2,1)S(1)} collective-permute-done((bf16[832,256]{1,0:T(8,128)(2,1)S(1)}, bf16[832,256]{1,0:T(8,128)(2,1)S(1)}, u32[]{:S(2)}, u32[]{:S(2)}) %collective-permute-start.16) | collective-permute-done | bytes 426016 | tf_op jit(solution)/shard_map/ppermute | solution.py:23
  154.9 2.2 %copy-done.3 = bf16[8192,256]{1,0:T(8,128)(2,1)S(1)} copy-done((bf16[8192,256]{1,0:T(8,128)(2,1)S(1)}, bf16[8192,256]{1,0:T(8,128)(2,1)}, u32[]{:S(2)}) %copy-start.3) | copy-done | bytes 4194328
  157.1 8.0 %token_grads.1 = (bf16[768,2048]{1,0:T(8,128)(2,1)}, f32[48,128]{1,0:T(8,128)}) custom-call(s32[4]{0:T(128)S(1)} %pad_add_fusion.ids, bf16[4,2048,256]{2,1,0:T(8,128)(2,1)S(1)} %bitcast.10, bf16[832,256]{1,0:T(8,128)(2,1)S(1)} %row_order.1.y0, bf16[832,256]{1,0:T(8,128)(2,1)S(1)} %collective-permute-done.14.y1, ...), custom_call_target="tpu_custom_call" | custom-call | flops 3221225472 | bytes 12582912 | tf_op jit(solution)/shard_map/token_grads/pallas_call | solution.py:396
  165.1 0.8 last_sum.1
  (22 shorter events, 0.1 us)
Async XLA Ops:
  7.2 147.8 %all-gather.3.cloned.1.call-start = ((), (), s32[]{:S(2)}) async-start(), calls=%async_computation | async-start | bytes 5242880 | tf_op jit(solution)/shard_map/all_gather | solution.py:458
  8.3 19.4 %collective-permute-start = (bf16[128,384]{1,0:T(8,128)(2,1)S(1)}, bf16[128,384]{1,0:T(8,128)(2,1)S(1)}, u32[]{:S(2)}, u32[]{:S(2)}) collective-permute-start(bf16[128,384]{1,0:T(8,128)(2,1)S(1)} %own_tiles.1.a), channel_id=1, source_target_pairs={{0,256},{64,320},{128,384},{192,448},{256,0},{320,64},{384,128},{4... | collective-permute-start | bytes 294920 | tf_op jit(solution)/shard_map/ppermute | solution.py:23
  18.0 9.7 %collective-permute-start.1 = (bf16[128,384]{1,0:T(8,128)(2,1)S(1)}, bf16[128,384]{1,0:T(8,128)(2,1)S(1)}, u32[]{:S(2)}, u32[]{:S(2)}) collective-permute-start(bf16[128,384]{1,0:T(8,128)(2,1)S(1)} %own_tiles.1.a), channel_id=1, source_target_pairs={{0,128},{64,192},{128,0},{192,64},{256,384},{320,448},{384,256},{4... | collective-permute-start | bytes 294920 | tf_op jit(solution)/shard_map/ppermute | solution.py:23
  22.9 11.1 %collective-permute-start.2 = (bf16[128,384]{1,0:T(8,128)(2,1)S(1)}, bf16[128,384]{1,0:T(8,128)(2,1)S(1)}, u32[]{:S(2)}, u32[]{:S(2)}) collective-permute-start(bf16[128,384]{1,0:T(8,128)(2,1)S(1)} %own_tiles.1.a), channel_id=1, source_target_pairs={{0,384},{64,448},{128,256},{192,320},{256,128},{320,192},{384,0},{... | collective-permute-start | bytes 294920 | tf_op jit(solution)/shard_map/ppermute | solution.py:23
  27.7 23.4 %copy-start = (bf16[768,2048]{1,0:T(8,128)(2,1)}, bf16[768,2048]{1,0:T(8,128)(2,1)S(1)}, u32[]{:S(2)}) copy-start(bf16[768,2048]{1,0:T(8,128)(2,1)S(1)} %get-tuple-element.24.out_grad) | copy-start | bytes 9437188
  34.0 48.7 %copy-start.4 = (s32[768]{0:T(1024)S(1)}, s32[768]{0:T(1024)}, u32[]{:S(2)}) copy-start(s32[768]{0:T(1024)} %param.15) | copy-start | bytes 9220
  34.0 9.6 %collective-permute-start.3 = (bf16[512,384]{1,0:T(8,128)(2,1)S(1)}, bf16[512,384]{1,0:T(8,128)(2,1)S(1)}, u32[]{:S(2)}, u32[]{:S(2)}) collective-permute-start(bf16[512,384]{1,0:T(8,128)(2,1)S(1)} %join.1.m0), channel_id=1, source_target_pairs={{0,64},{64,0},{128,192},{192,128},{256,320},{320,256},{384,448},{4... | collective-permute-start | bytes 1179656 | tf_op jit(solution)/shard_map/ppermute | solution.py:23
  37.6 12.1 %collective-permute-start.4 = (bf16[512,384]{1,0:T(8,128)(2,1)S(1)}, bf16[512,384]{1,0:T(8,128)(2,1)S(1)}, u32[]{:S(2)}, u32[]{:S(2)}) collective-permute-start(bf16[512,384]{1,0:T(8,128)(2,1)S(1)} %join.1.m0), channel_id=1, source_target_pairs={{0,32},{32,0},{1,33},{33,1},{2,34},{34,2},{3,35},{35,3},{4,36},{36... | collective-permute-start | bytes 1179656 | tf_op jit(solution)/shard_map/ppermute | solution.py:23
  43.6 7.5 %collective-permute-start.5 = (bf16[512,384]{1,0:T(8,128)(2,1)S(1)}, bf16[512,384]{1,0:T(8,128)(2,1)S(1)}, u32[]{:S(2)}, u32[]{:S(2)}) collective-permute-start(bf16[512,384]{1,0:T(8,128)(2,1)S(1)} %collective-permute-done.3.m1), channel_id=1, source_target_pairs={{0,32},{32,0},{1,33},{33,1},{2,34},{34,2},{3,35},{35,3},{4,36},{36... | collective-permute-start | bytes 1179656 | tf_op jit(solution)/shard_map/ppermute | solution.py:23
  55.5 9.6 %collective-permute-start.6 = (bf16[192,384]{1,0:T(8,128)(2,1)}, bf16[192,384]{1,0:T(8,128)(2,1)S(1)}, u32[]{:S(2)}, u32[]{:S(2)}) collective-permute-start(bf16[192,384]{1,0:T(8,128)(2,1)} %get-tuple-element.27), channel_id=1, source_target_pairs={{0,1},{1,0},{2,3},{3,2},{4,5},{5,4},{6,7},{7,6},{8,9},{9,8},{10,11... | collective-permute-start | bytes 442376 | tf_op jit(solution)/shard_map/ppermute | solution.py:23
  58.6 9.5 %collective-permute-start.7 = (bf16[192,384]{1,0:T(8,128)(2,1)}, bf16[192,384]{1,0:T(8,128)(2,1)S(1)}, u32[]{:S(2)}, u32[]{:S(2)}) collective-permute-start(bf16[192,384]{1,0:T(8,128)(2,1)} %get-tuple-element.28), channel_id=1, source_target_pairs={{0,2},{1,3},{2,0},{3,1},{4,6},{5,7},{6,4},{7,5},{8,10},{9,11},{10,... | collective-permute-start | bytes 442376 | tf_op jit(solution)/shard_map/ppermute | solution.py:23
  62.9 7.7 %collective-permute-start.8 = (bf16[192,384]{1,0:T(8,128)(2,1)}, bf16[192,384]{1,0:T(8,128)(2,1)S(1)}, u32[]{:S(2)}, u32[]{:S(2)}) collective-permute-start(bf16[192,384]{1,0:T(8,128)(2,1)} %get-tuple-element.29), channel_id=1, source_target_pairs={{0,3},{1,2},{2,1},{3,0},{4,7},{5,6},{6,5},{7,4},{8,11},{9,10},{10,... | collective-permute-start | bytes 442376 | tf_op jit(solution)/shard_map/ppermute | solution.py:23
  70.7 14.7 %collective-permute-start.9 = (bf16[192,384]{1,0:T(8,128)(2,1)S(1)}, bf16[192,384]{1,0:T(8,128)(2,1)S(1)}, u32[]{:S(2)}, u32[]{:S(2)}) collective-permute-start(bf16[192,384]{1,0:T(8,128)(2,1)S(1)} %add_convert_fusion.s_mine), channel_id=1, source_target_pairs={{0,4},{4,0},{1,5},{5,1},{2,6},{6,2},{3,7},{7,3},{8,12},{12,8},{9,1... | collective-permute-start | bytes 442376 | tf_op jit(solution)/shard_map/ppermute | solution.py:23
  83.4 0.7 copy-start.2
  86.3 9.7 %collective-permute-start.10 = (bf16[208,384]{1,0:T(8,128)(2,1)S(1)}, bf16[208,384]{1,0:T(8,128)(2,1)S(1)}, u32[]{:S(2)}, u32[]{:S(2)}) collective-permute-start(bf16[208,384]{1,0:T(8,128)(2,1)S(1)} %deltas.1.d0), channel_id=1, source_target_pairs={{0,1},{1,0},{2,3},{3,2},{4,5},{5,4},{6,7},{7,6},{8,9},{9,8},{10,11... | collective-permute-start | bytes 479240 | tf_op jit(solution)/shard_map/ppermute | solution.py:23
  89.4 9.3 %collective-permute-start.11 = (bf16[208,384]{1,0:T(8,128)(2,1)S(1)}, bf16[208,384]{1,0:T(8,128)(2,1)S(1)}, u32[]{:S(2)}, u32[]{:S(2)}) collective-permute-start(bf16[208,384]{1,0:T(8,128)(2,1)S(1)} %deltas.1.d0), channel_id=1, source_target_pairs={{0,2},{1,3},{2,0},{3,1},{4,6},{5,7},{6,4},{7,5},{8,10},{9,11},{10,... | collective-permute-start | bytes 479240 | tf_op jit(solution)/shard_map/ppermute | solution.py:23
  93.8 8.2 %collective-permute-start.12 = (bf16[208,384]{1,0:T(8,128)(2,1)S(1)}, bf16[208,384]{1,0:T(8,128)(2,1)S(1)}, u32[]{:S(2)}, u32[]{:S(2)}) collective-permute-start(bf16[208,384]{1,0:T(8,128)(2,1)S(1)} %deltas.1.d0), channel_id=1, source_target_pairs={{0,3},{1,2},{2,1},{3,0},{4,7},{5,6},{6,5},{7,4},{8,11},{9,10},{10,... | collective-permute-start | bytes 479240 | tf_op jit(solution)/shard_map/ppermute | solution.py:23
  102.1 1.9 %copy-start.1 = (bf16[768,2048]{1,0:T(8,128)(2,1)S(1)}, bf16[768,2048]{1,0:T(8,128)(2,1)}, u32[]{:S(2)}) copy-start(bf16[768,2048]{1,0:T(8,128)(2,1)} %copy-done) | copy-start | bytes 9437188
  108.9 6.0 %collective-permute-start.13 = (bf16[3072,128]{1,0:T(8,128)(2,1)S(1)}, bf16[3072,128]{1,0:T(8,128)(2,1)S(1)}, u32[]{:S(2)}, u32[]{:S(2)}) collective-permute-start(bf16[3072,128]{1,0:T(8,128)(2,1)S(1)} %get-tuple-element.31), channel_id=1, source_target_pairs={{0,32},{32,0},{1,33},{33,1},{2,34},{34,2},{3,35},{35,3},{4,36},{36... | collective-permute-start | bytes 2359304 | tf_op jit(solution)/shard_map/ppermute | solution.py:23
  115.0 19.4 %collective-permute-start.17 = (bf16[1728,128]{1,0:T(8,128)(2,1)S(1)}, bf16[1728,128]{1,0:T(8,128)(2,1)S(1)}, u32[]{:S(2)}, u32[]{:S(2)}) collective-permute-start(bf16[1728,128]{1,0:T(8,128)(2,1)S(1)} %core_sum.1.after), channel_id=1, source_target_pairs={{0,64},{64,0},{128,192},{192,128},{256,320},{320,256},{384,448},{4... | collective-permute-start | bytes 1327112 | tf_op jit(solution)/shard_map/ppermute | solution.py:23
  124.7 22.4 %collective-permute-start.14 = (bf16[832,256]{1,0:T(8,128)(2,1)S(1)}, bf16[832,256]{1,0:T(8,128)(2,1)S(1)}, u32[]{:S(2)}, u32[]{:S(2)}) collective-permute-start(bf16[832,256]{1,0:T(8,128)(2,1)S(1)} %row_order.1.y0), channel_id=1, source_target_pairs={{0,8},{8,0},{16,24},{24,16},{1,9},{9,1},{17,25},{25,17},{2,10},{10... | collective-permute-start | bytes 1277960 | tf_op jit(solution)/shard_map/ppermute | solution.py:23
  128.0 23.2 %collective-permute-start.15 = (bf16[832,256]{1,0:T(8,128)(2,1)S(1)}, bf16[832,256]{1,0:T(8,128)(2,1)S(1)}, u32[]{:S(2)}, u32[]{:S(2)}) collective-permute-start(bf16[832,256]{1,0:T(8,128)(2,1)S(1)} %row_order.1.y0), channel_id=1, source_target_pairs={{0,16},{8,24},{16,0},{24,8},{1,17},{9,25},{17,1},{25,9},{2,18},{10... | collective-permute-start | bytes 1277960 | tf_op jit(solution)/shard_map/ppermute | solution.py:23
  132.5 22.4 %collective-permute-start.16 = (bf16[832,256]{1,0:T(8,128)(2,1)S(1)}, bf16[832,256]{1,0:T(8,128)(2,1)S(1)}, u32[]{:S(2)}, u32[]{:S(2)}) collective-permute-start(bf16[832,256]{1,0:T(8,128)(2,1)S(1)} %row_order.1.y0), channel_id=1, source_target_pairs={{0,24},{8,16},{16,8},{24,0},{1,25},{9,17},{17,9},{25,1},{2,26},{10... | collective-permute-start | bytes 1277960 | tf_op jit(solution)/shard_map/ppermute | solution.py:23
  134.6 30.5 %collective-permute-start.18 = (bf16[384,128]{1,0:T(8,128)(2,1)S(1)}, bf16[384,128]{1,0:T(8,128)(2,1)S(1)}, u32[]{:S(2)}, u32[]{:S(2)}) collective-permute-start(bf16[384,128]{1,0:T(8,128)(2,1)S(1)} %get-tuple-element.32.after), channel_id=1, source_target_pairs={{0,256},{64,320},{128,384},{192,448},{256,0},{320,64},{384,128},{4... | collective-permute-start | bytes 294920 | tf_op jit(solution)/shard_map/ppermute | solution.py:23
  145.2 19.9 %collective-permute-start.19 = (bf16[384,128]{1,0:T(8,128)(2,1)S(1)}, bf16[384,128]{1,0:T(8,128)(2,1)S(1)}, u32[]{:S(2)}, u32[]{:S(2)}) collective-permute-start(bf16[384,128]{1,0:T(8,128)(2,1)S(1)} %get-tuple-element.35), channel_id=1, source_target_pairs={{0,128},{64,192},{128,0},{192,64},{256,384},{320,448},{384,256},{4... | collective-permute-start | bytes 294920 | tf_op jit(solution)/shard_map/ppermute | solution.py:23
  147.2 17.9 %collective-permute-start.20 = (bf16[384,128]{1,0:T(8,128)(2,1)S(1)}, bf16[384,128]{1,0:T(8,128)(2,1)S(1)}, u32[]{:S(2)}, u32[]{:S(2)}) collective-permute-start(bf16[384,128]{1,0:T(8,128)(2,1)S(1)} %get-tuple-element.36), channel_id=1, source_target_pairs={{0,384},{64,448},{128,256},{192,320},{256,128},{320,192},{384,0},{... | collective-permute-start | bytes 294920 | tf_op jit(solution)/shard_map/ppermute | solution.py:23
  154.9 2.2 %copy-start.3 = (bf16[8192,256]{1,0:T(8,128)(2,1)S(1)}, bf16[8192,256]{1,0:T(8,128)(2,1)}, u32[]{:S(2)}) copy-start(bf16[8192,256]{1,0:T(8,128)(2,1)} %all-gather.3.cloned.1.call-done) | copy-start | bytes 12582916
Sparse Core Ops, SparseCore 0:
  55.6 57.9 all-gather.2

commit v6 on v5

--- a/solution.py
+++ b/solution.py
@@ -14,6 +14,7 @@
 D = 2048
 RB = CAP // XS
 PAD = 192
+WIDE = 512
 MSG = RB + 16
 AXES = ("z", "core", "row", "zhi", "x")
 NT = (((1,), (1,)), ((), ()))
@@ -106,27 +107,26 @@
     )(ids, *in_hbm(gate_scales, up_scales, down_scales, gate, up, down))
 
 
-def load_kernel(tokens, out_grad, tokens_out, out_grad_out, sems):
-    copies = (
-        pltpu.make_async_copy(tokens, tokens_out, sems.at[0]),
-        pltpu.make_async_copy(out_grad, out_grad_out, sems.at[1]),
-    )
+def load_kernel(*refs):
+    n = len(refs) // 2
+    copies = [pltpu.make_async_copy(refs[i], refs[n + i], refs[-1].at[i]) for i in range(n)]
     for copy in copies:
         copy.start()
     for copy in copies:
         copy.wait()
 
 
-def load(tokens, out_grad):
+def load(*arrays):
+    n = len(arrays)
     return pl.pallas_call(
         load_kernel,
-        out_shape=[pltpu.VMEM((CAP, D), BF)] * 2,
-        in_specs=[ANY] * 2,
-        out_specs=[ANY] * 2,
-        scratch_shapes=[pltpu.SemaphoreType.DMA((2,))],
+        out_shape=[pltpu.VMEM(array.shape, array.dtype) for array in arrays],
+        in_specs=[ANY] * n,
+        out_specs=[ANY] * n,
+        scratch_shapes=[pltpu.SemaphoreType.DMA((n,))],
         compiler_params=params(1),
         name="load",
-    )(*in_hbm(tokens, out_grad))
+    )(*in_hbm(*arrays))
 
 
 def join_kernel(a, b, c, d, tokens, out_grad, out):
@@ -145,7 +145,7 @@
     )(*blocks, tokens, out_grad)
 
 
-def forward_kernel(ids, tokens, out_grad, m0, m1, t0, t1, own, p1, p2, p3, w_both, w_down):
+def forward_kernel(ids, tokens, out_grad, m0, m1, t0, t1, own, p1, p2, p3, w_out, w_both, w_down, sem):
     step = pl.program_id(0)
     z, core = ids[0], ids[1]
 
@@ -159,6 +159,8 @@
                 w_both[rows, :] = ref[j * T : (j + 1) * T, 0 : 2 * T]
                 w_down[rows, :] = ref[j * T : (j + 1) * T, 2 * T : 3 * T]
 
+        pltpu.make_async_copy(w_both, w_out, sem).start()
+
     gate_up = jnp.dot(tokens[...], w_both[...], preferred_element_type=F32)
     back = jnp.dot(out_grad[...], w_down[...], preferred_element_type=F32)
 
@@ -173,6 +175,10 @@
         def _():
             ref[:, 0 : 2 * T] = gate_up.astype(BF)
             ref[:, 2 * T : 3 * T] = back.astype(BF)
+
+    @pl.when(step == XS - 1)
+    def _():
+        pltpu.make_async_copy(w_both, w_out, sem).wait()
 
 
 def forward(ids, tokens, out_grad, mine, theirs):
@@ -185,8 +191,12 @@
             num_scalar_prefetch=1,
             grid=(XS,),
             in_specs=[rows, rows] + [whole(4 * T, 3 * T)] * 4,
-            out_specs=[whole(RB, 3 * T)] * 4 + [whole(D, 2 * T)],
-            scratch_shapes=[pltpu.VMEM((D, T), BF)],
+            out_specs=[whole(RB, 3 * T)] * 4 + [ANY],
+            scratch_shapes=[
+                pltpu.VMEM((D, 2 * T), BF),
+                pltpu.VMEM((D, T), BF),
+                pltpu.SemaphoreType.DMA,
+            ],
         ),
         out_shape=[
             jax.ShapeDtypeStruct((RB, 3 * T), F32),
@@ -201,7 +211,25 @@
     )(ids, tokens, out_grad, *mine, *theirs)
 
 
-def delta_kernel(ids, s_mine, s_theirs, per_row, out):
+def reduce_kernel(own, g1, g2, g3, total):
+    total[...] = (
+        own[...] + g1[...].astype(F32) + g2[...].astype(F32) + g3[...].astype(F32)
+    ).astype(BF)
+
+
+def reduce_rows(own, got):
+    return pl.pallas_call(
+        reduce_kernel,
+        out_shape=jax.ShapeDtypeStruct((RB, 3 * T), BF),
+        in_specs=[VMEM] * 4,
+        out_specs=VMEM,
+        compiler_params=params(8),
+        cost_estimate=work(20_000_000_000, 2),
+        name="reduce_rows",
+    )(own, *got)
+
+
+def delta_kernel(ids, s_mine, s_theirs, per_row, after, out):
     total = s_mine[...].astype(F32) + s_theirs[...].astype(F32)
     gate, up, back = total[:, 0:T], total[:, T : 2 * T], total[:, 2 * T : 3 * T]
     weight = per_row[pl.ds(pl.multiple_of(ids[2] * RB, RB), RB), :][:, 0:1]
@@ -227,19 +255,20 @@
     out[RB:MSG, 2 * T : 3 * T] = jnp.zeros((16, T), BF)
 
 
-def deltas(ids, s_mine, s_theirs, per_row):
+def deltas(ids, s_mine, s_theirs, per_row, after):
     return pl.pallas_call(
         delta_kernel,
         out_shape=jax.ShapeDtypeStruct((MSG, 3 * T), BF),
-        in_specs=[SMEM] + [VMEM] * 3,
-        out_specs=VMEM,
-        compiler_params=params(8),
+        in_specs=[SMEM] + [VMEM] * 3 + [ANY],
+        out_specs=VMEM,
+        compiler_params=params(8),
+        cost_estimate=work(20_000_000_000, 2),
         name="deltas",
-    )(ids, s_mine, s_theirs, per_row)
+    )(ids, s_mine, s_theirs, per_row, after)
 
 
 def weight_grad_kernel(
-    ids, tokens, out_grad, per_row, d0, d1, d2, d3, keep, send, flat, turned
+    ids, tokens, out_grad, per_row, d0, d1, d2, d3, w1, w2a, w2b, w3, keep, send, flat, turned
 ):
     step = pl.program_id(0)
     core, x = ids[1], ids[2]
@@ -260,7 +289,7 @@
         send[rows, :] = jnp.where(core == 0, high, low)
 
 
-def weight_grads(ids, tokens, out_grad, per_row, parts):
+def weight_grads(ids, tokens, out_grad, per_row, parts, after):
     whole = lambda *shape: pl.BlockSpec(shape, lambda i, ids: (0,) * len(shape))
     columns = pl.BlockSpec((CAP, 2 * T), lambda i, ids: (0, ids[0] ^ far_first(i ^ 4)))
     block = pl.BlockSpec((3 * T, T), lambda i, ids: (i, 0))
@@ -269,7 +298,7 @@
         grid_spec=pltpu.PrefetchScalarGridSpec(
             num_scalar_prefetch=1,
             grid=(Z,),
-            in_specs=[columns, columns, whole(CAP, T)] + [whole(MSG, 3 * T)] * 4,
+            in_specs=[columns, columns, whole(CAP, T)] + [whole(MSG, 3 * T)] * 4 + [ANY] * 4,
             out_specs=[block, block],
             scratch_shapes=[pltpu.VMEM((CAP, 3 * T), BF), pltpu.VMEM((3 * T, CAP), BF)],
         ),
@@ -280,7 +309,7 @@
         compiler_params=params(),
         cost_estimate=work(2 * CAP * D * 3 * T, 10),
         name="weight_grads",
-    )(ids, tokens, out_grad, per_row, *parts)
+    )(ids, tokens, out_grad, per_row, *parts, *in_hbm(*after))
 
 
 def rows_kernel(ids, d0, d1, d2, d3, after, out):
@@ -358,10 +387,10 @@
 
 
 def token_grad_kernel(
-    ids, weights, y0, y1, y2, y3, per_row, after, out, logits_out, router, flat, w
+    ids, w0, w1, w2a, w2b, w3, y0, y1, y2, y3, per_row, after, out, logits_out, router, flat
 ):
     step = pl.program_id(0)
-    x, y = ids[2], ids[3]
+    x = ids[2]
     rows_by_y = (y0, y1, y2, y3)
 
     @pl.when(step == 0)
@@ -386,31 +415,40 @@
             total = total + jnp.dot(upper, piece, preferred_element_type=F32)
         logits_out[...] = total[0 : SEQ // T, :]
 
-    for j in range(ROWS):
-        w[:, j * 2 * T : (j + 1) * 2 * T] = weights[y ^ j]
-    out[...] = lax.dot_general(flat[...], w[...], NT, preferred_element_type=F32).astype(BF)
+    total = jnp.zeros((CAP, WIDE), F32)
+    w2 = jnp.where(step < D // WIDE // 2, w2a[...], w2b[...])
+    for j, w in enumerate((w0[...], w1[...], w2, w3[...])):
+        total += lax.dot_general(
+            flat[:, j * 2 * T : (j + 1) * 2 * T], w, NT, preferred_element_type=F32
+        )
+    out[...] = total.astype(BF)
 
 
 def token_grads(ids, weights, rows_by_y, per_row, after):
     whole = lambda *shape: pl.BlockSpec(shape, lambda i, ids: (0,) * len(shape))
+    half = D // WIDE // 2
+    tiles = lambda index: pl.BlockSpec((WIDE, 2 * T), lambda i, ids: (index(i), 0))
     return pl.pallas_call(
         token_grad_kernel,
         grid_spec=pltpu.PrefetchScalarGridSpec(
             num_scalar_prefetch=1,
-            grid=(Z,),
+            grid=(D // WIDE,),
             in_specs=[
-                pl.BlockSpec((ROWS, 2 * T, 2 * T), lambda i, ids: (0, i, 0)),
+                tiles(lambda i: i),
+                tiles(lambda i: i),
+                tiles(lambda i: jnp.minimum(i, half - 1)),
+                tiles(lambda i: jnp.maximum(i - half, 0)),
+                tiles(lambda i: i),
             ]
             + [whole(CAP + XS * 16, 2 * T)] * 4
             + [whole(CAP, T), ANY],
             out_specs=[
-                pl.BlockSpec((CAP, 2 * T), lambda i, ids: (0, i)),
+                pl.BlockSpec((CAP, WIDE), lambda i, ids: (0, i)),
                 whole(SEQ // T, T),
             ],
             scratch_shapes=[
                 pltpu.VMEM((CAP, 1), F32),
                 pltpu.VMEM((CAP, 8 * T), BF),
-                pltpu.VMEM((2 * T, 8 * T), BF),
             ],
         ),
         out_shape=[
@@ -420,7 +458,7 @@
         compiler_params=params(),
         cost_estimate=work(2 * CAP * D * 8 * T, 12),
         name="token_grads",
-    )(ids, weights, *rows_by_y, per_row, after)
+    )(ids, *in_hbm(*weights), *rows_by_y, per_row, after)
 
 
 def local(
@@ -436,28 +474,28 @@
     up_scales,
     down_scales,
 ):
-    ids = jnp.stack([lax.axis_index(axis) for axis in ("z", "core", "x", "row")]).astype(jnp.int32)
+    ids = jnp.stack([lax.axis_index(axis) for axis in ("z", "core", "x")]).astype(jnp.int32)
 
     scales = (gate_scales.T, up_scales.T, down_scales)
     held = own_tiles(ids, *scales, gate_values, up_values, down_values)
-    tokens, out_grad = load(tokens, out_grad)
-    held = join([held] + [swap(held, "z", Z, mask) for mask in (4, 2, 6)], tokens, out_grad)
+    tokens, out_grad_early = load(tokens, out_grad)
+    held = join([held] + [swap(held, "z", Z, mask) for mask in (4, 2, 6)], tokens, out_grad_early)
     mine = (held, swap(held, "z", Z, 1))
     theirs = tuple(swap(h, "core", CORES, 1) for h in mine)
     per_row = rates(router_logits.reshape(SEQ // T, T), routed_positions[None, :], routed_counts)
 
-    own, p1, p2, p3, w_own = forward(ids, tokens, out_grad, mine, theirs)
+    own, p1, p2, p3, w_own = forward(ids, tokens, out_grad_early, mine, theirs)
     got = [swap(p, "x", XS, r) for r, p in ((1, p1), (2, p2), (3, p3))]
-    total = own
-    for g in got:
-        total = total + g.astype(F32)
-    total = total.astype(BF)
-    message = deltas(ids, total, swap(total, "zhi", Z_HI, 1), per_row)
+    total = reduce_rows(own, got)
+    (out_grad,) = load(out_grad)
+    message = deltas(ids, total, swap(total, "zhi", Z_HI, 1), per_row, out_grad)
     parts = [message] + [swap(message, "x", XS, r) for r in (1, 2, 3)]
 
-    weights = lax.all_gather(w_own, "row")
-
-    keep, send = weight_grads(ids, tokens, out_grad, per_row, parts)
+    w1, w3 = (swap(w_own, "row", ROWS, r) for r in (1, 3))
+    w2 = (swap(w3[: D // 2], "row", ROWS, 1), swap(w1[D // 2 :], "row", ROWS, 3))
+    weights = (w_own, w1, *w2, w3)
+
+    keep, send = weight_grads(ids, tokens, out_grad, per_row, parts, weights[1:])
     received = swap(send, "core", CORES, 1)
     sent = core_sum(keep, received)
     arrived = swap(sent, "z", Z, 1)

time: 176 us -> 165 us (0.938); the launches traced: 173 us -> 164 us
  between operations: 15 us -> 1.73 us
  starting transfers between devices: 102 us -> 107 us
  local copies, waits for them, and re-layouts: 4.87 us -> 1.7 us
  Pallas kernels: 24.3 us -> 26.4 us
    ppermute x21 -> x25, starting transfers between devices: 101 us -> 107 us  [swap(): return lax.ppermute(value, axis, [(i, i ^ mask) for i in range(size)])]
    unnamed x10 -> x12, local copies, waits for them, and re-layouts: 4.87 us -> 1.62 us
    pallas_call x1 -> x3, Pallas kernels: 2.87 us -> 4.84 us  [the longest x2 4.77 us: load(): pl.pallas_call(load_kernel, out_shape=[pltpu.VMEM(array.shape, array.dtyp...]
    ppermute x21 -> x25, waiting for transfers between devices: 26.8 us -> 27.1 us  [swap(): return lax.ppermute(value, axis, [(i, i ^ mask) for i in range(size)])]
  transfers between devices with their start and end apart: 22 -> 25, of which waited for: 10 -> 9; matrix products, arithmetic and copies ran while one was open for 0% -> 0% of each run, Pallas kernels for 10% -> 10%
where the time goes in v6:
time: 165 us; the launch traced here: 164 us
  starting transfers between devices  107 us (65%)
  waiting for transfers between devices  27.1 us (16%)
  Pallas kernels  26.4 us (16%)
  between operations  1.73 us (1%)
  local copies, waits for them, and re-layouts  1.7 us (1%)
    ppermute x25, starting transfers between devices, swap(): return lax.ppermute(value, axis, [(i, i ^ mask) for i in range(size)])  107 us
    ppermute x25, waiting for transfers between devices, swap(): return lax.ppermute(value, axis, [(i, i ^ mask) for i in range(size)])  27.1 us
    pallas_call x1, Pallas kernels, token_grads(): pl.pallas_call(token_grad_kernel, grid_spec=pltpu.PrefetchScalarGridSpec(...  8.5 us
    pallas_call x1, Pallas kernels, weight_grads(): pl.pallas_call(weight_grad_kernel, grid_spec=pltpu.PrefetchScalarGridSpec...  4.93 us
    pallas_call x2, Pallas kernels, load(): pl.pallas_call(load_kernel, out_shape=[pltpu.VMEM(array.shape, array.dtyp...  4.77 us
    pallas_call x1, Pallas kernels, forward(): pl.pallas_call(forward_kernel, grid_spec=pltpu.PrefetchScalarGridSpec(num...  3.9 us
  transfers between devices with their start and end apart: 25, of which 9 were waited for; matrix products, arithmetic and copies ran while one was open for 0% of the time, Pallas kernels for 10%

profile of v6, /device:TPU:1, one launch (start us, length us, event | category | flops | bytes accessed | tf_op | source)
XLA Modules:
  0.0 163.8 jit_solution(7163175111106102320)
XLA Ops:
  0.7 1.0 own_tiles.1.a
  1.7 9.6 %collective-permute-start = (bf16[128,384]{1,0:T(8,128)(2,1)S(1)}, bf16[128,384]{1,0:T(8,128)(2,1)S(1)}, u32[]{:S(2)}, u32[]{:S(2)}) collective-permute-start(bf16[128,384]{1,0:T(8,128)(2,1)S(1)} %own_tiles.1.a), channel_id=1, source_target_pairs={{0,256},{64,320},{128,384},{192,448},{256,0},{320,64},{384,128},{4... | collective-permute-start | bytes 294920 | tf_op jit(solution)/shard_map/ppermute | solution.py:24
  11.4 4.9 %collective-permute-start.1 = (bf16[128,384]{1,0:T(8,128)(2,1)S(1)}, bf16[128,384]{1,0:T(8,128)(2,1)S(1)}, u32[]{:S(2)}, u32[]{:S(2)}) collective-permute-start(bf16[128,384]{1,0:T(8,128)(2,1)S(1)} %own_tiles.1.a), channel_id=1, source_target_pairs={{0,128},{64,192},{128,0},{192,64},{256,384},{320,448},{384,256},{4... | collective-permute-start | bytes 294920 | tf_op jit(solution)/shard_map/ppermute | solution.py:24
  16.3 1.9 %collective-permute-start.2 = (bf16[128,384]{1,0:T(8,128)(2,1)S(1)}, bf16[128,384]{1,0:T(8,128)(2,1)S(1)}, u32[]{:S(2)}, u32[]{:S(2)}) collective-permute-start(bf16[128,384]{1,0:T(8,128)(2,1)S(1)} %own_tiles.1.a), channel_id=1, source_target_pairs={{0,384},{64,448},{128,256},{192,320},{256,128},{320,192},{384,0},{... | collective-permute-start | bytes 294920 | tf_op jit(solution)/shard_map/ppermute | solution.py:24
  18.2 2.9 %load.2 = (bf16[768,2048]{1,0:T(8,128)(2,1)S(1)}, bf16[768,2048]{1,0:T(8,128)(2,1)S(1)}) custom-call(bf16[768,2048]{1,0:T(8,128)(2,1)} %refs_0_.2, bf16[768,2048]{1,0:T(8,128)(2,1)} %refs_0_.3), custom_call_target="tpu_custom_call" | custom-call | tf_op jit(solution)/shard_map/load/pallas_call | solution.py:121
  21.1 6.2 %collective-permute-done.2.d = bf16[128,384]{1,0:T(8,128)(2,1)S(1)} collective-permute-done((bf16[128,384]{1,0:T(8,128)(2,1)S(1)}, bf16[128,384]{1,0:T(8,128)(2,1)S(1)}, u32[]{:S(2)}, u32[]{:S(2)}) %collective-permute-start.2) | collective-permute-done | bytes 98336 | tf_op jit(solution)/shard_map/ppermute | solution.py:24
  27.4 3.6 %collective-permute-start.3 = (bf16[512,384]{1,0:T(8,128)(2,1)S(1)}, bf16[512,384]{1,0:T(8,128)(2,1)S(1)}, u32[]{:S(2)}, u32[]{:S(2)}) collective-permute-start(bf16[512,384]{1,0:T(8,128)(2,1)S(1)} %join.1.m0), channel_id=1, source_target_pairs={{0,64},{64,0},{128,192},{192,128},{256,320},{320,256},{384,448},{4... | collective-permute-start | bytes 1179656 | tf_op jit(solution)/shard_map/ppermute | solution.py:24
  31.0 4.6 %collective-permute-start.4 = (bf16[512,384]{1,0:T(8,128)(2,1)S(1)}, bf16[512,384]{1,0:T(8,128)(2,1)S(1)}, u32[]{:S(2)}, u32[]{:S(2)}) collective-permute-start(bf16[512,384]{1,0:T(8,128)(2,1)S(1)} %join.1.m0), channel_id=1, source_target_pairs={{0,32},{32,0},{1,33},{33,1},{2,34},{34,2},{3,35},{35,3},{4,36},{36... | collective-permute-start | bytes 1179656 | tf_op jit(solution)/shard_map/ppermute | solution.py:24
  35.7 1.4 collective-permute-done.3.m1
  37.0 6.1 %collective-permute-start.5 = (bf16[512,384]{1,0:T(8,128)(2,1)S(1)}, bf16[512,384]{1,0:T(8,128)(2,1)S(1)}, u32[]{:S(2)}, u32[]{:S(2)}) collective-permute-start(bf16[512,384]{1,0:T(8,128)(2,1)S(1)} %collective-permute-done.3.m1), channel_id=1, source_target_pairs={{0,32},{32,0},{1,33},{33,1},{2,34},{34,2},{3,35},{35,3},{4,36},{36... | collective-permute-start | bytes 1179656 | tf_op jit(solution)/shard_map/ppermute | solution.py:24
  43.2 1.3 collective-permute-done.5.t1
  44.5 3.9 %forward.1 = (f32[192,384]{1,0:T(8,128)S(1)}, bf16[192,384]{1,0:T(8,128)(2,1)}, bf16[192,384]{1,0:T(8,128)(2,1)}, bf16[192,384]{1,0:T(8,128)(2,1)}, bf16[2048,256]{1,0:T(8,128)(2,1)}) custom-call(s32[3]{0:T(128)S(1)} %pad_add_fusion.ids, bf16[768,2048]{1,0:T(8,128)(2,1)S(1)} %get-tuple-element.23.tokens, bf16[768,2048]{1,0:T(8,128)(2,1)S(1)} %get-tuple-element.24.out_grad, ...), custom_call_target="tpu_custom_call" | custom-call | flops 1207959552 | bytes 10485760 | tf_op jit(solution)/shard_map/forward/pallas_call | solution.py:188
  48.4 3.1 %collective-permute-start.10 = (bf16[192,384]{1,0:T(8,128)(2,1)}, bf16[192,384]{1,0:T(8,128)(2,1)S(1)}, u32[]{:S(2)}, u32[]{:S(2)}) collective-permute-start(bf16[192,384]{1,0:T(8,128)(2,1)} %get-tuple-element.27), channel_id=1, source_target_pairs={{0,1},{1,0},{2,3},{3,2},{4,5},{5,4},{6,7},{7,6},{8,9},{9,8},{10,11... | collective-permute-start | bytes 442376 | tf_op jit(solution)/shard_map/ppermute | solution.py:24
  51.5 4.4 %collective-permute-start.11 = (bf16[192,384]{1,0:T(8,128)(2,1)}, bf16[192,384]{1,0:T(8,128)(2,1)S(1)}, u32[]{:S(2)}, u32[]{:S(2)}) collective-permute-start(bf16[192,384]{1,0:T(8,128)(2,1)} %get-tuple-element.28), channel_id=1, source_target_pairs={{0,2},{1,3},{2,0},{3,1},{4,6},{5,7},{6,4},{7,5},{8,10},{9,11},{10,... | collective-permute-start | bytes 442376 | tf_op jit(solution)/shard_map/ppermute | solution.py:24
  55.9 2.1 %collective-permute-start.12 = (bf16[192,384]{1,0:T(8,128)(2,1)}, bf16[192,384]{1,0:T(8,128)(2,1)S(1)}, u32[]{:S(2)}, u32[]{:S(2)}) collective-permute-start(bf16[192,384]{1,0:T(8,128)(2,1)} %get-tuple-element.29), channel_id=1, source_target_pairs={{0,3},{1,2},{2,1},{3,0},{4,7},{5,6},{6,5},{7,4},{8,11},{9,10},{10,... | collective-permute-start | bytes 442376 | tf_op jit(solution)/shard_map/ppermute | solution.py:24
  58.0 4.6 %collective-permute-start.7 = (bf16[2048,256]{1,0:T(8,128)(2,1)}, bf16[2048,256]{1,0:T(8,128)(2,1)S(1)}, u32[]{:S(2)}, u32[]{:S(2)}) collective-permute-start(bf16[2048,256]{1,0:T(8,128)(2,1)} %get-tuple-element.25.w0), channel_id=1, source_target_pairs={{0,24},{8,16},{16,8},{24,0},{1,25},{9,17},{17,9},{25,1},{2,26},{10... | collective-permute-start | bytes 3145736 | tf_op jit(solution)/shard_map/ppermute | solution.py:24
  62.6 1.9 %collective-permute-start.6 = (bf16[2048,256]{1,0:T(8,128)(2,1)}, bf16[2048,256]{1,0:T(8,128)(2,1)S(1)}, u32[]{:S(2)}, u32[]{:S(2)}) collective-permute-start(bf16[2048,256]{1,0:T(8,128)(2,1)} %get-tuple-element.25.w0), channel_id=1, source_target_pairs={{0,8},{8,0},{16,24},{24,16},{1,9},{9,1},{17,25},{25,17},{2,10},{10... | collective-permute-start | bytes 3145736 | tf_op jit(solution)/shard_map/ppermute | solution.py:24
  64.7 12.0 %collective-permute-start.13 = (bf16[192,384]{1,0:T(8,128)(2,1)S(1)}, bf16[192,384]{1,0:T(8,128)(2,1)S(1)}, u32[]{:S(2)}, u32[]{:S(2)}) collective-permute-start(bf16[192,384]{1,0:T(8,128)(2,1)S(1)} %reduce_rows.1.s_mine), channel_id=1, source_target_pairs={{0,4},{4,0},{1,5},{5,1},{2,6},{6,2},{3,7},{7,3},{8,12},{12,8},{9,1... | collective-permute-start | bytes 442376 | tf_op jit(solution)/shard_map/ppermute | solution.py:24
  76.7 1.9 %load.3.after.out_grad = bf16[768,2048]{1,0:T(8,128)(2,1)S(1)} custom-call(bf16[768,2048]{1,0:T(8,128)(2,1)} %refs_0_.3), custom_call_target="tpu_custom_call" | custom-call | tf_op jit(solution)/shard_map/load/pallas_call | solution.py:121
  79.2 0.8 rates.1.per_row
  80.0 4.8 %collective-permute-done.7.w3 = bf16[2048,256]{1,0:T(8,128)(2,1)S(1)} collective-permute-done((bf16[2048,256]{1,0:T(8,128)(2,1)}, bf16[2048,256]{1,0:T(8,128)(2,1)S(1)}, u32[]{:S(2)}, u32[]{:S(2)}) %collective-permute-start.7) | collective-permute-done | bytes 1048608 | tf_op jit(solution)/shard_map/ppermute | solution.py:24
  84.9 1.9 %collective-permute-start.8 = (bf16[1024,256]{1,0:T(8,128)(2,1)S(1)}, bf16[1024,256]{1,0:T(8,128)(2,1)S(1)}, u32[]{:S(2)}, u32[]{:S(2)}) collective-permute-start(bf16[1024,256]{1,0:T(8,128)(2,1)S(1)} %slice.8), channel_id=1, source_target_pairs={{0,8},{8,0},{16,24},{24,16},{1,9},{9,1},{17,25},{25,17},{2,10},{10... | collective-permute-start | bytes 1572872 | tf_op jit(solution)/shard_map/ppermute | solution.py:24
  86.8 1.0 collective-permute-done.6.w1
  87.9 3.5 %collective-permute-start.9 = (bf16[1024,256]{1,0:T(8,128)(2,1)S(1)}, bf16[1024,256]{1,0:T(8,128)(2,1)S(1)}, u32[]{:S(2)}, u32[]{:S(2)}) collective-permute-start(bf16[1024,256]{1,0:T(8,128)(2,1)S(1)} %slice.9), channel_id=1, source_target_pairs={{0,24},{8,16},{16,8},{24,0},{1,25},{9,17},{17,9},{25,1},{2,26},{10... | collective-permute-start | bytes 1572872 | tf_op jit(solution)/shard_map/ppermute | solution.py:24
  91.4 0.8 deltas.1.d0
  92.3 1.9 %collective-permute-start.14 = (bf16[208,384]{1,0:T(8,128)(2,1)S(1)}, bf16[208,384]{1,0:T(8,128)(2,1)S(1)}, u32[]{:S(2)}, u32[]{:S(2)}) collective-permute-start(bf16[208,384]{1,0:T(8,128)(2,1)S(1)} %deltas.1.d0), channel_id=1, source_target_pairs={{0,1},{1,0},{2,3},{3,2},{4,5},{5,4},{6,7},{7,6},{8,9},{9,8},{10,11... | collective-permute-start | bytes 479240 | tf_op jit(solution)/shard_map/ppermute | solution.py:24
  94.2 5.6 %collective-permute-start.15 = (bf16[208,384]{1,0:T(8,128)(2,1)S(1)}, bf16[208,384]{1,0:T(8,128)(2,1)S(1)}, u32[]{:S(2)}, u32[]{:S(2)}) collective-permute-start(bf16[208,384]{1,0:T(8,128)(2,1)S(1)} %deltas.1.d0), channel_id=1, source_target_pairs={{0,2},{1,3},{2,0},{3,1},{4,6},{5,7},{6,4},{7,5},{8,10},{9,11},{10,... | collective-permute-start | bytes 479240 | tf_op jit(solution)/shard_map/ppermute | solution.py:24
  99.8 2.1 %collective-permute-start.16 = (bf16[208,384]{1,0:T(8,128)(2,1)S(1)}, bf16[208,384]{1,0:T(8,128)(2,1)S(1)}, u32[]{:S(2)}, u32[]{:S(2)}) collective-permute-start(bf16[208,384]{1,0:T(8,128)(2,1)S(1)} %deltas.1.d0), channel_id=1, source_target_pairs={{0,3},{1,2},{2,1},{3,0},{4,7},{5,6},{6,5},{7,4},{8,11},{9,10},{10,... | collective-permute-start | bytes 479240 | tf_op jit(solution)/shard_map/ppermute | solution.py:24
  101.9 1.3 collective-permute-done.15.d2
  103.2 4.4 %collective-permute-done.16.d3 = bf16[208,384]{1,0:T(8,128)(2,1)S(1)} collective-permute-done((bf16[208,384]{1,0:T(8,128)(2,1)S(1)}, bf16[208,384]{1,0:T(8,128)(2,1)S(1)}, u32[]{:S(2)}, u32[]{:S(2)}) %collective-permute-start.16) | collective-permute-done | bytes 159776 | tf_op jit(solution)/shard_map/ppermute | solution.py:24
  107.6 0.8 copy-done.3
  108.3 0.8 copy-done.4
  109.2 4.9 %weight_grads.1 = (bf16[3072,128]{1,0:T(8,128)(2,1)S(1)}, bf16[3072,128]{1,0:T(8,128)(2,1)S(1)}) custom-call(s32[3]{0:T(128)S(1)} %pad_add_fusion.ids, bf16[768,2048]{1,0:T(8,128)(2,1)S(1)} %get-tuple-element.23.tokens, bf16[768,2048]{1,0:T(8,128)(2,1)S(1)} %load.3.after.out_grad, f32[768,128]{1,0:T(8,128)S(1)} %rates.1.per_row, ...), custom_call_target="tpu_custom_call" | custom-call | flops 1207959552 | bytes 10485760 | tf_op jit(solution)/shard_map/weight_grads/pallas_call | solution.py:296
  114.1 5.5 %collective-permute-start.17 = (bf16[3072,128]{1,0:T(8,128)(2,1)S(1)}, bf16[3072,128]{1,0:T(8,128)(2,1)S(1)}, u32[]{:S(2)}, u32[]{:S(2)}) collective-permute-start(bf16[3072,128]{1,0:T(8,128)(2,1)S(1)} %get-tuple-element.31), channel_id=1, source_target_pairs={{0,32},{32,0},{1,33},{33,1},{2,34},{34,2},{3,35},{35,3},{4,36},{36... | collective-permute-start | bytes 2359304 | tf_op jit(solution)/shard_map/ppermute | solution.py:24
  119.6 1.9 %collective-permute-done.17.received = bf16[3072,128]{1,0:T(8,128)(2,1)S(1)} collective-permute-done((bf16[3072,128]{1,0:T(8,128)(2,1)S(1)}, bf16[3072,128]{1,0:T(8,128)(2,1)S(1)}, u32[]{:S(2)}, u32[]{:S(2)}) %collective-permute-start.17) | collective-permute-done | bytes 786464 | tf_op jit(solution)/shard_map/ppermute | solution.py:24
  121.5 0.1 core_sum.1.after
  121.6 3.2 %collective-permute-start.21 = (bf16[1728,128]{1,0:T(8,128)(2,1)S(1)}, bf16[1728,128]{1,0:T(8,128)(2,1)S(1)}, u32[]{:S(2)}, u32[]{:S(2)}) collective-permute-start(bf16[1728,128]{1,0:T(8,128)(2,1)S(1)} %core_sum.1.after), channel_id=1, source_target_pairs={{0,64},{64,0},{128,192},{192,128},{256,320},{320,256},{384,448},{4... | collective-permute-start | bytes 1327112 | tf_op jit(solution)/shard_map/ppermute | solution.py:24
  124.8 0.6 row_order.1.y0
  125.4 3.0 %collective-permute-start.18 = (bf16[832,256]{1,0:T(8,128)(2,1)S(1)}, bf16[832,256]{1,0:T(8,128)(2,1)S(1)}, u32[]{:S(2)}, u32[]{:S(2)}) collective-permute-start(bf16[832,256]{1,0:T(8,128)(2,1)S(1)} %row_order.1.y0), channel_id=1, source_target_pairs={{0,8},{8,0},{16,24},{24,16},{1,9},{9,1},{17,25},{25,17},{2,10},{10... | collective-permute-start | bytes 1277960 | tf_op jit(solution)/shard_map/ppermute | solution.py:24
  128.4 3.7 %collective-permute-start.19 = (bf16[832,256]{1,0:T(8,128)(2,1)S(1)}, bf16[832,256]{1,0:T(8,128)(2,1)S(1)}, u32[]{:S(2)}, u32[]{:S(2)}) collective-permute-start(bf16[832,256]{1,0:T(8,128)(2,1)S(1)} %row_order.1.y0), channel_id=1, source_target_pairs={{0,16},{8,24},{16,0},{24,8},{1,17},{9,25},{17,1},{25,9},{2,18},{10... | collective-permute-start | bytes 1277960 | tf_op jit(solution)/shard_map/ppermute | solution.py:24
  132.1 2.9 %collective-permute-start.20 = (bf16[832,256]{1,0:T(8,128)(2,1)S(1)}, bf16[832,256]{1,0:T(8,128)(2,1)S(1)}, u32[]{:S(2)}, u32[]{:S(2)}) collective-permute-start(bf16[832,256]{1,0:T(8,128)(2,1)S(1)} %row_order.1.y0), channel_id=1, source_target_pairs={{0,24},{8,16},{16,8},{24,0},{1,25},{9,17},{17,9},{25,1},{2,26},{10... | collective-permute-start | bytes 1277960 | tf_op jit(solution)/shard_map/ppermute | solution.py:24
  135.0 0.1 pair_sum.1
  135.2 8.7 %collective-permute-start.22 = (bf16[384,128]{1,0:T(8,128)(2,1)S(1)}, bf16[384,128]{1,0:T(8,128)(2,1)S(1)}, u32[]{:S(2)}, u32[]{:S(2)}) collective-permute-start(bf16[384,128]{1,0:T(8,128)(2,1)S(1)} %get-tuple-element.32.after), channel_id=1, source_target_pairs={{0,256},{64,320},{128,384},{192,448},{256,0},{320,64},{384,128},{4... | collective-permute-start | bytes 294920 | tf_op jit(solution)/shard_map/ppermute | solution.py:24
  143.9 1.9 %collective-permute-start.23 = (bf16[384,128]{1,0:T(8,128)(2,1)S(1)}, bf16[384,128]{1,0:T(8,128)(2,1)S(1)}, u32[]{:S(2)}, u32[]{:S(2)}) collective-permute-start(bf16[384,128]{1,0:T(8,128)(2,1)S(1)} %get-tuple-element.35), channel_id=1, source_target_pairs={{0,128},{64,192},{128,0},{192,64},{256,384},{320,448},{384,256},{4... | collective-permute-start | bytes 294920 | tf_op jit(solution)/shard_map/ppermute | solution.py:24
  145.9 4.0 %collective-permute-start.24 = (bf16[384,128]{1,0:T(8,128)(2,1)S(1)}, bf16[384,128]{1,0:T(8,128)(2,1)S(1)}, u32[]{:S(2)}, u32[]{:S(2)}) collective-permute-start(bf16[384,128]{1,0:T(8,128)(2,1)S(1)} %get-tuple-element.36), channel_id=1, source_target_pairs={{0,384},{64,448},{128,256},{192,320},{256,128},{320,192},{384,0},{... | collective-permute-start | bytes 294920 | tf_op jit(solution)/shard_map/ppermute | solution.py:24
  149.9 4.7 %collective-permute-done.20.y3 = bf16[832,256]{1,0:T(8,128)(2,1)S(1)} collective-permute-done((bf16[832,256]{1,0:T(8,128)(2,1)S(1)}, bf16[832,256]{1,0:T(8,128)(2,1)S(1)}, u32[]{:S(2)}, u32[]{:S(2)}) %collective-permute-start.20) | collective-permute-done | bytes 426016 | tf_op jit(solution)/shard_map/ppermute | solution.py:24
  154.5 8.5 %token_grads.1 = (bf16[768,2048]{1,0:T(8,128)(2,1)}, f32[48,128]{1,0:T(8,128)}) custom-call(s32[3]{0:T(128)S(1)} %pad_add_fusion.ids, bf16[2048,256]{1,0:T(8,128)(2,1)} %get-tuple-element.25.w0, bf16[2048,256]{1,0:T(8,128)(2,1)} %copy-done.2, bf16[1024,256]{1,0:T(8,128)(2,1)} %copy-done.3, bf16[1024,256]{1,0:T(8,128)(2,1)} %copy-done.4, ...), custom_call_target="tpu_custom_call" | custom-call | flops 3221225472 | bytes 12582912 | tf_op jit(solution)/shard_map/token_grads/pallas_call | solution.py:431
  163.1 0.8 last_sum.1
  (32 shorter events, 0.3 us)
Async XLA Ops:
  1.7 19.4 %collective-permute-start = (bf16[128,384]{1,0:T(8,128)(2,1)S(1)}, bf16[128,384]{1,0:T(8,128)(2,1)S(1)}, u32[]{:S(2)}, u32[]{:S(2)}) collective-permute-start(bf16[128,384]{1,0:T(8,128)(2,1)S(1)} %own_tiles.1.a), channel_id=1, source_target_pairs={{0,256},{64,320},{128,384},{192,448},{256,0},{320,64},{384,128},{4... | collective-permute-start | bytes 294920 | tf_op jit(solution)/shard_map/ppermute | solution.py:24
  11.4 9.7 %collective-permute-start.1 = (bf16[128,384]{1,0:T(8,128)(2,1)S(1)}, bf16[128,384]{1,0:T(8,128)(2,1)S(1)}, u32[]{:S(2)}, u32[]{:S(2)}) collective-permute-start(bf16[128,384]{1,0:T(8,128)(2,1)S(1)} %own_tiles.1.a), channel_id=1, source_target_pairs={{0,128},{64,192},{128,0},{192,64},{256,384},{320,448},{384,256},{4... | collective-permute-start | bytes 294920 | tf_op jit(solution)/shard_map/ppermute | solution.py:24
  16.3 11.1 %collective-permute-start.2 = (bf16[128,384]{1,0:T(8,128)(2,1)S(1)}, bf16[128,384]{1,0:T(8,128)(2,1)S(1)}, u32[]{:S(2)}, u32[]{:S(2)}) collective-permute-start(bf16[128,384]{1,0:T(8,128)(2,1)S(1)} %own_tiles.1.a), channel_id=1, source_target_pairs={{0,384},{64,448},{128,256},{192,320},{256,128},{320,192},{384,0},{... | collective-permute-start | bytes 294920 | tf_op jit(solution)/shard_map/ppermute | solution.py:24
  27.4 9.6 %collective-permute-start.3 = (bf16[512,384]{1,0:T(8,128)(2,1)S(1)}, bf16[512,384]{1,0:T(8,128)(2,1)S(1)}, u32[]{:S(2)}, u32[]{:S(2)}) collective-permute-start(bf16[512,384]{1,0:T(8,128)(2,1)S(1)} %join.1.m0), channel_id=1, source_target_pairs={{0,64},{64,0},{128,192},{192,128},{256,320},{320,256},{384,448},{4... | collective-permute-start | bytes 1179656 | tf_op jit(solution)/shard_map/ppermute | solution.py:24
  31.0 12.1 %collective-permute-start.4 = (bf16[512,384]{1,0:T(8,128)(2,1)S(1)}, bf16[512,384]{1,0:T(8,128)(2,1)S(1)}, u32[]{:S(2)}, u32[]{:S(2)}) collective-permute-start(bf16[512,384]{1,0:T(8,128)(2,1)S(1)} %join.1.m0), channel_id=1, source_target_pairs={{0,32},{32,0},{1,33},{33,1},{2,34},{34,2},{3,35},{35,3},{4,36},{36... | collective-permute-start | bytes 1179656 | tf_op jit(solution)/shard_map/ppermute | solution.py:24
  37.0 7.5 %collective-permute-start.5 = (bf16[512,384]{1,0:T(8,128)(2,1)S(1)}, bf16[512,384]{1,0:T(8,128)(2,1)S(1)}, u32[]{:S(2)}, u32[]{:S(2)}) collective-permute-start(bf16[512,384]{1,0:T(8,128)(2,1)S(1)} %collective-permute-done.3.m1), channel_id=1, source_target_pairs={{0,32},{32,0},{1,33},{33,1},{2,34},{34,2},{3,35},{35,3},{4,36},{36... | collective-permute-start | bytes 1179656 | tf_op jit(solution)/shard_map/ppermute | solution.py:24
  48.4 16.2 %collective-permute-start.10 = (bf16[192,384]{1,0:T(8,128)(2,1)}, bf16[192,384]{1,0:T(8,128)(2,1)S(1)}, u32[]{:S(2)}, u32[]{:S(2)}) collective-permute-start(bf16[192,384]{1,0:T(8,128)(2,1)} %get-tuple-element.27), channel_id=1, source_target_pairs={{0,1},{1,0},{2,3},{3,2},{4,5},{5,4},{6,7},{7,6},{8,9},{9,8},{10,11... | collective-permute-start | bytes 442376 | tf_op jit(solution)/shard_map/ppermute | solution.py:24
  51.5 13.1 %collective-permute-start.11 = (bf16[192,384]{1,0:T(8,128)(2,1)}, bf16[192,384]{1,0:T(8,128)(2,1)S(1)}, u32[]{:S(2)}, u32[]{:S(2)}) collective-permute-start(bf16[192,384]{1,0:T(8,128)(2,1)} %get-tuple-element.28), channel_id=1, source_target_pairs={{0,2},{1,3},{2,0},{3,1},{4,6},{5,7},{6,4},{7,5},{8,10},{9,11},{10,... | collective-permute-start | bytes 442376 | tf_op jit(solution)/shard_map/ppermute | solution.py:24
  55.9 8.7 %collective-permute-start.12 = (bf16[192,384]{1,0:T(8,128)(2,1)}, bf16[192,384]{1,0:T(8,128)(2,1)S(1)}, u32[]{:S(2)}, u32[]{:S(2)}) collective-permute-start(bf16[192,384]{1,0:T(8,128)(2,1)} %get-tuple-element.29), channel_id=1, source_target_pairs={{0,3},{1,2},{2,1},{3,0},{4,7},{5,6},{6,5},{7,4},{8,11},{9,10},{10,... | collective-permute-start | bytes 442376 | tf_op jit(solution)/shard_map/ppermute | solution.py:24
  58.0 26.9 %collective-permute-start.7 = (bf16[2048,256]{1,0:T(8,128)(2,1)}, bf16[2048,256]{1,0:T(8,128)(2,1)S(1)}, u32[]{:S(2)}, u32[]{:S(2)}) collective-permute-start(bf16[2048,256]{1,0:T(8,128)(2,1)} %get-tuple-element.25.w0), channel_id=1, source_target_pairs={{0,24},{8,16},{16,8},{24,0},{1,25},{9,17},{17,9},{25,1},{2,26},{10... | collective-permute-start | bytes 3145736 | tf_op jit(solution)/shard_map/ppermute | solution.py:24
  62.6 25.3 %collective-permute-start.6 = (bf16[2048,256]{1,0:T(8,128)(2,1)}, bf16[2048,256]{1,0:T(8,128)(2,1)S(1)}, u32[]{:S(2)}, u32[]{:S(2)}) collective-permute-start(bf16[2048,256]{1,0:T(8,128)(2,1)} %get-tuple-element.25.w0), channel_id=1, source_target_pairs={{0,8},{8,0},{16,24},{24,16},{1,9},{9,1},{17,25},{25,17},{2,10},{10... | collective-permute-start | bytes 3145736 | tf_op jit(solution)/shard_map/ppermute | solution.py:24
  64.7 13.9 %copy-start.5 = (s32[768]{0:T(1024)S(1)}, s32[768]{0:T(1024)}, u32[]{:S(2)}) copy-start(s32[768]{0:T(1024)} %param.15) | copy-start | bytes 9220
  64.7 14.6 %copy-start = (f32[6144]{0:T(1024)S(1)}, f32[6144]{0:T(1024)}, u32[]{:S(2)}) copy-start(f32[6144]{0:T(1024)} %param.13) | copy-start | bytes 73732
  64.7 26.7 %collective-permute-start.13 = (bf16[192,384]{1,0:T(8,128)(2,1)S(1)}, bf16[192,384]{1,0:T(8,128)(2,1)S(1)}, u32[]{:S(2)}, u32[]{:S(2)}) collective-permute-start(bf16[192,384]{1,0:T(8,128)(2,1)S(1)} %reduce_rows.1.s_mine), channel_id=1, source_target_pairs={{0,4},{4,0},{1,5},{5,1},{2,6},{6,2},{3,7},{7,3},{8,12},{12,8},{9,1... | collective-permute-start | bytes 442376 | tf_op jit(solution)/shard_map/ppermute | solution.py:24
  84.9 7.4 %copy-start.1 = (bf16[2048,256]{1,0:T(8,128)(2,1)}, bf16[2048,256]{1,0:T(8,128)(2,1)S(1)}, u32[]{:S(2)}) copy-start(bf16[2048,256]{1,0:T(8,128)(2,1)S(1)} %collective-permute-done.7.w3) | copy-start | bytes 3145732
  84.9 22.6 %collective-permute-start.8 = (bf16[1024,256]{1,0:T(8,128)(2,1)S(1)}, bf16[1024,256]{1,0:T(8,128)(2,1)S(1)}, u32[]{:S(2)}, u32[]{:S(2)}) collective-permute-start(bf16[1024,256]{1,0:T(8,128)(2,1)S(1)} %slice.8), channel_id=1, source_target_pairs={{0,8},{8,0},{16,24},{24,16},{1,9},{9,1},{17,25},{25,17},{2,10},{10... | collective-permute-start | bytes 1572872 | tf_op jit(solution)/shard_map/ppermute | solution.py:24
  87.9 4.4 %copy-start.2 = (bf16[2048,256]{1,0:T(8,128)(2,1)}, bf16[2048,256]{1,0:T(8,128)(2,1)S(1)}, u32[]{:S(2)}) copy-start(bf16[2048,256]{1,0:T(8,128)(2,1)S(1)} %collective-permute-done.6.w1) | copy-start | bytes 3145732
  87.9 19.6 %collective-permute-start.9 = (bf16[1024,256]{1,0:T(8,128)(2,1)S(1)}, bf16[1024,256]{1,0:T(8,128)(2,1)S(1)}, u32[]{:S(2)}, u32[]{:S(2)}) collective-permute-start(bf16[1024,256]{1,0:T(8,128)(2,1)S(1)} %slice.9), channel_id=1, source_target_pairs={{0,24},{8,16},{16,8},{24,0},{1,25},{9,17},{17,9},{25,1},{2,26},{10... | collective-permute-start | bytes 1572872 | tf_op jit(solution)/shard_map/ppermute | solution.py:24
  92.3 9.6 %collective-permute-start.14 = (bf16[208,384]{1,0:T(8,128)(2,1)S(1)}, bf16[208,384]{1,0:T(8,128)(2,1)S(1)}, u32[]{:S(2)}, u32[]{:S(2)}) collective-permute-start(bf16[208,384]{1,0:T(8,128)(2,1)S(1)} %deltas.1.d0), channel_id=1, source_target_pairs={{0,1},{1,0},{2,3},{3,2},{4,5},{5,4},{6,7},{7,6},{8,9},{9,8},{10,11... | collective-permute-start | bytes 479240 | tf_op jit(solution)/shard_map/ppermute | solution.py:24
  94.2 9.0 %collective-permute-start.15 = (bf16[208,384]{1,0:T(8,128)(2,1)S(1)}, bf16[208,384]{1,0:T(8,128)(2,1)S(1)}, u32[]{:S(2)}, u32[]{:S(2)}) collective-permute-start(bf16[208,384]{1,0:T(8,128)(2,1)S(1)} %deltas.1.d0), channel_id=1, source_target_pairs={{0,2},{1,3},{2,0},{3,1},{4,6},{5,7},{6,4},{7,5},{8,10},{9,11},{10,... | collective-permute-start | bytes 479240 | tf_op jit(solution)/shard_map/ppermute | solution.py:24
  99.8 7.8 %collective-permute-start.16 = (bf16[208,384]{1,0:T(8,128)(2,1)S(1)}, bf16[208,384]{1,0:T(8,128)(2,1)S(1)}, u32[]{:S(2)}, u32[]{:S(2)}) collective-permute-start(bf16[208,384]{1,0:T(8,128)(2,1)S(1)} %deltas.1.d0), channel_id=1, source_target_pairs={{0,3},{1,2},{2,1},{3,0},{4,7},{5,6},{6,5},{7,4},{8,11},{9,10},{10,... | collective-permute-start | bytes 479240 | tf_op jit(solution)/shard_map/ppermute | solution.py:24
  107.6 0.8 copy-start.3
  108.3 0.8 copy-start.4
  114.1 7.4 %collective-permute-start.17 = (bf16[3072,128]{1,0:T(8,128)(2,1)S(1)}, bf16[3072,128]{1,0:T(8,128)(2,1)S(1)}, u32[]{:S(2)}, u32[]{:S(2)}) collective-permute-start(bf16[3072,128]{1,0:T(8,128)(2,1)S(1)} %get-tuple-element.31), channel_id=1, source_target_pairs={{0,32},{32,0},{1,33},{33,1},{2,34},{34,2},{3,35},{35,3},{4,36},{36... | collective-permute-start | bytes 2359304 | tf_op jit(solution)/shard_map/ppermute | solution.py:24
  121.6 13.4 %collective-permute-start.21 = (bf16[1728,128]{1,0:T(8,128)(2,1)S(1)}, bf16[1728,128]{1,0:T(8,128)(2,1)S(1)}, u32[]{:S(2)}, u32[]{:S(2)}) collective-permute-start(bf16[1728,128]{1,0:T(8,128)(2,1)S(1)} %core_sum.1.after), channel_id=1, source_target_pairs={{0,64},{64,0},{128,192},{192,128},{256,320},{320,256},{384,448},{4... | collective-permute-start | bytes 1327112 | tf_op jit(solution)/shard_map/ppermute | solution.py:24
  125.4 20.5 %collective-permute-start.18 = (bf16[832,256]{1,0:T(8,128)(2,1)S(1)}, bf16[832,256]{1,0:T(8,128)(2,1)S(1)}, u32[]{:S(2)}, u32[]{:S(2)}) collective-permute-start(bf16[832,256]{1,0:T(8,128)(2,1)S(1)} %row_order.1.y0), channel_id=1, source_target_pairs={{0,8},{8,0},{16,24},{24,16},{1,9},{9,1},{17,25},{25,17},{2,10},{10... | collective-permute-start | bytes 1277960 | tf_op jit(solution)/shard_map/ppermute | solution.py:24
  128.4 21.4 %collective-permute-start.19 = (bf16[832,256]{1,0:T(8,128)(2,1)S(1)}, bf16[832,256]{1,0:T(8,128)(2,1)S(1)}, u32[]{:S(2)}, u32[]{:S(2)}) collective-permute-start(bf16[832,256]{1,0:T(8,128)(2,1)S(1)} %row_order.1.y0), channel_id=1, source_target_pairs={{0,16},{8,24},{16,0},{24,8},{1,17},{9,25},{17,1},{25,9},{2,18},{10... | collective-permute-start | bytes 1277960 | tf_op jit(solution)/shard_map/ppermute | solution.py:24
  132.1 22.4 %collective-permute-start.20 = (bf16[832,256]{1,0:T(8,128)(2,1)S(1)}, bf16[832,256]{1,0:T(8,128)(2,1)S(1)}, u32[]{:S(2)}, u32[]{:S(2)}) collective-permute-start(bf16[832,256]{1,0:T(8,128)(2,1)S(1)} %row_order.1.y0), channel_id=1, source_target_pairs={{0,24},{8,16},{16,8},{24,0},{1,25},{9,17},{17,9},{25,1},{2,26},{10... | collective-permute-start | bytes 1277960 | tf_op jit(solution)/shard_map/ppermute | solution.py:24
  135.2 27.9 %collective-permute-start.22 = (bf16[384,128]{1,0:T(8,128)(2,1)S(1)}, bf16[384,128]{1,0:T(8,128)(2,1)S(1)}, u32[]{:S(2)}, u32[]{:S(2)}) collective-permute-start(bf16[384,128]{1,0:T(8,128)(2,1)S(1)} %get-tuple-element.32.after), channel_id=1, source_target_pairs={{0,256},{64,320},{128,384},{192,448},{256,0},{320,64},{384,128},{4... | collective-permute-start | bytes 294920 | tf_op jit(solution)/shard_map/ppermute | solution.py:24
  143.9 19.1 %collective-permute-start.23 = (bf16[384,128]{1,0:T(8,128)(2,1)S(1)}, bf16[384,128]{1,0:T(8,128)(2,1)S(1)}, u32[]{:S(2)}, u32[]{:S(2)}) collective-permute-start(bf16[384,128]{1,0:T(8,128)(2,1)S(1)} %get-tuple-element.35), channel_id=1, source_target_pairs={{0,128},{64,192},{128,0},{192,64},{256,384},{320,448},{384,256},{4... | collective-permute-start | bytes 294920 | tf_op jit(solution)/shard_map/ppermute | solution.py:24
  145.9 17.2 %collective-permute-start.24 = (bf16[384,128]{1,0:T(8,128)(2,1)S(1)}, bf16[384,128]{1,0:T(8,128)(2,1)S(1)}, u32[]{:S(2)}, u32[]{:S(2)}) collective-permute-start(bf16[384,128]{1,0:T(8,128)(2,1)S(1)} %get-tuple-element.36), channel_id=1, source_target_pairs={{0,384},{64,448},{128,256},{192,320},{256,128},{320,192},{384,0},{... | collective-permute-start | bytes 294920 | tf_op jit(solution)/shard_map/ppermute | solution.py:24

commit v7 on v6

--- a/solution.py
+++ b/solution.py
@@ -309,7 +309,7 @@
         compiler_params=params(),
         cost_estimate=work(2 * CAP * D * 3 * T, 10),
         name="weight_grads",
-    )(ids, tokens, out_grad, per_row, *parts, *in_hbm(*after))
+    )(ids, tokens, out_grad, per_row, *parts, *after)
 
 
 def rows_kernel(ids, d0, d1, d2, d3, after, out):

time: 165 us -> 164 us (level)
  no operation moved by 1% of the time
where the time goes in v7:
time: 164 us; the launch traced here: 162 us
  starting transfers between devices  107 us (65%)
  waiting for transfers between devices  27.1 us (17%)
  Pallas kernels  26.5 us (16%)
  between operations  1.75 us (1%)
    ppermute x25, starting transfers between devices, swap(): return lax.ppermute(value, axis, [(i, i ^ mask) for i in range(size)])  107 us
    ppermute x25, waiting for transfers between devices, swap(): return lax.ppermute(value, axis, [(i, i ^ mask) for i in range(size)])  27.1 us
    pallas_call x1, Pallas kernels, token_grads(): pl.pallas_call(token_grad_kernel, grid_spec=pltpu.PrefetchScalarGridSpec(...  8.5 us
    pallas_call x1, Pallas kernels, weight_grads(): pl.pallas_call(weight_grad_kernel, grid_spec=pltpu.PrefetchScalarGridSpec...  4.93 us
    pallas_call x2, Pallas kernels, load(): pl.pallas_call(load_kernel, out_shape=[pltpu.VMEM(array.shape, array.dtyp...  4.77 us
    pallas_call x1, Pallas kernels, forward(): pl.pallas_call(forward_kernel, grid_spec=pltpu.PrefetchScalarGridSpec(num...  3.9 us
  transfers between devices with their start and end apart: 25, of which 9 were waited for; matrix products, arithmetic and copies ran while one was open for 0% of the time, Pallas kernels for 10%

profile of v7, /device:TPU:1, one launch (start us, length us, event | category | flops | bytes accessed | tf_op | source)
XLA Modules:
  0.0 162.3 jit_solution(2107031739599856100)
XLA Ops:
  0.6 0.1 pad_add_fusion.ids
  0.7 1.0 own_tiles.1.a
  1.7 9.6 %collective-permute-start = (bf16[128,384]{1,0:T(8,128)(2,1)S(1)}, bf16[128,384]{1,0:T(8,128)(2,1)S(1)}, u32[]{:S(2)}, u32[]{:S(2)}) collective-permute-start(bf16[128,384]{1,0:T(8,128)(2,1)S(1)} %own_tiles.1.a), channel_id=1, source_target_pairs={{0,256},{64,320},{128,384},{192,448},{256,0},{320,64},{384,128},{4... | collective-permute-start | bytes 294920 | tf_op jit(solution)/shard_map/ppermute | solution.py:24
  11.4 4.9 %collective-permute-start.1 = (bf16[128,384]{1,0:T(8,128)(2,1)S(1)}, bf16[128,384]{1,0:T(8,128)(2,1)S(1)}, u32[]{:S(2)}, u32[]{:S(2)}) collective-permute-start(bf16[128,384]{1,0:T(8,128)(2,1)S(1)} %own_tiles.1.a), channel_id=1, source_target_pairs={{0,128},{64,192},{128,0},{192,64},{256,384},{320,448},{384,256},{4... | collective-permute-start | bytes 294920 | tf_op jit(solution)/shard_map/ppermute | solution.py:24
  16.3 1.9 %collective-permute-start.2 = (bf16[128,384]{1,0:T(8,128)(2,1)S(1)}, bf16[128,384]{1,0:T(8,128)(2,1)S(1)}, u32[]{:S(2)}, u32[]{:S(2)}) collective-permute-start(bf16[128,384]{1,0:T(8,128)(2,1)S(1)} %own_tiles.1.a), channel_id=1, source_target_pairs={{0,384},{64,448},{128,256},{192,320},{256,128},{320,192},{384,0},{... | collective-permute-start | bytes 294920 | tf_op jit(solution)/shard_map/ppermute | solution.py:24
  18.2 2.9 %load.2 = (bf16[768,2048]{1,0:T(8,128)(2,1)S(1)}, bf16[768,2048]{1,0:T(8,128)(2,1)S(1)}) custom-call(bf16[768,2048]{1,0:T(8,128)(2,1)} %refs_0_.2, bf16[768,2048]{1,0:T(8,128)(2,1)} %refs_0_.3), custom_call_target="tpu_custom_call" | custom-call | tf_op jit(solution)/shard_map/load/pallas_call | solution.py:121
  21.1 6.2 %collective-permute-done.2.d = bf16[128,384]{1,0:T(8,128)(2,1)S(1)} collective-permute-done((bf16[128,384]{1,0:T(8,128)(2,1)S(1)}, bf16[128,384]{1,0:T(8,128)(2,1)S(1)}, u32[]{:S(2)}, u32[]{:S(2)}) %collective-permute-start.2) | collective-permute-done | bytes 98336 | tf_op jit(solution)/shard_map/ppermute | solution.py:24
  27.4 3.6 %collective-permute-start.3 = (bf16[512,384]{1,0:T(8,128)(2,1)S(1)}, bf16[512,384]{1,0:T(8,128)(2,1)S(1)}, u32[]{:S(2)}, u32[]{:S(2)}) collective-permute-start(bf16[512,384]{1,0:T(8,128)(2,1)S(1)} %join.1.m0), channel_id=1, source_target_pairs={{0,64},{64,0},{128,192},{192,128},{256,320},{320,256},{384,448},{4... | collective-permute-start | bytes 1179656 | tf_op jit(solution)/shard_map/ppermute | solution.py:24
  31.0 4.6 %collective-permute-start.4 = (bf16[512,384]{1,0:T(8,128)(2,1)S(1)}, bf16[512,384]{1,0:T(8,128)(2,1)S(1)}, u32[]{:S(2)}, u32[]{:S(2)}) collective-permute-start(bf16[512,384]{1,0:T(8,128)(2,1)S(1)} %join.1.m0), channel_id=1, source_target_pairs={{0,32},{32,0},{1,33},{33,1},{2,34},{34,2},{3,35},{35,3},{4,36},{36... | collective-permute-start | bytes 1179656 | tf_op jit(solution)/shard_map/ppermute | solution.py:24
  35.7 1.4 collective-permute-done.3.m1
  37.0 6.1 %collective-permute-start.5 = (bf16[512,384]{1,0:T(8,128)(2,1)S(1)}, bf16[512,384]{1,0:T(8,128)(2,1)S(1)}, u32[]{:S(2)}, u32[]{:S(2)}) collective-permute-start(bf16[512,384]{1,0:T(8,128)(2,1)S(1)} %collective-permute-done.3.m1), channel_id=1, source_target_pairs={{0,32},{32,0},{1,33},{33,1},{2,34},{34,2},{3,35},{35,3},{4,36},{36... | collective-permute-start | bytes 1179656 | tf_op jit(solution)/shard_map/ppermute | solution.py:24
  43.2 1.3 collective-permute-done.5.t1
  44.5 3.9 %forward.1 = (f32[192,384]{1,0:T(8,128)S(1)}, bf16[192,384]{1,0:T(8,128)(2,1)}, bf16[192,384]{1,0:T(8,128)(2,1)}, bf16[192,384]{1,0:T(8,128)(2,1)}, bf16[2048,256]{1,0:T(8,128)(2,1)}) custom-call(s32[3]{0:T(128)S(1)} %pad_add_fusion.ids, bf16[768,2048]{1,0:T(8,128)(2,1)S(1)} %get-tuple-element.23.tokens, bf16[768,2048]{1,0:T(8,128)(2,1)S(1)} %get-tuple-element.24.out_grad, ...), custom_call_target="tpu_custom_call" | custom-call | flops 1207959552 | bytes 10485760 | tf_op jit(solution)/shard_map/forward/pallas_call | solution.py:188
  48.4 3.1 %collective-permute-start.10 = (bf16[192,384]{1,0:T(8,128)(2,1)}, bf16[192,384]{1,0:T(8,128)(2,1)S(1)}, u32[]{:S(2)}, u32[]{:S(2)}) collective-permute-start(bf16[192,384]{1,0:T(8,128)(2,1)} %get-tuple-element.27), channel_id=1, source_target_pairs={{0,1},{1,0},{2,3},{3,2},{4,5},{5,4},{6,7},{7,6},{8,9},{9,8},{10,11... | collective-permute-start | bytes 442376 | tf_op jit(solution)/shard_map/ppermute | solution.py:24
  51.5 4.4 %collective-permute-start.11 = (bf16[192,384]{1,0:T(8,128)(2,1)}, bf16[192,384]{1,0:T(8,128)(2,1)S(1)}, u32[]{:S(2)}, u32[]{:S(2)}) collective-permute-start(bf16[192,384]{1,0:T(8,128)(2,1)} %get-tuple-element.28), channel_id=1, source_target_pairs={{0,2},{1,3},{2,0},{3,1},{4,6},{5,7},{6,4},{7,5},{8,10},{9,11},{10,... | collective-permute-start | bytes 442376 | tf_op jit(solution)/shard_map/ppermute | solution.py:24
  55.9 2.1 %collective-permute-start.12 = (bf16[192,384]{1,0:T(8,128)(2,1)}, bf16[192,384]{1,0:T(8,128)(2,1)S(1)}, u32[]{:S(2)}, u32[]{:S(2)}) collective-permute-start(bf16[192,384]{1,0:T(8,128)(2,1)} %get-tuple-element.29), channel_id=1, source_target_pairs={{0,3},{1,2},{2,1},{3,0},{4,7},{5,6},{6,5},{7,4},{8,11},{9,10},{10,... | collective-permute-start | bytes 442376 | tf_op jit(solution)/shard_map/ppermute | solution.py:24
  58.0 4.6 %collective-permute-start.7 = (bf16[2048,256]{1,0:T(8,128)(2,1)}, bf16[2048,256]{1,0:T(8,128)(2,1)S(1)}, u32[]{:S(2)}, u32[]{:S(2)}) collective-permute-start(bf16[2048,256]{1,0:T(8,128)(2,1)} %get-tuple-element.25.w0), channel_id=1, source_target_pairs={{0,24},{8,16},{16,8},{24,0},{1,25},{9,17},{17,9},{25,1},{2,26},{10... | collective-permute-start | bytes 3145736 | tf_op jit(solution)/shard_map/ppermute | solution.py:24
  62.6 1.9 %collective-permute-start.6 = (bf16[2048,256]{1,0:T(8,128)(2,1)}, bf16[2048,256]{1,0:T(8,128)(2,1)S(1)}, u32[]{:S(2)}, u32[]{:S(2)}) collective-permute-start(bf16[2048,256]{1,0:T(8,128)(2,1)} %get-tuple-element.25.w0), channel_id=1, source_target_pairs={{0,8},{8,0},{16,24},{24,16},{1,9},{9,1},{17,25},{25,17},{2,10},{10... | collective-permute-start | bytes 3145736 | tf_op jit(solution)/shard_map/ppermute | solution.py:24
  64.6 0.1 reduce_rows.1.s_mine
  64.7 12.0 %collective-permute-start.13 = (bf16[192,384]{1,0:T(8,128)(2,1)S(1)}, bf16[192,384]{1,0:T(8,128)(2,1)S(1)}, u32[]{:S(2)}, u32[]{:S(2)}) collective-permute-start(bf16[192,384]{1,0:T(8,128)(2,1)S(1)} %reduce_rows.1.s_mine), channel_id=1, source_target_pairs={{0,4},{4,0},{1,5},{5,1},{2,6},{6,2},{3,7},{7,3},{8,12},{12,8},{9,1... | collective-permute-start | bytes 442376 | tf_op jit(solution)/shard_map/ppermute | solution.py:24
  76.7 1.9 %load.3.after.out_grad = bf16[768,2048]{1,0:T(8,128)(2,1)S(1)} custom-call(bf16[768,2048]{1,0:T(8,128)(2,1)} %refs_0_.3), custom_call_target="tpu_custom_call" | custom-call | tf_op jit(solution)/shard_map/load/pallas_call | solution.py:121
  79.3 0.8 rates.1.per_row
  80.0 4.8 %collective-permute-done.7.w3 = bf16[2048,256]{1,0:T(8,128)(2,1)S(1)} collective-permute-done((bf16[2048,256]{1,0:T(8,128)(2,1)}, bf16[2048,256]{1,0:T(8,128)(2,1)S(1)}, u32[]{:S(2)}, u32[]{:S(2)}) %collective-permute-start.7) | collective-permute-done | bytes 1048608 | tf_op jit(solution)/shard_map/ppermute | solution.py:24
  84.9 1.9 %collective-permute-start.8 = (bf16[1024,256]{1,0:T(8,128)(2,1)S(1)}, bf16[1024,256]{1,0:T(8,128)(2,1)S(1)}, u32[]{:S(2)}, u32[]{:S(2)}) collective-permute-start(bf16[1024,256]{1,0:T(8,128)(2,1)S(1)} %slice.8), channel_id=1, source_target_pairs={{0,8},{8,0},{16,24},{24,16},{1,9},{9,1},{17,25},{25,17},{2,10},{10... | collective-permute-start | bytes 1572872 | tf_op jit(solution)/shard_map/ppermute | solution.py:24
  86.8 1.0 collective-permute-done.6.w1
  87.9 3.5 %collective-permute-start.9 = (bf16[1024,256]{1,0:T(8,128)(2,1)S(1)}, bf16[1024,256]{1,0:T(8,128)(2,1)S(1)}, u32[]{:S(2)}, u32[]{:S(2)}) collective-permute-start(bf16[1024,256]{1,0:T(8,128)(2,1)S(1)} %slice.9), channel_id=1, source_target_pairs={{0,24},{8,16},{16,8},{24,0},{1,25},{9,17},{17,9},{25,1},{2,26},{10... | collective-permute-start | bytes 1572872 | tf_op jit(solution)/shard_map/ppermute | solution.py:24
  91.4 0.8 deltas.1.d0
  92.3 1.9 %collective-permute-start.14 = (bf16[208,384]{1,0:T(8,128)(2,1)S(1)}, bf16[208,384]{1,0:T(8,128)(2,1)S(1)}, u32[]{:S(2)}, u32[]{:S(2)}) collective-permute-start(bf16[208,384]{1,0:T(8,128)(2,1)S(1)} %deltas.1.d0), channel_id=1, source_target_pairs={{0,1},{1,0},{2,3},{3,2},{4,5},{5,4},{6,7},{7,6},{8,9},{9,8},{10,11... | collective-permute-start | bytes 479240 | tf_op jit(solution)/shard_map/ppermute | solution.py:24
  94.2 5.5 %collective-permute-start.15 = (bf16[208,384]{1,0:T(8,128)(2,1)S(1)}, bf16[208,384]{1,0:T(8,128)(2,1)S(1)}, u32[]{:S(2)}, u32[]{:S(2)}) collective-permute-start(bf16[208,384]{1,0:T(8,128)(2,1)S(1)} %deltas.1.d0), channel_id=1, source_target_pairs={{0,2},{1,3},{2,0},{3,1},{4,6},{5,7},{6,4},{7,5},{8,10},{9,11},{10,... | collective-permute-start | bytes 479240 | tf_op jit(solution)/shard_map/ppermute | solution.py:24
  99.8 2.1 %collective-permute-start.16 = (bf16[208,384]{1,0:T(8,128)(2,1)S(1)}, bf16[208,384]{1,0:T(8,128)(2,1)S(1)}, u32[]{:S(2)}, u32[]{:S(2)}) collective-permute-start(bf16[208,384]{1,0:T(8,128)(2,1)S(1)} %deltas.1.d0), channel_id=1, source_target_pairs={{0,3},{1,2},{2,1},{3,0},{4,7},{5,6},{6,5},{7,4},{8,11},{9,10},{10,... | collective-permute-start | bytes 479240 | tf_op jit(solution)/shard_map/ppermute | solution.py:24
  101.9 1.3 collective-permute-done.15.d2
  103.2 4.4 %collective-permute-done.16.d3 = bf16[208,384]{1,0:T(8,128)(2,1)S(1)} collective-permute-done((bf16[208,384]{1,0:T(8,128)(2,1)S(1)}, bf16[208,384]{1,0:T(8,128)(2,1)S(1)}, u32[]{:S(2)}, u32[]{:S(2)}) %collective-permute-start.16) | collective-permute-done | bytes 159776 | tf_op jit(solution)/shard_map/ppermute | solution.py:24
  107.6 4.9 %weight_grads.1 = (bf16[3072,128]{1,0:T(8,128)(2,1)S(1)}, bf16[3072,128]{1,0:T(8,128)(2,1)S(1)}) custom-call(s32[3]{0:T(128)S(1)} %pad_add_fusion.ids, bf16[768,2048]{1,0:T(8,128)(2,1)S(1)} %get-tuple-element.23.tokens, bf16[768,2048]{1,0:T(8,128)(2,1)S(1)} %load.3.after.out_grad, f32[768,128]{1,0:T(8,128)S(1)} %rates.1.per_row, ...), custom_call_target="tpu_custom_call" | custom-call | flops 1207959552 | bytes 10485760 | tf_op jit(solution)/shard_map/weight_grads/pallas_call | solution.py:296
  112.5 5.5 %collective-permute-start.17 = (bf16[3072,128]{1,0:T(8,128)(2,1)S(1)}, bf16[3072,128]{1,0:T(8,128)(2,1)S(1)}, u32[]{:S(2)}, u32[]{:S(2)}) collective-permute-start(bf16[3072,128]{1,0:T(8,128)(2,1)S(1)} %get-tuple-element.31), channel_id=1, source_target_pairs={{0,32},{32,0},{1,33},{33,1},{2,34},{34,2},{3,35},{35,3},{4,36},{36... | collective-permute-start | bytes 2359304 | tf_op jit(solution)/shard_map/ppermute | solution.py:24
  118.0 1.9 %collective-permute-done.17.received = bf16[3072,128]{1,0:T(8,128)(2,1)S(1)} collective-permute-done((bf16[3072,128]{1,0:T(8,128)(2,1)S(1)}, bf16[3072,128]{1,0:T(8,128)(2,1)S(1)}, u32[]{:S(2)}, u32[]{:S(2)}) %collective-permute-start.17) | collective-permute-done | bytes 786464 | tf_op jit(solution)/shard_map/ppermute | solution.py:24
  119.9 0.1 core_sum.1.after
  120.0 3.2 %collective-permute-start.21 = (bf16[1728,128]{1,0:T(8,128)(2,1)S(1)}, bf16[1728,128]{1,0:T(8,128)(2,1)S(1)}, u32[]{:S(2)}, u32[]{:S(2)}) collective-permute-start(bf16[1728,128]{1,0:T(8,128)(2,1)S(1)} %core_sum.1.after), channel_id=1, source_target_pairs={{0,64},{64,0},{128,192},{192,128},{256,320},{320,256},{384,448},{4... | collective-permute-start | bytes 1327112 | tf_op jit(solution)/shard_map/ppermute | solution.py:24
  123.2 0.6 row_order.1.y0
  123.8 3.0 %collective-permute-start.18 = (bf16[832,256]{1,0:T(8,128)(2,1)S(1)}, bf16[832,256]{1,0:T(8,128)(2,1)S(1)}, u32[]{:S(2)}, u32[]{:S(2)}) collective-permute-start(bf16[832,256]{1,0:T(8,128)(2,1)S(1)} %row_order.1.y0), channel_id=1, source_target_pairs={{0,8},{8,0},{16,24},{24,16},{1,9},{9,1},{17,25},{25,17},{2,10},{10... | collective-permute-start | bytes 1277960 | tf_op jit(solution)/shard_map/ppermute | solution.py:24
  126.9 3.7 %collective-permute-start.19 = (bf16[832,256]{1,0:T(8,128)(2,1)S(1)}, bf16[832,256]{1,0:T(8,128)(2,1)S(1)}, u32[]{:S(2)}, u32[]{:S(2)}) collective-permute-start(bf16[832,256]{1,0:T(8,128)(2,1)S(1)} %row_order.1.y0), channel_id=1, source_target_pairs={{0,16},{8,24},{16,0},{24,8},{1,17},{9,25},{17,1},{25,9},{2,18},{10... | collective-permute-start | bytes 1277960 | tf_op jit(solution)/shard_map/ppermute | solution.py:24
  130.6 2.9 %collective-permute-start.20 = (bf16[832,256]{1,0:T(8,128)(2,1)S(1)}, bf16[832,256]{1,0:T(8,128)(2,1)S(1)}, u32[]{:S(2)}, u32[]{:S(2)}) collective-permute-start(bf16[832,256]{1,0:T(8,128)(2,1)S(1)} %row_order.1.y0), channel_id=1, source_target_pairs={{0,24},{8,16},{16,8},{24,0},{1,25},{9,17},{17,9},{25,1},{2,26},{10... | collective-permute-start | bytes 1277960 | tf_op jit(solution)/shard_map/ppermute | solution.py:24
  133.5 0.1 pair_sum.1
  133.6 8.8 %collective-permute-start.22 = (bf16[384,128]{1,0:T(8,128)(2,1)S(1)}, bf16[384,128]{1,0:T(8,128)(2,1)S(1)}, u32[]{:S(2)}, u32[]{:S(2)}) collective-permute-start(bf16[384,128]{1,0:T(8,128)(2,1)S(1)} %get-tuple-element.32.after), channel_id=1, source_target_pairs={{0,256},{64,320},{128,384},{192,448},{256,0},{320,64},{384,128},{4... | collective-permute-start | bytes 294920 | tf_op jit(solution)/shard_map/ppermute | solution.py:24
  142.4 1.9 %collective-permute-start.23 = (bf16[384,128]{1,0:T(8,128)(2,1)S(1)}, bf16[384,128]{1,0:T(8,128)(2,1)S(1)}, u32[]{:S(2)}, u32[]{:S(2)}) collective-permute-start(bf16[384,128]{1,0:T(8,128)(2,1)S(1)} %get-tuple-element.35), channel_id=1, source_target_pairs={{0,128},{64,192},{128,0},{192,64},{256,384},{320,448},{384,256},{4... | collective-permute-start | bytes 294920 | tf_op jit(solution)/shard_map/ppermute | solution.py:24
  144.3 4.0 %collective-permute-start.24 = (bf16[384,128]{1,0:T(8,128)(2,1)S(1)}, bf16[384,128]{1,0:T(8,128)(2,1)S(1)}, u32[]{:S(2)}, u32[]{:S(2)}) collective-permute-start(bf16[384,128]{1,0:T(8,128)(2,1)S(1)} %get-tuple-element.36), channel_id=1, source_target_pairs={{0,384},{64,448},{128,256},{192,320},{256,128},{320,192},{384,0},{... | collective-permute-start | bytes 294920 | tf_op jit(solution)/shard_map/ppermute | solution.py:24
  148.3 4.7 %collective-permute-done.20.y3 = bf16[832,256]{1,0:T(8,128)(2,1)S(1)} collective-permute-done((bf16[832,256]{1,0:T(8,128)(2,1)S(1)}, bf16[832,256]{1,0:T(8,128)(2,1)S(1)}, u32[]{:S(2)}, u32[]{:S(2)}) %collective-permute-start.20) | collective-permute-done | bytes 426016 | tf_op jit(solution)/shard_map/ppermute | solution.py:24
  153.0 8.5 %token_grads.1 = (bf16[768,2048]{1,0:T(8,128)(2,1)}, f32[48,128]{1,0:T(8,128)}) custom-call(s32[3]{0:T(128)S(1)} %pad_add_fusion.ids, bf16[2048,256]{1,0:T(8,128)(2,1)} %get-tuple-element.25.w0, bf16[2048,256]{1,0:T(8,128)(2,1)} %copy-done.1, bf16[1024,256]{1,0:T(8,128)(2,1)} %copy-done.2, bf16[1024,256]{1,0:T(8,128)(2,1)} %copy-done.3, ...), custom_call_target="tpu_custom_call" | custom-call | flops 3221225472 | bytes 12582912 | tf_op jit(solution)/shard_map/token_grads/pallas_call | solution.py:431
  161.5 0.8 last_sum.1
  (32 shorter events, 0.2 us)
Async XLA Ops:
  1.7 19.4 %collective-permute-start = (bf16[128,384]{1,0:T(8,128)(2,1)S(1)}, bf16[128,384]{1,0:T(8,128)(2,1)S(1)}, u32[]{:S(2)}, u32[]{:S(2)}) collective-permute-start(bf16[128,384]{1,0:T(8,128)(2,1)S(1)} %own_tiles.1.a), channel_id=1, source_target_pairs={{0,256},{64,320},{128,384},{192,448},{256,0},{320,64},{384,128},{4... | collective-permute-start | bytes 294920 | tf_op jit(solution)/shard_map/ppermute | solution.py:24
  11.4 9.7 %collective-permute-start.1 = (bf16[128,384]{1,0:T(8,128)(2,1)S(1)}, bf16[128,384]{1,0:T(8,128)(2,1)S(1)}, u32[]{:S(2)}, u32[]{:S(2)}) collective-permute-start(bf16[128,384]{1,0:T(8,128)(2,1)S(1)} %own_tiles.1.a), channel_id=1, source_target_pairs={{0,128},{64,192},{128,0},{192,64},{256,384},{320,448},{384,256},{4... | collective-permute-start | bytes 294920 | tf_op jit(solution)/shard_map/ppermute | solution.py:24
  16.3 11.1 %collective-permute-start.2 = (bf16[128,384]{1,0:T(8,128)(2,1)S(1)}, bf16[128,384]{1,0:T(8,128)(2,1)S(1)}, u32[]{:S(2)}, u32[]{:S(2)}) collective-permute-start(bf16[128,384]{1,0:T(8,128)(2,1)S(1)} %own_tiles.1.a), channel_id=1, source_target_pairs={{0,384},{64,448},{128,256},{192,320},{256,128},{320,192},{384,0},{... | collective-permute-start | bytes 294920 | tf_op jit(solution)/shard_map/ppermute | solution.py:24
  27.4 9.6 %collective-permute-start.3 = (bf16[512,384]{1,0:T(8,128)(2,1)S(1)}, bf16[512,384]{1,0:T(8,128)(2,1)S(1)}, u32[]{:S(2)}, u32[]{:S(2)}) collective-permute-start(bf16[512,384]{1,0:T(8,128)(2,1)S(1)} %join.1.m0), channel_id=1, source_target_pairs={{0,64},{64,0},{128,192},{192,128},{256,320},{320,256},{384,448},{4... | collective-permute-start | bytes 1179656 | tf_op jit(solution)/shard_map/ppermute | solution.py:24
  31.0 12.1 %collective-permute-start.4 = (bf16[512,384]{1,0:T(8,128)(2,1)S(1)}, bf16[512,384]{1,0:T(8,128)(2,1)S(1)}, u32[]{:S(2)}, u32[]{:S(2)}) collective-permute-start(bf16[512,384]{1,0:T(8,128)(2,1)S(1)} %join.1.m0), channel_id=1, source_target_pairs={{0,32},{32,0},{1,33},{33,1},{2,34},{34,2},{3,35},{35,3},{4,36},{36... | collective-permute-start | bytes 1179656 | tf_op jit(solution)/shard_map/ppermute | solution.py:24
  37.0 7.5 %collective-permute-start.5 = (bf16[512,384]{1,0:T(8,128)(2,1)S(1)}, bf16[512,384]{1,0:T(8,128)(2,1)S(1)}, u32[]{:S(2)}, u32[]{:S(2)}) collective-permute-start(bf16[512,384]{1,0:T(8,128)(2,1)S(1)} %collective-permute-done.3.m1), channel_id=1, source_target_pairs={{0,32},{32,0},{1,33},{33,1},{2,34},{34,2},{3,35},{35,3},{4,36},{36... | collective-permute-start | bytes 1179656 | tf_op jit(solution)/shard_map/ppermute | solution.py:24
  48.4 16.2 %collective-permute-start.10 = (bf16[192,384]{1,0:T(8,128)(2,1)}, bf16[192,384]{1,0:T(8,128)(2,1)S(1)}, u32[]{:S(2)}, u32[]{:S(2)}) collective-permute-start(bf16[192,384]{1,0:T(8,128)(2,1)} %get-tuple-element.27), channel_id=1, source_target_pairs={{0,1},{1,0},{2,3},{3,2},{4,5},{5,4},{6,7},{7,6},{8,9},{9,8},{10,11... | collective-permute-start | bytes 442376 | tf_op jit(solution)/shard_map/ppermute | solution.py:24
  51.5 13.1 %collective-permute-start.11 = (bf16[192,384]{1,0:T(8,128)(2,1)}, bf16[192,384]{1,0:T(8,128)(2,1)S(1)}, u32[]{:S(2)}, u32[]{:S(2)}) collective-permute-start(bf16[192,384]{1,0:T(8,128)(2,1)} %get-tuple-element.28), channel_id=1, source_target_pairs={{0,2},{1,3},{2,0},{3,1},{4,6},{5,7},{6,4},{7,5},{8,10},{9,11},{10,... | collective-permute-start | bytes 442376 | tf_op jit(solution)/shard_map/ppermute | solution.py:24
  55.9 8.7 %collective-permute-start.12 = (bf16[192,384]{1,0:T(8,128)(2,1)}, bf16[192,384]{1,0:T(8,128)(2,1)S(1)}, u32[]{:S(2)}, u32[]{:S(2)}) collective-permute-start(bf16[192,384]{1,0:T(8,128)(2,1)} %get-tuple-element.29), channel_id=1, source_target_pairs={{0,3},{1,2},{2,1},{3,0},{4,7},{5,6},{6,5},{7,4},{8,11},{9,10},{10,... | collective-permute-start | bytes 442376 | tf_op jit(solution)/shard_map/ppermute | solution.py:24
  58.0 26.9 %collective-permute-start.7 = (bf16[2048,256]{1,0:T(8,128)(2,1)}, bf16[2048,256]{1,0:T(8,128)(2,1)S(1)}, u32[]{:S(2)}, u32[]{:S(2)}) collective-permute-start(bf16[2048,256]{1,0:T(8,128)(2,1)} %get-tuple-element.25.w0), channel_id=1, source_target_pairs={{0,24},{8,16},{16,8},{24,0},{1,25},{9,17},{17,9},{25,1},{2,26},{10... | collective-permute-start | bytes 3145736 | tf_op jit(solution)/shard_map/ppermute | solution.py:24
  62.6 25.3 %collective-permute-start.6 = (bf16[2048,256]{1,0:T(8,128)(2,1)}, bf16[2048,256]{1,0:T(8,128)(2,1)S(1)}, u32[]{:S(2)}, u32[]{:S(2)}) collective-permute-start(bf16[2048,256]{1,0:T(8,128)(2,1)} %get-tuple-element.25.w0), channel_id=1, source_target_pairs={{0,8},{8,0},{16,24},{24,16},{1,9},{9,1},{17,25},{25,17},{2,10},{10... | collective-permute-start | bytes 3145736 | tf_op jit(solution)/shard_map/ppermute | solution.py:24
  64.7 13.9 %copy-start.5 = (s32[768]{0:T(1024)S(1)}, s32[768]{0:T(1024)}, u32[]{:S(2)}) copy-start(s32[768]{0:T(1024)} %param.15) | copy-start | bytes 9220
  64.7 14.6 %copy-start.4 = (f32[6144]{0:T(1024)S(1)}, f32[6144]{0:T(1024)}, u32[]{:S(2)}) copy-start(f32[6144]{0:T(1024)} %param.13) | copy-start | bytes 73732
  64.7 26.7 %collective-permute-start.13 = (bf16[192,384]{1,0:T(8,128)(2,1)S(1)}, bf16[192,384]{1,0:T(8,128)(2,1)S(1)}, u32[]{:S(2)}, u32[]{:S(2)}) collective-permute-start(bf16[192,384]{1,0:T(8,128)(2,1)S(1)} %reduce_rows.1.s_mine), channel_id=1, source_target_pairs={{0,4},{4,0},{1,5},{5,1},{2,6},{6,2},{3,7},{7,3},{8,12},{12,8},{9,1... | collective-permute-start | bytes 442376 | tf_op jit(solution)/shard_map/ppermute | solution.py:24
  84.9 22.7 %copy-start = (bf16[2048,256]{1,0:T(8,128)(2,1)}, bf16[2048,256]{1,0:T(8,128)(2,1)S(1)}, u32[]{:S(2)}) copy-start(bf16[2048,256]{1,0:T(8,128)(2,1)S(1)} %collective-permute-done.7.w3) | copy-start | bytes 3145732
  84.9 22.6 %collective-permute-start.8 = (bf16[1024,256]{1,0:T(8,128)(2,1)S(1)}, bf16[1024,256]{1,0:T(8,128)(2,1)S(1)}, u32[]{:S(2)}, u32[]{:S(2)}) collective-permute-start(bf16[1024,256]{1,0:T(8,128)(2,1)S(1)} %slice.8), channel_id=1, source_target_pairs={{0,8},{8,0},{16,24},{24,16},{1,9},{9,1},{17,25},{25,17},{2,10},{10... | collective-permute-start | bytes 1572872 | tf_op jit(solution)/shard_map/ppermute | solution.py:24
  87.9 19.7 %copy-start.1 = (bf16[2048,256]{1,0:T(8,128)(2,1)}, bf16[2048,256]{1,0:T(8,128)(2,1)S(1)}, u32[]{:S(2)}) copy-start(bf16[2048,256]{1,0:T(8,128)(2,1)S(1)} %collective-permute-done.6.w1) | copy-start | bytes 3145732
  87.9 19.6 %collective-permute-start.9 = (bf16[1024,256]{1,0:T(8,128)(2,1)S(1)}, bf16[1024,256]{1,0:T(8,128)(2,1)S(1)}, u32[]{:S(2)}, u32[]{:S(2)}) collective-permute-start(bf16[1024,256]{1,0:T(8,128)(2,1)S(1)} %slice.9), channel_id=1, source_target_pairs={{0,24},{8,16},{16,8},{24,0},{1,25},{9,17},{17,9},{25,1},{2,26},{10... | collective-permute-start | bytes 1572872 | tf_op jit(solution)/shard_map/ppermute | solution.py:24
  92.3 9.6 %collective-permute-start.14 = (bf16[208,384]{1,0:T(8,128)(2,1)S(1)}, bf16[208,384]{1,0:T(8,128)(2,1)S(1)}, u32[]{:S(2)}, u32[]{:S(2)}) collective-permute-start(bf16[208,384]{1,0:T(8,128)(2,1)S(1)} %deltas.1.d0), channel_id=1, source_target_pairs={{0,1},{1,0},{2,3},{3,2},{4,5},{5,4},{6,7},{7,6},{8,9},{9,8},{10,11... | collective-permute-start | bytes 479240 | tf_op jit(solution)/shard_map/ppermute | solution.py:24
  94.2 9.0 %collective-permute-start.15 = (bf16[208,384]{1,0:T(8,128)(2,1)S(1)}, bf16[208,384]{1,0:T(8,128)(2,1)S(1)}, u32[]{:S(2)}, u32[]{:S(2)}) collective-permute-start(bf16[208,384]{1,0:T(8,128)(2,1)S(1)} %deltas.1.d0), channel_id=1, source_target_pairs={{0,2},{1,3},{2,0},{3,1},{4,6},{5,7},{6,4},{7,5},{8,10},{9,11},{10,... | collective-permute-start | bytes 479240 | tf_op jit(solution)/shard_map/ppermute | solution.py:24
  99.8 7.8 %collective-permute-start.16 = (bf16[208,384]{1,0:T(8,128)(2,1)S(1)}, bf16[208,384]{1,0:T(8,128)(2,1)S(1)}, u32[]{:S(2)}, u32[]{:S(2)}) collective-permute-start(bf16[208,384]{1,0:T(8,128)(2,1)S(1)} %deltas.1.d0), channel_id=1, source_target_pairs={{0,3},{1,2},{2,1},{3,0},{4,7},{5,6},{6,5},{7,4},{8,11},{9,10},{10,... | collective-permute-start | bytes 479240 | tf_op jit(solution)/shard_map/ppermute | solution.py:24
  107.5 5.0 %copy-start.2 = (bf16[1024,256]{1,0:T(8,128)(2,1)}, bf16[1024,256]{1,0:T(8,128)(2,1)S(1)}, u32[]{:S(2)}) copy-start(bf16[1024,256]{1,0:T(8,128)(2,1)S(1)} %collective-permute-done.8.w2a) | copy-start | bytes 1572868
  107.6 5.0 %copy-start.3 = (bf16[1024,256]{1,0:T(8,128)(2,1)}, bf16[1024,256]{1,0:T(8,128)(2,1)S(1)}, u32[]{:S(2)}) copy-start(bf16[1024,256]{1,0:T(8,128)(2,1)S(1)} %collective-permute-done.9.w2b) | copy-start | bytes 1572868
  112.5 7.4 %collective-permute-start.17 = (bf16[3072,128]{1,0:T(8,128)(2,1)S(1)}, bf16[3072,128]{1,0:T(8,128)(2,1)S(1)}, u32[]{:S(2)}, u32[]{:S(2)}) collective-permute-start(bf16[3072,128]{1,0:T(8,128)(2,1)S(1)} %get-tuple-element.31), channel_id=1, source_target_pairs={{0,32},{32,0},{1,33},{33,1},{2,34},{34,2},{3,35},{35,3},{4,36},{36... | collective-permute-start | bytes 2359304 | tf_op jit(solution)/shard_map/ppermute | solution.py:24
  120.0 13.4 %collective-permute-start.21 = (bf16[1728,128]{1,0:T(8,128)(2,1)S(1)}, bf16[1728,128]{1,0:T(8,128)(2,1)S(1)}, u32[]{:S(2)}, u32[]{:S(2)}) collective-permute-start(bf16[1728,128]{1,0:T(8,128)(2,1)S(1)} %core_sum.1.after), channel_id=1, source_target_pairs={{0,64},{64,0},{128,192},{192,128},{256,320},{320,256},{384,448},{4... | collective-permute-start | bytes 1327112 | tf_op jit(solution)/shard_map/ppermute | solution.py:24
  123.8 20.5 %collective-permute-start.18 = (bf16[832,256]{1,0:T(8,128)(2,1)S(1)}, bf16[832,256]{1,0:T(8,128)(2,1)S(1)}, u32[]{:S(2)}, u32[]{:S(2)}) collective-permute-start(bf16[832,256]{1,0:T(8,128)(2,1)S(1)} %row_order.1.y0), channel_id=1, source_target_pairs={{0,8},{8,0},{16,24},{24,16},{1,9},{9,1},{17,25},{25,17},{2,10},{10... | collective-permute-start | bytes 1277960 | tf_op jit(solution)/shard_map/ppermute | solution.py:24
  126.9 21.4 %collective-permute-start.19 = (bf16[832,256]{1,0:T(8,128)(2,1)S(1)}, bf16[832,256]{1,0:T(8,128)(2,1)S(1)}, u32[]{:S(2)}, u32[]{:S(2)}) collective-permute-start(bf16[832,256]{1,0:T(8,128)(2,1)S(1)} %row_order.1.y0), channel_id=1, source_target_pairs={{0,16},{8,24},{16,0},{24,8},{1,17},{9,25},{17,1},{25,9},{2,18},{10... | collective-permute-start | bytes 1277960 | tf_op jit(solution)/shard_map/ppermute | solution.py:24
  130.6 22.4 %collective-permute-start.20 = (bf16[832,256]{1,0:T(8,128)(2,1)S(1)}, bf16[832,256]{1,0:T(8,128)(2,1)S(1)}, u32[]{:S(2)}, u32[]{:S(2)}) collective-permute-start(bf16[832,256]{1,0:T(8,128)(2,1)S(1)} %row_order.1.y0), channel_id=1, source_target_pairs={{0,24},{8,16},{16,8},{24,0},{1,25},{9,17},{17,9},{25,1},{2,26},{10... | collective-permute-start | bytes 1277960 | tf_op jit(solution)/shard_map/ppermute | solution.py:24
  133.6 27.9 %collective-permute-start.22 = (bf16[384,128]{1,0:T(8,128)(2,1)S(1)}, bf16[384,128]{1,0:T(8,128)(2,1)S(1)}, u32[]{:S(2)}, u32[]{:S(2)}) collective-permute-start(bf16[384,128]{1,0:T(8,128)(2,1)S(1)} %get-tuple-element.32.after), channel_id=1, source_target_pairs={{0,256},{64,320},{128,384},{192,448},{256,0},{320,64},{384,128},{4... | collective-permute-start | bytes 294920 | tf_op jit(solution)/shard_map/ppermute | solution.py:24
  142.4 19.1 %collective-permute-start.23 = (bf16[384,128]{1,0:T(8,128)(2,1)S(1)}, bf16[384,128]{1,0:T(8,128)(2,1)S(1)}, u32[]{:S(2)}, u32[]{:S(2)}) collective-permute-start(bf16[384,128]{1,0:T(8,128)(2,1)S(1)} %get-tuple-element.35), channel_id=1, source_target_pairs={{0,128},{64,192},{128,0},{192,64},{256,384},{320,448},{384,256},{4... | collective-permute-start | bytes 294920 | tf_op jit(solution)/shard_map/ppermute | solution.py:24
  144.3 17.2 %collective-permute-start.24 = (bf16[384,128]{1,0:T(8,128)(2,1)S(1)}, bf16[384,128]{1,0:T(8,128)(2,1)S(1)}, u32[]{:S(2)}, u32[]{:S(2)}) collective-permute-start(bf16[384,128]{1,0:T(8,128)(2,1)S(1)} %get-tuple-element.36), channel_id=1, source_target_pairs={{0,384},{64,448},{128,256},{192,320},{256,128},{320,192},{384,0},{... | collective-permute-start | bytes 294920 | tf_op jit(solution)/shard_map/ppermute | solution.py:24
